TPU v7x, 32 devices: a whole 2x2x4 slice. The times are simulated.
32 devices in a mesh: sector: 4 (over z), rows: 8 (over y, x, core).
Axes of the slice: x: 2, y: 2, z: 4, core: 2. Of those that a mesh axis runs over, the one named last changes fastest.
Arguments:
- x_block: bfloat16 [4, 10240, 300], P('sector', 'rows')
- h_diag: bfloat16 [4, 10240, 1280], P('sector', 'rows')
- h_right: bfloat16 [4, 10240, 1280], P('sector', 'rows')
- pattern: int32 [4, 2, 80, 10], P('sector', None, 'rows'), may hold values from 0 to 1, as said below
Outputs:
- q_block: bfloat16 [4, 10240, 300], P('sector', 'rows')
- hproj: float32 [4, 300, 300], P('sector')
- correlation: float32 [4, 300, 300], P('sector')
Inputs may be any that keep to these rules, and one draw needn't show every extreme that they name: Within each 1280 x 1280 tile, pattern[s, 0] is symmetric with ones on its diagonal; h_diag's tiles are symmetric.
All inputs are finite; a program needn't handle non-finite values.
Results may differ from a plain program's by a relative error of at most 0.011.
Values may be sent and summed in bfloat16 or wider, within the bound.
No kernel may reach another device: no remote copies, remote signals or barrier semaphores. Data moves between devices by JAX's collectives and lax.ppermute only.
A program may use at most 64 MiB of HBM per device.

v0:
```python
import functools

import jax
import jax.numpy as jnp
from jax import lax
from jax.experimental import pallas as pl
from jax.experimental.pallas import tpu as pltpu
from jax.sharding import PartitionSpec as P

SUBBLOCK = 128
LANES = 128
PANEL = 16
EARLY_PANELS = 4
WHOLE = pl.BlockSpec(memory_space=pltpu.VMEM)
SCALARS = pl.BlockSpec(memory_space=pltpu.SMEM)
ANYWHERE = pl.BlockSpec(memory_space=pl.ANY)
MIB = 1024 * 1024
FIRST_STAGE_FLOPS = 3500 * 10**6
LAST_STAGES_FLOPS = 4 * 10**9


def params(mib=48):
    return pltpu.CompilerParams(vmem_limit_bytes=mib * MIB)


def cost(flops, bytes_accessed):
    return pl.CostEstimate(flops=flops, bytes_accessed=bytes_accessed, transcendentals=0)


def round_up(value, step):
    return (value + step - 1) // step * step


def dot(left, right, dims, precision=None):
    return lax.dot_general(
        left, right, (dims, ((), ())), precision=precision, preferred_element_type=jnp.float32
    )


def block_mask(mask_ref, which, cols):
    blocks = mask_ref[:, which, :].astype(jnp.float32)
    col = lax.broadcasted_iota(jnp.int32, (blocks.shape[1], cols), 1)
    block = lax.broadcasted_iota(jnp.int32, (blocks.shape[1], cols), 0)
    return dot(blocks, jnp.where(col // SUBBLOCK == block, 1.0, 0.0), ((1,), (0,)))


def mask_rows(tile_ref, mask, start, size):
    cols = tile_ref.shape[1]
    for i in range(start // SUBBLOCK, (start + size) // SUBBLOCK):
        keep = jnp.broadcast_to(mask[i : i + 1, :], (PANEL, cols)).astype(tile_ref.dtype)
        for row in range(i * SUBBLOCK, (i + 1) * SUBBLOCK, PANEL):
            tile_ref[row : row + PANEL, :] = tile_ref[row : row + PANEL, :] * keep


def strips(rows, width):
    return [(start, min(width, rows - start)) for start in range(0, rows, width)]


def halves(rows):
    first = rows // 512 * 256
    return [(0, first), (first, rows - first)] if first else [(0, rows)]


def copies_of(source, target, sems):
    copies = []
    for n, (start, size) in enumerate(halves(target.shape[0])):
        here = (pl.ds(start, size), slice(None))
        copies.append(pltpu.make_async_copy(source.at[here], target.at[here], sems.at[n]))
    return copies


def product(x_ref, tile_ref, copies, mask, sum_ref, out_ref):
    rows = tile_ref.shape[0]
    for n, (start, size) in enumerate(halves(rows)):
        copies[n].wait()
        mask_rows(tile_ref, mask, start, size)
        last = n + 1 == len(copies)
        for col, cols in strips(rows, 2 * SUBBLOCK):
            here = (slice(None), slice(col, col + cols))
            term = dot(
                x_ref[:, start : start + size],
                tile_ref[start : start + size, col : col + cols],
                ((1,), (0,)),
            )
            if n > 0:
                term = sum_ref[here] + term
            if last:
                out_ref[here] = term.astype(out_ref.dtype)
            else:
                sum_ref[here] = term


def tile_kernel(which, mask_ref, x_hbm, tile_hbm, out_ref, x_ref, tile_ref, sum_ref, x_sem, sems):
    rows = tile_ref.shape[0]
    copies = copies_of(tile_hbm, tile_ref, sems)
    copy_x = pltpu.make_async_copy(x_hbm, x_ref, x_sem)
    copy_x.start()
    for copy in copies:
        copy.start()
    mask = block_mask(mask_ref, which, rows)
    copy_x.wait()
    product(x_ref, tile_ref, copies, mask, sum_ref, out_ref)


def tile_product(which, masks, x_t, tile, dtype, mib):
    channels, rows = x_t.shape
    return pl.pallas_call(
        functools.partial(tile_kernel, which),
        in_specs=[WHOLE, ANYWHERE, ANYWHERE],
        out_specs=WHOLE,
        out_shape=jax.ShapeDtypeStruct((channels, rows), dtype),
        scratch_shapes=[
            pltpu.VMEM((channels, rows), x_t.dtype),
            pltpu.VMEM((rows, rows), tile.dtype),
            pltpu.VMEM((channels, rows), jnp.float32),
            pltpu.SemaphoreType.DMA,
            pltpu.SemaphoreType.DMA((2,)),
        ],
        compiler_params=params(mib),
        cost_estimate=cost(2 * channels * rows * rows, 2 * rows * rows),
    )(masks, x_t, tile)


def later_kernel(mask_ref, later_ref, tile_hbm, first_ref, out_ref, tile_ref, sems):
    rows = tile_ref.shape[0]
    copies = copies_of(tile_hbm, tile_ref, sems)
    for copy in copies:
        copy.start()
    mask = block_mask(mask_ref, 1, rows)
    for n, (start, size) in enumerate(halves(rows)):
        copies[n].wait()
        mask_rows(tile_ref, mask, start, size)
        for row, count in strips(size, 2 * SUBBLOCK):
            here = (slice(None), slice(start + row, start + row + count))
            out_ref[here] = first_ref[here] + dot(
                later_ref[...], tile_ref[start + row : start + row + count, :], ((1,), (1,))
            )


def later_product(masks, later, tile, first):
    channels, rows = later.shape
    return pl.pallas_call(
        later_kernel,
        in_specs=[WHOLE, WHOLE, ANYWHERE, WHOLE],
        out_specs=WHOLE,
        out_shape=jax.ShapeDtypeStruct((channels, rows), jnp.float32),
        scratch_shapes=[
            pltpu.VMEM((rows, rows), tile.dtype),
            pltpu.SemaphoreType.DMA((2,)),
        ],
        compiler_params=params(),
        cost_estimate=cost(2 * channels * rows * rows, 2 * rows * rows),
    )(masks, later, tile, first)


def lower_rows(channels):
    rows = round_up(channels, PANEL)
    return sum(rows - g * LANES for g in range(round_up(channels, LANES) // LANES))


def full_rows(channels):
    rows, wide = round_up(channels, PANEL), round_up(channels, LANES)
    whole = channels // LANES
    rest = rows - whole * LANES
    return round_up(whole * rows + rest * (wide // LANES), 4 * PANEL)


def lower_products(ref, out_ref):
    channels = ref.shape[0]
    rows = round_up(channels, PANEL)
    offset = 0
    for start, size in strips(channels, LANES):
        tall = rows - start
        if size < LANES:
            out_ref[offset : offset + tall, :] = jnp.zeros((tall, LANES), jnp.float32)
        elif rows > channels:
            out_ref[offset + channels - start : offset + tall, :] = jnp.zeros(
                (rows - channels, LANES), jnp.float32
            )
        out_ref[offset : offset + channels - start, 0:size] = dot(
            ref[start:channels, :], ref[start : start + size, :], ((1,), (1,))
        )
        offset += tall


def full_products(left_ref, right_ref, out_ref):
    channels = left_ref.shape[0]
    rows = round_up(channels, PANEL)
    whole = channels // LANES
    for g in range(whole):
        out_ref[g * rows : g * rows + channels, :] = dot(
            left_ref[...], right_ref[g * LANES : (g + 1) * LANES, :], ((1,), (1,))
        )
        if rows > channels:
            out_ref[g * rows + channels : (g + 1) * rows, :] = jnp.zeros(
                (rows - channels, LANES), jnp.float32
            )
    base = whole * rows
    if base < out_ref.shape[0]:
        out_ref[base:, :] = jnp.zeros((out_ref.shape[0] - base, LANES), jnp.float32)
    first, rest = whole * LANES, rows - whole * LANES
    for n, (start, size) in enumerate(strips(channels, LANES) if first < channels else []):
        place = base + n * rest
        out_ref[place : place + channels - first, 0:size] = dot(
            right_ref[first:channels, :], left_ref[start : start + size, :], ((1,), (1,))
        )


def full_matrix(pack_ref, channels):
    rows, wide = round_up(channels, PANEL), round_up(channels, LANES)
    whole = channels // LANES
    rest = rows - whole * LANES
    parts = [pack_ref[g * rows : (g + 1) * rows, :] for g in range(whole)]
    if rest:
        tail = jnp.concatenate(
            [
                pack_ref[whole * rows + g * rest : whole * rows + (g + 1) * rest, :]
                for g in range(wide // LANES)
            ],
            axis=1,
        )
        tail = jnp.concatenate([tail, jnp.zeros((LANES - rest, wide), tail.dtype)], axis=0)
        parts.append(tail.T[0:rows, :])
    return jnp.concatenate(parts, axis=1)


def folded_rows(channels):
    if channels < 2 * LANES:
        return lower_rows(channels)
    return lower_rows(channels) - LANES + PANEL


def corner(channels):
    return round_up(channels, PANEL)


def square_index():
    row = lax.broadcasted_iota(jnp.int32, (LANES, LANES), 0)
    return row, lax.broadcasted_iota(jnp.int32, (LANES, LANES), 1)


def fold(pack_ref, out_ref, channels, symmetric):
    if channels < 2 * LANES:
        out_ref[...] = pack_ref[...]
        return
    start = corner(channels)
    end = pack_ref.shape[0]
    row, lane = square_index()
    second = pack_ref[start : start + LANES, :]
    upper = second if symmetric else second.T
    out_ref[0:LANES, :] = jnp.where(row >= lane, pack_ref[0:LANES, :], upper)
    out_ref[LANES:start, :] = pack_ref[LANES:start, :]
    out_ref[start : end - LANES, :] = pack_ref[start + LANES : end, :]
    diagonal = jnp.sum(jnp.where(row == lane, second, 0.0), axis=0, keepdims=True)
    out_ref[end - LANES :, :] = jnp.broadcast_to(diagonal, (PANEL, LANES))


def unfold(folded_ref, pack_ref, channels, symmetric):
    if channels < 2 * LANES:
        pack_ref[...] = folded_ref[...]
        return
    start = corner(channels)
    end = pack_ref.shape[0]
    row, lane = square_index()
    both = folded_ref[0:LANES, :]
    turned = both.T
    first_upper, second_upper = (turned, both) if symmetric else (0.0, 0.0)
    pack_ref[0:LANES, :] = jnp.where(row >= lane, both, first_upper)
    pack_ref[LANES:start, :] = folded_ref[LANES:start, :]
    second = jnp.where(row > lane, turned, second_upper)
    diagonal = folded_ref[end - LANES : end - LANES + 1, :]
    pack_ref[start : start + LANES, :] = jnp.where(row == lane, diagonal, second)
    pack_ref[start + LANES : end, :] = folded_ref[start : end - LANES, :]


def cut(pack_ref, core, mine_ref, other_ref):
    half = mine_ref.shape[0]
    mine_ref[...] = pack_ref[pl.ds(pl.multiple_of(core * half, 8), half), :].astype(mine_ref.dtype)
    other_ref[...] = pack_ref[pl.ds(pl.multiple_of((1 - core) * half, 8), half), :].astype(
        other_ref.dtype
    )


def join(pack_ref, core, mine, other):
    half = mine.shape[0]
    pack_ref[pl.ds(pl.multiple_of(core * half, 8), half), :] = mine
    pack_ref[pl.ds(pl.multiple_of((1 - core) * half, 8), half), :] = other


def gram_kernel(core_ref, part_ref, carried_ref, y_ref, g_mine, g_other, gram_ref, folded_ref):
    image = part_ref[...] + carried_ref[...].astype(jnp.float32)
    y_ref[...] = image.astype(y_ref.dtype)
    lower_products(y_ref, gram_ref)
    fold(gram_ref, folded_ref, y_ref.shape[0], True)
    cut(folded_ref, core_ref[0], g_mine, g_other)


def gram(core, part, carried):
    channels, rows = carried.shape
    lower, folded = lower_rows(channels), folded_rows(channels)
    half = jax.ShapeDtypeStruct((folded // 2, LANES), jnp.float32)
    return pl.pallas_call(
        gram_kernel,
        in_specs=[SCALARS] + [WHOLE] * 2,
        out_specs=[WHOLE] * 3,
        out_shape=[jax.ShapeDtypeStruct((channels, rows), carried.dtype), half, half],
        scratch_shapes=[
            pltpu.VMEM((lower, LANES), jnp.float32),
            pltpu.VMEM((folded, LANES), jnp.float32),
        ],
        compiler_params=params(),
        cost_estimate=cost(2 * channels * channels * rows, 8 * channels * rows),
    )(core, part, carried)


def cross_kernel(core_ref, left_ref, right_ref, after_ref, mine_ref, other_ref, pack_ref):
    full_products(left_ref, right_ref, pack_ref)
    cut(pack_ref, core_ref[0], mine_ref, other_ref)


def cross(core, left, right, after, dtype):
    channels, rows = left.shape
    full = full_rows(channels)
    return pl.pallas_call(
        cross_kernel,
        in_specs=[SCALARS, WHOLE, WHOLE, ANYWHERE],
        out_specs=[WHOLE] * 2,
        out_shape=[jax.ShapeDtypeStruct((full // 2, LANES), dtype)] * 2,
        scratch_shapes=[pltpu.VMEM((full, LANES), jnp.float32)],
        compiler_params=params(),
        cost_estimate=cost(2 * channels * channels * rows, 4 * channels * rows),
    )(core, left, right, after)


def add_kernel(left_ref, right_ref, *refs):
    total = left_ref[...].astype(jnp.float32) + right_ref[...].astype(jnp.float32)
    refs[-1][...] = total.astype(refs[-1].dtype)


def add_after(left, right, *after):
    return pl.pallas_call(
        add_kernel,
        in_specs=[WHOLE] * 2 + [ANYWHERE] * len(after),
        out_specs=WHOLE,
        out_shape=jax.ShapeDtypeStruct(left.shape, left.dtype),
        compiler_params=params(),
        cost_estimate=cost(10**5, 10**5),
    )(left, right, *after)


def split3(value):
    high = value.astype(jnp.bfloat16)
    rest = value - high.astype(jnp.float32)
    mid = rest.astype(jnp.bfloat16)
    low = (rest - mid.astype(jnp.float32)).astype(jnp.bfloat16)
    return high, mid, low


def sublane(value, index):
    return jnp.broadcast_to(value[index : index + 1, :], value.shape)


def lane_of(value, index):
    return jnp.take_along_axis(value, jnp.broadcast_to(index, value.shape), axis=1)


def eliminate(columns, panel):
    half = 8
    row = lax.broadcasted_iota(jnp.int32, (half, LANES), 0)
    scales = [jnp.zeros((half, LANES), jnp.float32) for _ in range(2)]
    columns = [list(c) for c in columns]
    panel = [list(p) for p in panel]
    for j in range(0, PANEL, 2):
        h, r = divmod(j, half)
        left, right = columns[j], columns[j + 1]
        a, b, c = sublane(left[h], r), sublane(left[h], r + 1), sublane(right[h], r + 1)
        det = a * c - b * b
        inverse = pl.reciprocal(det, approx=True)
        first, second = [None, None], [None, None]
        for t in range(h, 2):
            x, y = left[t], right[t]
            if t == h:
                x, y = jnp.where(row > r + 1, x, 0.0), jnp.where(row > r + 1, y, 0.0)
            first[t] = (c * x - b * y) * inverse
            second[t] = (a * y - b * x) * inverse
        for later in range(j + 2, PANEL):
            q = later // half
            x, y = sublane(left[q], later % half), sublane(right[q], later % half)
            for t in range(max(h, q), 2):
                columns[later][t] = columns[later][t] - (first[t] * x + second[t] * y)
        inverse_a = pl.reciprocal(a, approx=True)
        first[h] = jnp.where(row == r + 1, b * inverse_a, first[h])
        for group in panel:
            x, y = sublane(group[h], r), sublane(group[h], r + 1)
            for t in range(h, 2):
                group[t] = group[t] - (first[t] * x + second[t] * y)
        scales[h] = jnp.where(row == r, lax.rsqrt(a), scales[h])
        scales[h] = jnp.where(row == r + 1, lax.rsqrt(det * inverse_a), scales[h])
    return [jnp.concatenate([g[0] * scales[0], g[1] * scales[1]], axis=0) for g in panel]


def fill_work(channels, scale, pack_ref, work_ref):
    rows, wide = work_ref.shape
    groups = wide // LANES
    offset = 0
    for g in range(groups):
        top = g * LANES
        size = min(LANES, rows - top)
        column = pack_ref[offset : offset + rows - top, :] * scale
        offset += rows - top
        diag = column[0:size, :]
        if top + LANES > channels:
            row = lax.broadcasted_iota(jnp.int32, diag.shape, 0)
            lane = lax.broadcasted_iota(jnp.int32, diag.shape, 1)
            diag = jnp.where((row == lane) & (lane + top >= channels), 1.0, diag)
        work_ref[top : top + size, top : top + LANES] = diag
        for below in range(g + 1, groups):
            start = (below - g) * LANES
            size_b = min(LANES, rows - below * LANES)
            block = column[start : start + size_b, :]
            if size_b < LANES:
                block = jnp.concatenate(
                    [block, jnp.zeros((LANES - size_b, LANES), jnp.float32)], axis=0
                )
            work_ref[top : top + size, below * LANES : (below + 1) * LANES] = block.T
            work_ref[below * LANES : below * LANES + size_b, top : top + LANES] = jnp.zeros(
                (size_b, LANES), jnp.float32
            )


def eliminate_group(g, work_ref, turned_ref, first=0, last=LANES // PANEL):
    rows, wide = work_ref.shape
    groups = wide // LANES
    row = lax.broadcasted_iota(jnp.int32, (PANEL, LANES), 0)
    lane = lax.broadcasted_iota(jnp.int32, (PANEL, LANES), 1)
    top = g * LANES
    count = min(LANES, rows - top) // PANEL

    def load(local):
        place = pl.ds(pl.multiple_of(top + local, PANEL), PANEL)
        return [work_ref[place, q * LANES : (q + 1) * LANES] for q in range(groups)]

    def panel_step(b, parts, slot):
        local = b * PANEL
        following = jnp.minimum(local + PANEL, (count - 1) * PANEL)
        ahead = load(following)
        pivots = [parts[g][0:8, :], parts[g][8:16, :]]
        columns = [[lane_of(p, local + j) for p in pivots] for j in range(PANEL)]
        inside = (lane >= local) & (lane < local + PANEL)
        identity = jnp.where(lane - local == row, 1.0, 0.0)
        parts = list(parts)
        parts[g] = jnp.where(inside, identity, parts[g])
        done = eliminate(columns, [[p[0:8, :], p[8:16, :]] for p in parts])
        right = []
        for q in range(groups):
            high, mid, low = split3(done[q])
            right.append(jnp.concatenate([high, mid, high, low, mid, high], axis=0))
            if q >= g:
                if q == g:
                    high, mid, low = split3(jnp.where(lane >= local + PANEL, done[q], 0.0))
                left = jnp.concatenate([high, high, mid, high, mid, low], axis=0)
                turned_ref[slot, (q - g) * LANES : (q - g + 1) * LANES, :] = left.T
        right = jnp.concatenate(right, axis=1)
        near = turned_ref[slot, pl.ds(pl.multiple_of(following, PANEL), PANEL), :]
        update = dot(near, right, ((1,), (0,)))
        ahead[g] = jnp.where(inside, 0.0, ahead[g])
        ahead = [ahead[q] - update[:, q * LANES : (q + 1) * LANES] for q in range(groups)]
        for q in range(g, groups):
            low_row = q * LANES
            high_row = min(rows, low_row + LANES)
            base = low_row - top
            update = dot(turned_ref[slot, base : base + high_row - low_row, :], right, ((1,), (0,)))
            for c in range(groups):
                lanes = slice(c * LANES, (c + 1) * LANES)
                old = work_ref[low_row:high_row, lanes]
                if c == g:
                    here = lax.broadcasted_iota(jnp.int32, old.shape, 1)
                    old = jnp.where((here >= local) & (here < local + PANEL), 0.0, old)
                work_ref[low_row:high_row, lanes] = old - update[:, lanes]
        for q in range(groups):
            if q == g:
                done[q] = jnp.where(lane < local + PANEL, done[q], 0.0)
            elif q > g:
                done[q] = jnp.zeros_like(done[q])
            place = pl.ds(pl.multiple_of(top + local, PANEL), PANEL)
            work_ref[place, q * LANES : (q + 1) * LANES] = done[q]
        return ahead

    def two_panels(i, parts):
        return panel_step(first + 2 * i + 1, panel_step(first + 2 * i, parts, 0), 1)

    last = min(last, count)
    parts = lax.fori_loop(0, (last - first) // 2, two_panels, load(first * PANEL))
    if (last - first) % 2:
        panel_step(jnp.int32(last - 1), parts, 0)


def first_stage_kernel(
    channels, scale, core_ref, mine_ref, other_ref, work_ref, pack_ref, folded_ref, turned_ref
):
    join(folded_ref, core_ref[0], mine_ref[...], other_ref[...])
    unfold(folded_ref, pack_ref, channels, True)
    fill_work(channels, scale, pack_ref, work_ref)
    eliminate_group(0, work_ref, turned_ref)
    if work_ref.shape[1] > LANES:
        eliminate_group(1, work_ref, turned_ref, 0, EARLY_PANELS)


def last_stages_kernel(
    channels, before_ref, after_ref, work_ref, folded_ref, pack_ref, turned_ref
):
    work_ref[...] = before_ref[...]
    rows, wide = work_ref.shape
    for g in range(1, wide // LANES):
        eliminate_group(g, work_ref, turned_ref, EARLY_PANELS if g == 1 else 0)
    offset = 0
    for q in range(wide // LANES):
        tall = rows - q * LANES
        pack_ref[offset : offset + tall, :] = work_ref[q * LANES : rows, q * LANES : (q + 1) * LANES]
        offset += tall
    fold(pack_ref, folded_ref, channels, False)


def turned_scratch(channels):
    return pltpu.VMEM((2, round_up(channels, LANES), 6 * PANEL), jnp.bfloat16)


def work_shape(channels):
    return jax.ShapeDtypeStruct((round_up(channels, PANEL), round_up(channels, LANES)), jnp.float32)


def first_stage(core, mine, other, channels, total_rows):
    return pl.pallas_call(
        functools.partial(first_stage_kernel, channels, 1.0 / total_rows),
        in_specs=[SCALARS] + [WHOLE] * 2,
        out_specs=WHOLE,
        out_shape=work_shape(channels),
        scratch_shapes=[
            pltpu.VMEM((lower_rows(channels), LANES), jnp.float32),
            pltpu.VMEM((folded_rows(channels), LANES), jnp.float32),
            turned_scratch(channels),
        ],
        compiler_params=params(),
        cost_estimate=cost(FIRST_STAGE_FLOPS, 10**6),
    )(core, mine, other)


def last_stages(work, channels, after):
    return pl.pallas_call(
        functools.partial(last_stages_kernel, channels),
        in_specs=[WHOLE, ANYWHERE],
        out_specs=[WHOLE] * 2,
        out_shape=[
            work_shape(channels),
            jax.ShapeDtypeStruct((folded_rows(channels), LANES), jnp.float32),
        ],
        scratch_shapes=[
            pltpu.VMEM((lower_rows(channels), LANES), jnp.float32),
            turned_scratch(channels),
        ],
        compiler_params=params(),
        cost_estimate=cost(LAST_STAGES_FLOPS, 10**5),
    )(work, after)


def split2(value):
    high = value.astype(jnp.bfloat16)
    return high, (value - high.astype(jnp.float32)).astype(jnp.bfloat16)


def dot3(left, right, dims):
    left_high, left_low = split2(left)
    right_high, right_low = split2(right)
    return (
        dot(left_high, right_high, dims)
        + dot(left_high, right_low, dims)
        + dot(left_low, right_high, dims)
    )


def lower_matrix(pack_ref, out_ref):
    rows, wide = out_ref.shape
    offset = 0
    for g in range(wide // LANES):
        top = g * LANES
        lanes = slice(top, top + LANES)
        if top:
            out_ref[0:top, lanes] = jnp.zeros((top, LANES), jnp.float32)
        out_ref[top:rows, lanes] = pack_ref[offset : offset + rows - top, :]
        offset += rows - top


def basis_kernel(inverse_ref, y_ref, q_ref):
    channels = y_ref.shape[0]
    image = y_ref[...]
    for start, size in strips(channels, 2 * LANES):
        used = min(channels, start + size)
        high, low = split2(inverse_ref[start : start + size, 0:used])
        both = dot(jnp.concatenate([high, low], axis=0), image[0:used, :], ((1,), (0,)))
        q_ref[start : start + size, :] = (both[0:size, :] + both[size:, :]).astype(q_ref.dtype)


def basis(inverse, y_t):
    channels, rows = y_t.shape
    return pl.pallas_call(
        basis_kernel,
        in_specs=[WHOLE] * 2,
        out_specs=WHOLE,
        out_shape=jax.ShapeDtypeStruct(y_t.shape, y_t.dtype),
        compiler_params=params(),
        cost_estimate=cost(10**5, 10**5),
    )(inverse, y_t)


def matrix_shape(channels):
    return jax.ShapeDtypeStruct((channels, 1, channels), jnp.float32)


def ray_kernel(scale, core_ref, mine_ref, other_ref, out_ref, token_ref, pack_ref):
    token_ref[...] = jnp.zeros_like(token_ref)
    channels = out_ref.shape[0]
    join(pack_ref, core_ref[0], mine_ref[...].astype(jnp.float32), other_ref[...].astype(jnp.float32))
    out_ref[:, 0, :] = full_matrix(pack_ref, channels)[0:channels, 0:channels] * scale


def unpack_ray(core, mine, other, channels, total_rows):
    return pl.pallas_call(
        functools.partial(ray_kernel, 1.0 / total_rows),
        in_specs=[SCALARS] + [WHOLE] * 2,
        out_specs=[WHOLE] * 2,
        out_shape=[matrix_shape(channels), jax.ShapeDtypeStruct((8, LANES), jnp.float32)],
        scratch_shapes=[pltpu.VMEM((full_rows(channels), LANES), jnp.float32)],
        compiler_params=params(),
        cost_estimate=cost(10**5, 10**5),
    )(core, mine, other)


def part_kernel(
    channels, scale, core_ref, mine_ref, inverse_ref, previous_ref, out_ref,
    pack_ref, lower_ref, before_ref,
):
    rows, wide = inverse_ref.shape
    half = mine_ref.shape[0]
    join(pack_ref, core_ref[0], mine_ref[...], jnp.zeros((half, LANES), jnp.float32))
    turned = dot3(full_matrix(pack_ref, channels), inverse_ref[...], ((1,), (1,)))
    unfold(previous_ref, lower_ref, channels, False)
    lower_matrix(lower_ref, before_ref)
    total = dot3(before_ref[:, 0:rows], turned, ((1,), (0,))) * scale
    out_ref[:, 0:rows] = total.astype(out_ref.dtype)
    if rows < wide:
        out_ref[:, rows:wide] = jnp.zeros((rows, wide - rows), out_ref.dtype)


def correlation_part(core, mine, inverse, previous, channels, total_rows):
    return pl.pallas_call(
        functools.partial(part_kernel, channels, 1.0 / total_rows),
        in_specs=[SCALARS] + [WHOLE] * 3,
        out_specs=WHOLE,
        out_shape=jax.ShapeDtypeStruct(inverse.shape, jnp.bfloat16),
        scratch_shapes=[
            pltpu.VMEM((full_rows(channels), LANES), jnp.float32),
            pltpu.VMEM((lower_rows(channels), LANES), jnp.float32),
            pltpu.VMEM(inverse.shape, jnp.float32),
        ],
        compiler_params=params(),
        cost_estimate=cost(10**5, 10**5),
    )(core, mine, inverse, previous)


def both_kernel(left_ref, right_ref, out_ref):
    channels = out_ref.shape[0]
    total = left_ref[...].astype(jnp.float32) + right_ref[...].astype(jnp.float32)
    out_ref[:, 0, :] = total[0:channels, 0:channels]


def both_parts(left, right, channels):
    return pl.pallas_call(
        both_kernel,
        in_specs=[WHOLE] * 2,
        out_specs=WHOLE,
        out_shape=matrix_shape(channels),
        compiler_params=params(),
        cost_estimate=cost(10**5, 10**5),
    )(left, right)


def from_behind(value, axis, steps):
    count = lax.axis_size(axis)
    leading, last = (max(0, -steps), min(count, count - steps))
    return lax.ppermute(value, axis, [(source, source + steps) for source in range(leading, last)])


def other_core(value):
    return lax.ppermute(value, "rows", [(s, s ^ 1) for s in range(lax.axis_size("rows"))])


def chip_rounds():
    count = lax.axis_size("rows")
    bits = []
    while 2 << len(bits) < count:
        bits.append(2 << len(bits))
    return [
        [(s, s ^ (bits[n] if s % 2 == 0 else bits[-1 - n])) for s in range(count)]
        for n in range(len(bits))
    ]


def shards(x_block, h_diag, h_right, pattern):
    x_t = x_block[0].T
    channels, block_rows = x_t.shape
    masks = pattern[0].transpose(1, 0, 2)
    total_rows = lax.axis_size("rows") * block_rows
    core = (lax.axis_index("rows") % 2).astype(jnp.int32).reshape(1)
    later = from_behind(x_t, "rows", -1)
    carried = from_behind(tile_product(1, masks, x_t, h_right[0], x_t.dtype, 53), "rows", 1)
    first = tile_product(0, masks, x_t, h_diag[0], jnp.float32, 50)
    part = later_product(masks, later, h_right[0], first)
    y_t, g_mine, g_other = gram(core, part, carried)
    previous_y = from_behind(y_t, "sector", 1)
    rounds = chip_rounds()
    g_sum = g_mine + other_core(g_other)
    r_mine, r_other = cross(core, x_t, y_t, g_sum, jnp.bfloat16)
    r_sum = add_after(r_mine, other_core(r_other))
    for n, pairs in enumerate(rounds):
        g_sum = add_after(g_sum, lax.ppermute(g_sum, "rows", pairs), r_sum)
        if n + 1 < len(rounds):
            r_sum = add_after(r_sum, lax.ppermute(r_sum, "rows", pairs))
    work = first_stage(core, g_sum, other_core(g_sum), channels, total_rows)
    r_sum = add_after(r_sum, lax.ppermute(r_sum, "rows", rounds[-1]), work)
    m_mine, m_other = cross(core, previous_y, y_t, r_sum, jnp.float32)
    inverse, pack = last_stages(work, channels, m_other)
    m_sum = add_after(m_mine, other_core(m_other), inverse)
    previous = from_behind(pack, "sector", 1)
    rayleigh, token = unpack_ray(core, r_sum, other_core(r_sum), channels, total_rows)
    q_t = basis(inverse, y_t)
    for pairs in rounds[:-1]:
        m_sum = add_after(m_sum, lax.ppermute(m_sum, "rows", pairs))
    m_sum = add_after(m_sum, lax.ppermute(m_sum, "rows", rounds[-1]), token)
    part = correlation_part(core, m_sum, inverse, previous, channels, total_rows)
    correlation = both_parts(part, other_core(part), channels)
    return (q_t.T[None], rayleigh.transpose(1, 0, 2), correlation.transpose(1, 0, 2))


def solution(mesh):
    in_specs = (
        P("sector", "rows", None),
        P("sector", "rows", None),
        P("sector", "rows", None),
        P("sector", None, "rows", None),
    )
    out_specs = (P("sector", "rows", None), P("sector", None, None), P("sector", None, None))
    return jax.shard_map(shards, mesh=mesh, in_specs=in_specs, out_specs=out_specs, check_vma=False)
```

profile of v0, /device:TPU:0, one launch (start us, length us, event | category | flops | bytes accessed | tf_op | source)
XLA Modules:
  0.0 65.8 jit_solution(1231994529844116357)
XLA Ops:
  0.6 1.4 %collective-permute-start = (bf16[300,1280]{1,0:T(8,128)(2,1)}, bf16[300,1280]{1,0:T(8,128)(2,1)S(1)}, u32[]{:S(2)}, u32[]{:S(2)}) collective-permute-start(bf16[300,1280]{1,0:T(8,128)(2,1)} %bitcast.14), channel_id=1, source_target_pairs={{1,0},{2,1},{3,2},{4,3},{5,4},{6,5},{7,6},{9,8},{10,9},{11,10},{12... | collective-permute-start | bytes 2304008 | tf_op jit(solution)/shard_map/ppermute | solution.py:690
  2.8 3.1 %shard_map.69 = bf16[300,1280]{1,0:T(8,128)(2,1)S(1)} custom-call(s32[10,2,10]{2,1,0:T(2,128)S(1)} %bitcast.18, bf16[300,1280]{1,0:T(8,128)(2,1)} %bitcast.15, bf16[1280,1280]{1,0:T(8,128)(2,1)} %bitcast.21), custom_call_target="tpu_custom_call" | custom-call | flops 983040000 | bytes 3276800 | tf_op jit(solution)/shard_map/pallas_call | solution.py:107
  5.9 3.1 %collective-permute-start.1 = (bf16[300,1280]{1,0:T(8,128)(2,1)S(1)}, bf16[300,1280]{1,0:T(8,128)(2,1)S(1)}, u32[]{:S(2)}, u32[]{:S(2)}) collective-permute-start(bf16[300,1280]{1,0:T(8,128)(2,1)S(1)} %shard_map.69), channel_id=1, source_target_pairs={{0,1},{1,2},{2,3},{3,4},{4,5},{5,6},{6,7},{8,9},{9,10},{10,11},{11... | collective-permute-start | bytes 2304008 | tf_op jit(solution)/shard_map/ppermute | solution.py:690
  9.0 3.3 %shard_map.67.first_ref = f32[300,1280]{1,0:T(8,128)S(1)} custom-call(s32[10,2,10]{2,1,0:T(2,128)S(1)} %bitcast.19, bf16[300,1280]{1,0:T(8,128)(2,1)S(1)} %bitcast.16, bf16[1280,1280]{1,0:T(8,128)(2,1)} %bitcast.23), custom_call_target="tpu_custom_call" | custom-call | flops 983040000 | bytes 3276800 | tf_op jit(solution)/shard_map/pallas_call | solution.py:107
  12.3 3.1 %shard_map.68.part_ref = f32[300,1280]{1,0:T(8,128)S(1)} custom-call(s32[10,2,10]{2,1,0:T(2,128)S(1)} %bitcast.20, bf16[300,1280]{1,0:T(8,128)(2,1)S(1)} %collective-permute-done.later_ref, bf16[1280,1280]{1,0:T(8,128)(2,1)} %bitcast.22, f32[300,1280]{1,0:T(8,128)S(1)} %shard_map.67.first_ref), custom_call_target="tpu_custom_call" | custom-call | flops 983040000 | bytes 3276800 | tf_op jit(solution)/shard_map/pallas_call | solution.py:142
  16.1 4.9 %collective-permute-start.2 = (f32[208,128]{1,0:T(8,128)S(1)}, f32[208,128]{1,0:T(8,128)S(1)}, u32[]{:S(2)}, u32[]{:S(2)}) collective-permute-start(f32[208,128]{1,0:T(8,128)S(1)} %get-tuple-element.15), channel_id=1, source_target_pairs={{0,1},{1,0},{2,3},{3,2},{4,5},{5,4},{6,7},{7,6},{8,9},{9,8},{10,11... | collective-permute-start | bytes 319496 | tf_op jit(solution)/shard_map/ppermute | solution.py:694
  21.0 3.5 %collective-permute-start.8 = (bf16[300,1280]{1,0:T(8,128)(2,1)S(1)}, bf16[300,1280]{1,0:T(8,128)(2,1)S(1)}, u32[]{:S(2)}, u32[]{:S(2)}) collective-permute-start(bf16[300,1280]{1,0:T(8,128)(2,1)S(1)} %get-tuple-element.16.right_ref.y_ref), channel_id=1, source_target_pairs={{0,8},{8,16},{16,24},{1,9},{9,17},{17,25},{2,10},{10,18},{18,26},{... | collective-permute-start | bytes 2304008 | tf_op jit(solution)/shard_map/ppermute | solution.py:690
  24.5 3.4 %collective-permute-start.3 = (f32[208,128]{1,0:T(8,128)S(1)}, f32[208,128]{1,0:T(8,128)S(1)}, u32[]{:S(2)}, u32[]{:S(2)}) collective-permute-start(f32[208,128]{1,0:T(8,128)S(1)} %add.8.after_ref.left_ref), channel_id=1, source_target_pairs={{0,2},{1,5},{2,0},{3,7},{4,6},{5,1},{6,4},{7,3},{8,10},{9,13},{10,... | collective-permute-start | bytes 319496 | tf_op jit(solution)/shard_map/ppermute | solution.py:725
  28.8 1.8 %collective-permute-start.4 = (bf16[384,128]{1,0:T(8,128)(2,1)S(1)}, bf16[384,128]{1,0:T(8,128)(2,1)S(1)}, u32[]{:S(2)}, u32[]{:S(2)}) collective-permute-start(bf16[384,128]{1,0:T(8,128)(2,1)S(1)} %get-tuple-element.18), channel_id=1, source_target_pairs={{0,1},{1,0},{2,3},{3,2},{4,5},{5,4},{6,7},{7,6},{8,9},{9,8},{10,11... | collective-permute-start | bytes 294920 | tf_op jit(solution)/shard_map/ppermute | solution.py:694
  30.6 0.9 %collective-permute-done.4.right_ref = bf16[384,128]{1,0:T(8,128)(2,1)S(1)} collective-permute-done((bf16[384,128]{1,0:T(8,128)(2,1)S(1)}, bf16[384,128]{1,0:T(8,128)(2,1)S(1)}, u32[]{:S(2)}, u32[]{:S(2)}) %collective-permute-start.4) | collective-permute-done | bytes 98336 | tf_op jit(solution)/shard_map/ppermute | solution.py:694
  31.6 3.0 %collective-permute-start.5 = (f32[208,128]{1,0:T(8,128)S(1)}, f32[208,128]{1,0:T(8,128)S(1)}, u32[]{:S(2)}, u32[]{:S(2)}) collective-permute-start(f32[208,128]{1,0:T(8,128)S(1)} %shard_map.73.left_ref), channel_id=1, source_target_pairs={{0,4},{1,3},{2,6},{3,1},{4,0},{5,7},{6,2},{7,5},{8,12},{9,11},{10,... | collective-permute-start | bytes 319496 | tf_op jit(solution)/shard_map/ppermute | solution.py:725
  34.6 1.4 %collective-permute-start.6 = (bf16[384,128]{1,0:T(8,128)(2,1)S(1)}, bf16[384,128]{1,0:T(8,128)(2,1)S(1)}, u32[]{:S(2)}, u32[]{:S(2)}) collective-permute-start(bf16[384,128]{1,0:T(8,128)(2,1)S(1)} %shard_map.72.refs_0_.left_ref), channel_id=1, source_target_pairs={{0,2},{1,5},{2,0},{3,7},{4,6},{5,1},{6,4},{7,3},{8,10},{9,13},{10,... | collective-permute-start | bytes 294920 | tf_op jit(solution)/shard_map/ppermute | solution.py:727
  36.0 3.2 %collective-permute-done.6.right_ref = bf16[384,128]{1,0:T(8,128)(2,1)S(1)} collective-permute-done((bf16[384,128]{1,0:T(8,128)(2,1)S(1)}, bf16[384,128]{1,0:T(8,128)(2,1)S(1)}, u32[]{:S(2)}, u32[]{:S(2)}) %collective-permute-start.6) | collective-permute-done | bytes 98336 | tf_op jit(solution)/shard_map/ppermute | solution.py:727
  40.6 5.5 %shard_map.76.refs_0_.before_ref = f32[304,384]{1,0:T(8,128)S(1)} custom-call(s32[1]{0:T(128)} %bitcast.core_ref, f32[208,128]{1,0:T(8,128)S(1)} %shard_map.75.mine_ref, f32[208,128]{1,0:T(8,128)S(1)} %collective-permute-done.7.other_ref), custom_call_target="tpu_custom_call" | custom-call | flops 3500000000 | bytes 1000000 | tf_op jit(solution)/shard_map/pallas_call | solution.py:533
  47.5 2.9 %shard_map.79 = (f32[304,384]{1,0:T(8,128)S(1)}, f32[416,128]{1,0:T(8,128)S(1)}) custom-call(f32[304,384]{1,0:T(8,128)S(1)} %shard_map.76.refs_0_.before_ref, f32[384,128]{1,0:T(8,128)S(1)} %get-tuple-element.19.after_ref), custom_call_target="tpu_custom_call" | custom-call | flops 4000000000 | bytes 100000 | tf_op jit(solution)/shard_map/pallas_call | solution.py:549
  50.4 1.3 %collective-permute-start.12 = (f32[384,128]{1,0:T(8,128)S(1)}, f32[384,128]{1,0:T(8,128)S(1)}, u32[]{:S(2)}, u32[]{:S(2)}) collective-permute-start(f32[384,128]{1,0:T(8,128)S(1)} %shard_map.82.left_ref), channel_id=1, source_target_pairs={{0,2},{1,5},{2,0},{3,7},{4,6},{5,1},{6,4},{7,3},{8,10},{9,13},{10,... | collective-permute-start | bytes 589832 | tf_op jit(solution)/shard_map/ppermute | solution.py:737
  51.7 3.4 %collective-permute-start.14 = (f32[416,128]{1,0:T(8,128)S(1)}, f32[416,128]{1,0:T(8,128)S(1)}, u32[]{:S(2)}, u32[]{:S(2)}) collective-permute-start(f32[416,128]{1,0:T(8,128)S(1)} %get-tuple-element.24), channel_id=1, source_target_pairs={{0,8},{8,16},{16,24},{1,9},{9,17},{17,25},{2,10},{10,18},{18,26},{... | collective-permute-start | bytes 638984 | tf_op jit(solution)/shard_map/ppermute | solution.py:690
  55.1 1.0 %collective-permute-done.12.right_ref = f32[384,128]{1,0:T(8,128)S(1)} collective-permute-done((f32[384,128]{1,0:T(8,128)S(1)}, f32[384,128]{1,0:T(8,128)S(1)}, u32[]{:S(2)}, u32[]{:S(2)}) %collective-permute-start.12) | collective-permute-done | bytes 196640 | tf_op jit(solution)/shard_map/ppermute | solution.py:737
  56.7 1.3 %collective-permute-done.10.other_ref = bf16[384,128]{1,0:T(8,128)(2,1)S(1)} collective-permute-done((bf16[384,128]{1,0:T(8,128)(2,1)S(1)}, bf16[384,128]{1,0:T(8,128)(2,1)S(1)}, u32[]{:S(2)}, u32[]{:S(2)}) %collective-permute-start.10) | collective-permute-done | bytes 98336 | tf_op jit(solution)/shard_map/ppermute | solution.py:694
  58.0 1.0 %shard_map.81 = (f32[300,1,300]{2,1,0:T(1,128)}, f32[8,128]{1,0:T(8,128)S(1)}) custom-call(s32[1]{0:T(128)} %bitcast.core_ref, bf16[384,128]{1,0:T(8,128)(2,1)S(1)} %shard_map.77.after_ref.mine_ref, bf16[384,128]{1,0:T(8,128)(2,1)S(1)} %collective-permute-done.10.other_ref), custom_call_target="tpu_custom_call" | custom-call | flops 100000 | bytes 100000 | tf_op jit(solution)/shard_map/pallas_call | solution.py:627
  59.0 2.9 %collective-permute-done.13.right_ref = f32[384,128]{1,0:T(8,128)S(1)} collective-permute-done((f32[384,128]{1,0:T(8,128)S(1)}, f32[384,128]{1,0:T(8,128)S(1)}, u32[]{:S(2)}, u32[]{:S(2)}) %collective-permute-start.13) | collective-permute-done | bytes 196640 | tf_op jit(solution)/shard_map/ppermute | solution.py:738
  61.9 1.3 %shard_map.85.left_ref = bf16[304,384]{1,0:T(8,128)(2,1)S(1)} custom-call(s32[1]{0:T(128)} %bitcast.core_ref, f32[384,128]{1,0:T(8,128)S(1)} %shard_map.84.mine_ref, f32[304,384]{1,0:T(8,128)S(1)} %get-tuple-element.20.inverse_ref.refs_0_, f32[416,128]{1,0:T(8,128)S(1)} %collective-permute-done.14.previous_ref), custom_call_target="tpu_custom_call" | custom-call | flops 100000 | bytes 100000 | tf_op jit(solution)/shard_map/pallas_call | solution.py:655
  63.3 1.5 %shard_map.80 = bf16[300,1280]{1,0:T(8,128)(2,1)} custom-call(f32[304,384]{1,0:T(8,128)S(1)} %get-tuple-element.20.inverse_ref.refs_0_, bf16[300,1280]{1,0:T(8,128)(2,1)S(1)} %get-tuple-element.16.right_ref.y_ref), custom_call_target="tpu_custom_call" | custom-call | flops 100000 | bytes 100000 | tf_op jit(solution)/shard_map/pallas_call | solution.py:605
  64.8 0.9 %shard_map.86 = f32[300,1,300]{2,1,0:T(1,128)} custom-call(bf16[304,384]{1,0:T(8,128)(2,1)S(1)} %shard_map.85.left_ref, bf16[304,384]{1,0:T(8,128)(2,1)S(1)} %collective-permute-done.15.right_ref), custom_call_target="tpu_custom_call" | custom-call | flops 100000 | bytes 100000 | tf_op jit(solution)/shard_map/pallas_call | solution.py:677
  (35 shorter events, 5.5 us)
Async XLA Ops:
  0.6 8.4 %copy-start = (bf16[1,1280,300]{1,2,0:T(8,128)(2,1)S(1)}, bf16[1,1280,300]{1,2,0:T(8,128)(2,1)}, u32[]{:S(2)}) copy-start(bf16[1,1280,300]{1,2,0:T(8,128)(2,1)} %param.4) | copy-start | bytes 2304004
  0.6 11.7 %collective-permute-start = (bf16[300,1280]{1,0:T(8,128)(2,1)}, bf16[300,1280]{1,0:T(8,128)(2,1)S(1)}, u32[]{:S(2)}, u32[]{:S(2)}) collective-permute-start(bf16[300,1280]{1,0:T(8,128)(2,1)} %bitcast.14), channel_id=1, source_target_pairs={{1,0},{2,1},{3,2},{4,3},{5,4},{6,5},{7,6},{9,8},{10,9},{11,10},{12... | collective-permute-start | bytes 2304008 | tf_op jit(solution)/shard_map/ppermute | solution.py:690
  2.1 0.7 %copy-start.1 = (s32[1,2,10,10]{3,1,2,0:T(2,128)S(1)}, s32[1,2,10,10]{3,1,2,0:T(2,128)}, u32[]{:S(2)}) copy-start(s32[1,2,10,10]{3,1,2,0:T(2,128)} %param.7) | copy-start | bytes 2404
  2.8 6.3 %copy-start.2 = (s32[1,2,10,10]{3,1,2,0:T(2,128)S(1)}, s32[1,2,10,10]{3,1,2,0:T(2,128)}, u32[]{:S(2)}) copy-start(s32[1,2,10,10]{3,1,2,0:T(2,128)} %param.7) | copy-start | bytes 2404
  5.9 9.6 %collective-permute-start.1 = (bf16[300,1280]{1,0:T(8,128)(2,1)S(1)}, bf16[300,1280]{1,0:T(8,128)(2,1)S(1)}, u32[]{:S(2)}, u32[]{:S(2)}) collective-permute-start(bf16[300,1280]{1,0:T(8,128)(2,1)S(1)} %shard_map.69), channel_id=1, source_target_pairs={{0,1},{1,2},{2,3},{3,4},{4,5},{5,6},{6,7},{8,9},{9,10},{10,11},{11... | collective-permute-start | bytes 2304008 | tf_op jit(solution)/shard_map/ppermute | solution.py:690
  16.1 8.4 %collective-permute-start.2 = (f32[208,128]{1,0:T(8,128)S(1)}, f32[208,128]{1,0:T(8,128)S(1)}, u32[]{:S(2)}, u32[]{:S(2)}) collective-permute-start(f32[208,128]{1,0:T(8,128)S(1)} %get-tuple-element.15), channel_id=1, source_target_pairs={{0,1},{1,0},{2,3},{3,2},{4,5},{5,4},{6,7},{7,6},{8,9},{9,8},{10,11... | collective-permute-start | bytes 319496 | tf_op jit(solution)/shard_map/ppermute | solution.py:694
  21.0 25.2 %collective-permute-start.8 = (bf16[300,1280]{1,0:T(8,128)(2,1)S(1)}, bf16[300,1280]{1,0:T(8,128)(2,1)S(1)}, u32[]{:S(2)}, u32[]{:S(2)}) collective-permute-start(bf16[300,1280]{1,0:T(8,128)(2,1)S(1)} %get-tuple-element.16.right_ref.y_ref), channel_id=1, source_target_pairs={{0,8},{8,16},{16,24},{1,9},{9,17},{17,25},{2,10},{10,18},{18,26},{... | collective-permute-start | bytes 2304008 | tf_op jit(solution)/shard_map/ppermute | solution.py:690
  24.5 7.0 %collective-permute-start.3 = (f32[208,128]{1,0:T(8,128)S(1)}, f32[208,128]{1,0:T(8,128)S(1)}, u32[]{:S(2)}, u32[]{:S(2)}) collective-permute-start(f32[208,128]{1,0:T(8,128)S(1)} %add.8.after_ref.left_ref), channel_id=1, source_target_pairs={{0,2},{1,5},{2,0},{3,7},{4,6},{5,1},{6,4},{7,3},{8,10},{9,13},{10,... | collective-permute-start | bytes 319496 | tf_op jit(solution)/shard_map/ppermute | solution.py:725
  28.8 2.8 %collective-permute-start.4 = (bf16[384,128]{1,0:T(8,128)(2,1)S(1)}, bf16[384,128]{1,0:T(8,128)(2,1)S(1)}, u32[]{:S(2)}, u32[]{:S(2)}) collective-permute-start(bf16[384,128]{1,0:T(8,128)(2,1)S(1)} %get-tuple-element.18), channel_id=1, source_target_pairs={{0,1},{1,0},{2,3},{3,2},{4,5},{5,4},{6,7},{7,6},{8,9},{9,8},{10,11... | collective-permute-start | bytes 294920 | tf_op jit(solution)/shard_map/ppermute | solution.py:694
  31.6 7.6 %collective-permute-start.5 = (f32[208,128]{1,0:T(8,128)S(1)}, f32[208,128]{1,0:T(8,128)S(1)}, u32[]{:S(2)}, u32[]{:S(2)}) collective-permute-start(f32[208,128]{1,0:T(8,128)S(1)} %shard_map.73.left_ref), channel_id=1, source_target_pairs={{0,4},{1,3},{2,6},{3,1},{4,0},{5,7},{6,2},{7,5},{8,12},{9,11},{10,... | collective-permute-start | bytes 319496 | tf_op jit(solution)/shard_map/ppermute | solution.py:725
  34.6 4.6 %collective-permute-start.6 = (bf16[384,128]{1,0:T(8,128)(2,1)S(1)}, bf16[384,128]{1,0:T(8,128)(2,1)S(1)}, u32[]{:S(2)}, u32[]{:S(2)}) collective-permute-start(bf16[384,128]{1,0:T(8,128)(2,1)S(1)} %shard_map.72.refs_0_.left_ref), channel_id=1, source_target_pairs={{0,2},{1,5},{2,0},{3,7},{4,6},{5,1},{6,4},{7,3},{8,10},{9,13},{10,... | collective-permute-start | bytes 294920 | tf_op jit(solution)/shard_map/ppermute | solution.py:727
  39.3 1.4 %collective-permute-start.7 = (f32[208,128]{1,0:T(8,128)S(1)}, f32[208,128]{1,0:T(8,128)S(1)}, u32[]{:S(2)}, u32[]{:S(2)}) collective-permute-start(f32[208,128]{1,0:T(8,128)S(1)} %shard_map.75.mine_ref), channel_id=1, source_target_pairs={{0,1},{1,0},{2,3},{3,2},{4,5},{5,4},{6,7},{7,6},{8,9},{9,8},{10,11... | collective-permute-start | bytes 319496 | tf_op jit(solution)/shard_map/ppermute | solution.py:694
  39.3 6.8 %collective-permute-start.9 = (bf16[384,128]{1,0:T(8,128)(2,1)S(1)}, bf16[384,128]{1,0:T(8,128)(2,1)S(1)}, u32[]{:S(2)}, u32[]{:S(2)}) collective-permute-start(bf16[384,128]{1,0:T(8,128)(2,1)S(1)} %shard_map.74.refs_0_.left_ref), channel_id=1, source_target_pairs={{0,4},{1,3},{2,6},{3,1},{4,0},{5,7},{6,2},{7,5},{8,12},{9,11},{10,... | collective-permute-start | bytes 294920 | tf_op jit(solution)/shard_map/ppermute | solution.py:729
  47.0 3.3 %collective-permute-start.11 = (f32[384,128]{1,0:T(8,128)S(1)}, f32[384,128]{1,0:T(8,128)S(1)}, u32[]{:S(2)}, u32[]{:S(2)}) collective-permute-start(f32[384,128]{1,0:T(8,128)S(1)} %get-tuple-element.19.after_ref), channel_id=1, source_target_pairs={{0,1},{1,0},{2,3},{3,2},{4,5},{5,4},{6,7},{7,6},{8,9},{9,8},{10,11... | collective-permute-start | bytes 589832 | tf_op jit(solution)/shard_map/ppermute | solution.py:694
  50.4 5.7 %collective-permute-start.12 = (f32[384,128]{1,0:T(8,128)S(1)}, f32[384,128]{1,0:T(8,128)S(1)}, u32[]{:S(2)}, u32[]{:S(2)}) collective-permute-start(f32[384,128]{1,0:T(8,128)S(1)} %shard_map.82.left_ref), channel_id=1, source_target_pairs={{0,2},{1,5},{2,0},{3,7},{4,6},{5,1},{6,4},{7,3},{8,10},{9,13},{10,... | collective-permute-start | bytes 589832 | tf_op jit(solution)/shard_map/ppermute | solution.py:737
  51.7 10.2 %collective-permute-start.14 = (f32[416,128]{1,0:T(8,128)S(1)}, f32[416,128]{1,0:T(8,128)S(1)}, u32[]{:S(2)}, u32[]{:S(2)}) collective-permute-start(f32[416,128]{1,0:T(8,128)S(1)} %get-tuple-element.24), channel_id=1, source_target_pairs={{0,8},{8,16},{16,24},{1,9},{9,17},{17,25},{2,10},{10,18},{18,26},{... | collective-permute-start | bytes 638984 | tf_op jit(solution)/shard_map/ppermute | solution.py:690
  56.2 5.7 %collective-permute-start.13 = (f32[384,128]{1,0:T(8,128)S(1)}, f32[384,128]{1,0:T(8,128)S(1)}, u32[]{:S(2)}, u32[]{:S(2)}) collective-permute-start(f32[384,128]{1,0:T(8,128)S(1)} %shard_map.83.left_ref), channel_id=1, source_target_pairs={{0,4},{1,3},{2,6},{3,1},{4,0},{5,7},{6,2},{7,5},{8,12},{9,11},{10,... | collective-permute-start | bytes 589832 | tf_op jit(solution)/shard_map/ppermute | solution.py:738
  56.7 1.3 %collective-permute-start.10 = (bf16[384,128]{1,0:T(8,128)(2,1)S(1)}, bf16[384,128]{1,0:T(8,128)(2,1)S(1)}, u32[]{:S(2)}, u32[]{:S(2)}) collective-permute-start(bf16[384,128]{1,0:T(8,128)(2,1)S(1)} %shard_map.77.after_ref.mine_ref), channel_id=1, source_target_pairs={{0,1},{1,0},{2,3},{3,2},{4,5},{5,4},{6,7},{7,6},{8,9},{9,8},{10,11... | collective-permute-start | bytes 294920 | tf_op jit(solution)/shard_map/ppermute | solution.py:694
  63.2 1.6 %collective-permute-start.15 = (bf16[304,384]{1,0:T(8,128)(2,1)S(1)}, bf16[304,384]{1,0:T(8,128)(2,1)S(1)}, u32[]{:S(2)}, u32[]{:S(2)}) collective-permute-start(bf16[304,384]{1,0:T(8,128)(2,1)S(1)} %shard_map.85.left_ref), channel_id=1, source_target_pairs={{0,1},{1,0},{2,3},{3,2},{4,5},{5,4},{6,7},{7,6},{8,9},{9,8},{10,11... | collective-permute-start | bytes 700424 | tf_op jit(solution)/shard_map/ppermute | solution.py:694
where the time goes:
time: 66.1 us; the launch traced here: 65.8 us
  starting transfers between devices  29.2 us (44%)
  Pallas kernels  25 us (38%)
  waiting for transfers between devices  9.93 us (15%)
  between operations  0.91 us (1%)
  local copies, waits for them, and re-layouts  0.7 us (1%)
    ppermute x4, starting transfers between devices, from_behind(): lax.ppermute(value, axis, [(source, source + steps) for source in range(l...  11.5 us
    ppermute x6, starting transfers between devices, other_core(): lax.ppermute(value, 'rows', [(s, s ^ 1) for s in range(lax.axis_size('row...  7.3 us
    ppermute x2, starting transfers between devices, shards(): g_sum = add_after(g_sum, lax.ppermute(g_sum, 'rows', pairs), r_sum)  6.42 us
    pallas_call x2, Pallas kernels, tile_product(): pl.pallas_call(functools.partial(tile_kernel, which), in_specs=[WHOLE, AN...  6.41 us
    pallas_call x1, Pallas kernels, first_stage(): pl.pallas_call(functools.partial(first_stage_kernel, channels, 1.0 / tota...  5.53 us
    ppermute x1, waiting for transfers between devices, shards(): r_sum = add_after(r_sum, lax.ppermute(r_sum, 'rows', pairs))  3.17 us
    pallas_call x1, Pallas kernels, later_product(): pl.pallas_call(later_kernel, in_specs=[WHOLE, WHOLE, ANYWHERE, WHOLE], ou...  3.15 us
    ppermute x1, waiting for transfers between devices, shards(): m_sum = add_after(m_sum, lax.ppermute(m_sum, 'rows', rounds[-1]), token)  2.9 us
  transfers between devices with their start and end apart: 16, of which 6 were waited for; matrix products, arithmetic and copies ran while one was open for 0% of the time, Pallas kernels for 33%

commit v1 on v0

--- a/solution.py
+++ b/solution.py
@@ -10,12 +10,12 @@
 SUBBLOCK = 128
 LANES = 128
 PANEL = 16
-EARLY_PANELS = 4
+EARLY_PANELS = 6
 WHOLE = pl.BlockSpec(memory_space=pltpu.VMEM)
 SCALARS = pl.BlockSpec(memory_space=pltpu.SMEM)
 ANYWHERE = pl.BlockSpec(memory_space=pl.ANY)
 MIB = 1024 * 1024
-FIRST_STAGE_FLOPS = 3500 * 10**6
+FIRST_STAGE_FLOPS = 5500 * 10**6
 LAST_STAGES_FLOPS = 4 * 10**9
 
 
@@ -335,6 +335,24 @@
 def add_kernel(left_ref, right_ref, *refs):
     total = left_ref[...].astype(jnp.float32) + right_ref[...].astype(jnp.float32)
     refs[-1][...] = total.astype(refs[-1].dtype)
+
+
+def add_four_kernel(own_ref, first_ref, second_ref, both_ref, after_ref, out_ref):
+    own, first, second, both = (
+        ref[...].astype(jnp.float32) for ref in (own_ref, first_ref, second_ref, both_ref)
+    )
+    out_ref[...] = ((own + first) + (second + both)).astype(out_ref.dtype)
+
+
+def add_four(own, first, second, both, after):
+    return pl.pallas_call(
+        add_four_kernel,
+        in_specs=[WHOLE] * 4 + [ANYWHERE],
+        out_specs=WHOLE,
+        out_shape=jax.ShapeDtypeStruct(own.shape, own.dtype),
+        compiler_params=params(),
+        cost_estimate=cost(10**5, 10**5),
+    )(own, first, second, both, after)
 
 
 def add_after(left, right, *after):
@@ -590,9 +608,10 @@
         offset += rows - top
 
 
-def basis_kernel(inverse_ref, y_ref, q_ref):
+def basis_kernel(inverse_ref, y_ref, q_ref, token_ref):
     channels = y_ref.shape[0]
     image = y_ref[...]
+    token_ref[...] = jnp.zeros_like(token_ref)
     for start, size in strips(channels, 2 * LANES):
         used = min(channels, start + size)
         high, low = split2(inverse_ref[start : start + size, 0:used])
@@ -605,8 +624,11 @@
     return pl.pallas_call(
         basis_kernel,
         in_specs=[WHOLE] * 2,
-        out_specs=WHOLE,
-        out_shape=jax.ShapeDtypeStruct(y_t.shape, y_t.dtype),
+        out_specs=[WHOLE] * 2,
+        out_shape=[
+            jax.ShapeDtypeStruct(y_t.shape, y_t.dtype),
+            jax.ShapeDtypeStruct((8, LANES), jnp.float32),
+        ],
         compiler_params=params(),
         cost_estimate=cost(10**5, 10**5),
     )(inverse, y_t)
@@ -703,6 +725,18 @@
         [(s, s ^ (bits[n] if s % 2 == 0 else bits[-1 - n])) for s in range(count)]
         for n in range(len(bits))
     ]
+
+
+def sum_chips(value, after):
+    count = lax.axis_size("rows")
+    if count == 8:
+        others = [
+            lax.ppermute(value, "rows", [(s, s ^ bits) for s in range(count)]) for bits in (2, 4, 6)
+        ]
+        return add_four(value, *others, after)
+    for pairs in chip_rounds():
+        value = add_after(value, lax.ppermute(value, "rows", pairs), after)
+    return value
 
 
 def shards(x_block, h_diag, h_right, pattern):
@@ -721,21 +755,18 @@
     g_sum = g_mine + other_core(g_other)
     r_mine, r_other = cross(core, x_t, y_t, g_sum, jnp.bfloat16)
     r_sum = add_after(r_mine, other_core(r_other))
-    for n, pairs in enumerate(rounds):
-        g_sum = add_after(g_sum, lax.ppermute(g_sum, "rows", pairs), r_sum)
-        if n + 1 < len(rounds):
-            r_sum = add_after(r_sum, lax.ppermute(r_sum, "rows", pairs))
+    g_sum = sum_chips(g_sum, r_sum)
     work = first_stage(core, g_sum, other_core(g_sum), channels, total_rows)
-    r_sum = add_after(r_sum, lax.ppermute(r_sum, "rows", rounds[-1]), work)
+    r_sum = sum_chips(r_sum, work)
     m_mine, m_other = cross(core, previous_y, y_t, r_sum, jnp.float32)
     inverse, pack = last_stages(work, channels, m_other)
     m_sum = add_after(m_mine, other_core(m_other), inverse)
     previous = from_behind(pack, "sector", 1)
     rayleigh, token = unpack_ray(core, r_sum, other_core(r_sum), channels, total_rows)
-    q_t = basis(inverse, y_t)
+    q_t, basis_token = basis(inverse, y_t)
     for pairs in rounds[:-1]:
         m_sum = add_after(m_sum, lax.ppermute(m_sum, "rows", pairs))
-    m_sum = add_after(m_sum, lax.ppermute(m_sum, "rows", rounds[-1]), token)
+    m_sum = add_after(m_sum, lax.ppermute(m_sum, "rows", rounds[-1]), token, basis_token)
     part = correlation_part(core, m_sum, inverse, previous, channels, total_rows)
     correlation = both_parts(part, other_core(part), channels)
     return (q_t.T[None], rayleigh.transpose(1, 0, 2), correlation.transpose(1, 0, 2))

time: 66.1 us -> 65.5 us (level)
  waiting for transfers between devices: 9.93 us -> 8.87 us
    ppermute x5 -> x7, starting transfers between devices: 9.14 us -> 11.8 us  [the longest x6 10.3 us: sum_chips(): lax.ppermute(value, 'rows', [(s, s ^ bits) for s in range(count)])]
    ppermute x5 -> x7, waiting for transfers between devices: 6.08 us -> 3.76 us  [the longest x6 3.38 us: sum_chips(): lax.ppermute(value, 'rows', [(s, s ^ bits) for s in range(count)])]
    ppermute x6, starting transfers between devices: 7.3 us -> 5.19 us  [other_core(): lax.ppermute(value, 'rows', [(s, s ^ 1) for s in range(lax.axis_size('row...]
    ppermute x6, waiting for transfers between devices: 2.84 us -> 4.08 us  [other_core(): lax.ppermute(value, 'rows', [(s, s ^ 1) for s in range(lax.axis_size('row...]
    pallas_call x1, Pallas kernels: 2.88 us -> 1.93 us  [last_stages(): pl.pallas_call(functools.partial(last_stages_kernel, channels), in_specs=...]
    pallas_call x1, Pallas kernels: 5.53 us -> 6.39 us  [first_stage(): pl.pallas_call(functools.partial(first_stage_kernel, channels, 1.0 / tota...]
    pallas_call x1 -> x3, Pallas kernels: 1.55 us -> 1.63 us  [the longest x1 1.54 us: basis(): pl.pallas_call(basis_kernel, in_specs=[WHOLE] * 2, out_specs=[WHOLE] * 2,...]
  transfers between devices with their start and end apart: 16 -> 18, of which waited for: 6 -> 7; matrix products, arithmetic and copies ran while one was open for 0% -> 0% of each run, Pallas kernels for 33% -> 33%
where the time goes in v1:
time: 65.5 us; the launch traced here: 65.2 us
  starting transfers between devices  29.7 us (45%)
  Pallas kernels  24.9 us (38%)
  waiting for transfers between devices  8.87 us (14%)
  between operations  0.92 us (1%)
  local copies, waits for them, and re-layouts  0.7 us (1%)
    ppermute x4, starting transfers between devices, from_behind(): lax.ppermute(value, axis, [(source, source + steps) for source in range(l...  11.5 us
    ppermute x6, starting transfers between devices, sum_chips(): lax.ppermute(value, 'rows', [(s, s ^ bits) for s in range(count)])  10.3 us
    pallas_call x2, Pallas kernels, tile_product(): pl.pallas_call(functools.partial(tile_kernel, which), in_specs=[WHOLE, AN...  6.41 us
    pallas_call x1, Pallas kernels, first_stage(): pl.pallas_call(functools.partial(first_stage_kernel, channels, 1.0 / tota...  6.39 us
    ppermute x6, starting transfers between devices, other_core(): lax.ppermute(value, 'rows', [(s, s ^ 1) for s in range(lax.axis_size('row...  5.19 us
    ppermute x6, waiting for transfers between devices, other_core(): lax.ppermute(value, 'rows', [(s, s ^ 1) for s in range(lax.axis_size('row...  4.08 us
    ppermute x6, waiting for transfers between devices, sum_chips(): lax.ppermute(value, 'rows', [(s, s ^ bits) for s in range(count)])  3.38 us
    pallas_call x1, Pallas kernels, later_product(): pl.pallas_call(later_kernel, in_specs=[WHOLE, WHOLE, ANYWHERE, WHOLE], ou...  3.15 us
  transfers between devices with their start and end apart: 18, of which 7 were waited for; matrix products, arithmetic and copies ran while one was open for 0% of the time, Pallas kernels for 33%

profile of v1, /device:TPU:0, one launch (start us, length us, event | category | flops | bytes accessed | tf_op | source)
XLA Modules:
  0.0 65.2 jit_solution(2038300332573288470)
XLA Ops:
  0.6 1.4 %collective-permute-start = (bf16[300,1280]{1,0:T(8,128)(2,1)}, bf16[300,1280]{1,0:T(8,128)(2,1)S(1)}, u32[]{:S(2)}, u32[]{:S(2)}) collective-permute-start(bf16[300,1280]{1,0:T(8,128)(2,1)} %bitcast.14), channel_id=1, source_target_pairs={{1,0},{2,1},{3,2},{4,3},{5,4},{6,5},{7,6},{9,8},{10,9},{11,10},{12... | collective-permute-start | bytes 2304008 | tf_op jit(solution)/shard_map/ppermute | solution.py:712
  2.8 3.1 %shard_map.69 = bf16[300,1280]{1,0:T(8,128)(2,1)S(1)} custom-call(s32[10,2,10]{2,1,0:T(2,128)S(1)} %bitcast.18, bf16[300,1280]{1,0:T(8,128)(2,1)} %bitcast.15, bf16[1280,1280]{1,0:T(8,128)(2,1)} %bitcast.21), custom_call_target="tpu_custom_call" | custom-call | flops 983040000 | bytes 3276800 | tf_op jit(solution)/shard_map/pallas_call | solution.py:107
  5.9 3.1 %collective-permute-start.1 = (bf16[300,1280]{1,0:T(8,128)(2,1)S(1)}, bf16[300,1280]{1,0:T(8,128)(2,1)S(1)}, u32[]{:S(2)}, u32[]{:S(2)}) collective-permute-start(bf16[300,1280]{1,0:T(8,128)(2,1)S(1)} %shard_map.69), channel_id=1, source_target_pairs={{0,1},{1,2},{2,3},{3,4},{4,5},{5,6},{6,7},{8,9},{9,10},{10,11},{11... | collective-permute-start | bytes 2304008 | tf_op jit(solution)/shard_map/ppermute | solution.py:712
  9.0 3.3 %shard_map.67.first_ref = f32[300,1280]{1,0:T(8,128)S(1)} custom-call(s32[10,2,10]{2,1,0:T(2,128)S(1)} %bitcast.19, bf16[300,1280]{1,0:T(8,128)(2,1)S(1)} %bitcast.16, bf16[1280,1280]{1,0:T(8,128)(2,1)} %bitcast.23), custom_call_target="tpu_custom_call" | custom-call | flops 983040000 | bytes 3276800 | tf_op jit(solution)/shard_map/pallas_call | solution.py:107
  12.3 3.1 %shard_map.68.part_ref = f32[300,1280]{1,0:T(8,128)S(1)} custom-call(s32[10,2,10]{2,1,0:T(2,128)S(1)} %bitcast.20, bf16[300,1280]{1,0:T(8,128)(2,1)S(1)} %collective-permute-done.later_ref, bf16[1280,1280]{1,0:T(8,128)(2,1)} %bitcast.22, f32[300,1280]{1,0:T(8,128)S(1)} %shard_map.67.first_ref), custom_call_target="tpu_custom_call" | custom-call | flops 983040000 | bytes 3276800 | tf_op jit(solution)/shard_map/pallas_call | solution.py:142
  16.1 4.9 %collective-permute-start.2 = (f32[208,128]{1,0:T(8,128)S(1)}, f32[208,128]{1,0:T(8,128)S(1)}, u32[]{:S(2)}, u32[]{:S(2)}) collective-permute-start(f32[208,128]{1,0:T(8,128)S(1)} %get-tuple-element.17), channel_id=1, source_target_pairs={{0,1},{1,0},{2,3},{3,2},{4,5},{5,4},{6,7},{7,6},{8,9},{9,8},{10,11... | collective-permute-start | bytes 319496 | tf_op jit(solution)/shard_map/ppermute | solution.py:716
  21.0 3.5 %collective-permute-start.8 = (bf16[300,1280]{1,0:T(8,128)(2,1)S(1)}, bf16[300,1280]{1,0:T(8,128)(2,1)S(1)}, u32[]{:S(2)}, u32[]{:S(2)}) collective-permute-start(bf16[300,1280]{1,0:T(8,128)(2,1)S(1)} %get-tuple-element.18.right_ref.y_ref), channel_id=1, source_target_pairs={{0,8},{8,16},{16,24},{1,9},{9,17},{17,25},{2,10},{10,18},{18,26},{... | collective-permute-start | bytes 2304008 | tf_op jit(solution)/shard_map/ppermute | solution.py:712
  24.5 3.4 %collective-permute-start.3 = (f32[208,128]{1,0:T(8,128)S(1)}, f32[208,128]{1,0:T(8,128)S(1)}, u32[]{:S(2)}, u32[]{:S(2)}) collective-permute-start(f32[208,128]{1,0:T(8,128)S(1)} %add.8.after_ref.own_ref), channel_id=1, source_target_pairs={{0,2},{1,3},{2,0},{3,1},{4,6},{5,7},{6,4},{7,5},{8,10},{9,11},{10,... | collective-permute-start | bytes 319496 | tf_op jit(solution)/shard_map/ppermute | solution.py:734
  28.0 3.3 %collective-permute-start.4 = (f32[208,128]{1,0:T(8,128)S(1)}, f32[208,128]{1,0:T(8,128)S(1)}, u32[]{:S(2)}, u32[]{:S(2)}) collective-permute-start(f32[208,128]{1,0:T(8,128)S(1)} %add.8.after_ref.own_ref), channel_id=1, source_target_pairs={{0,4},{1,5},{2,6},{3,7},{4,0},{5,1},{6,2},{7,3},{8,12},{9,13},{10,... | collective-permute-start | bytes 319496 | tf_op jit(solution)/shard_map/ppermute | solution.py:734
  32.1 1.3 %collective-permute-done.6.right_ref = bf16[384,128]{1,0:T(8,128)(2,1)S(1)} collective-permute-done((bf16[384,128]{1,0:T(8,128)(2,1)S(1)}, bf16[384,128]{1,0:T(8,128)(2,1)S(1)}, u32[]{:S(2)}, u32[]{:S(2)}) %collective-permute-start.6) | collective-permute-done | bytes 98336 | tf_op jit(solution)/shard_map/ppermute | solution.py:716
  33.5 2.4 %collective-permute-done.4.second_ref = f32[208,128]{1,0:T(8,128)S(1)} collective-permute-done((f32[208,128]{1,0:T(8,128)S(1)}, f32[208,128]{1,0:T(8,128)S(1)}, u32[]{:S(2)}, u32[]{:S(2)}) %collective-permute-start.4) | collective-permute-done | bytes 106528 | tf_op jit(solution)/shard_map/ppermute | solution.py:734
  35.8 1.0 %collective-permute-done.5.both_ref = f32[208,128]{1,0:T(8,128)S(1)} collective-permute-done((f32[208,128]{1,0:T(8,128)S(1)}, f32[208,128]{1,0:T(8,128)S(1)}, u32[]{:S(2)}, u32[]{:S(2)}) %collective-permute-start.5) | collective-permute-done | bytes 106528 | tf_op jit(solution)/shard_map/ppermute | solution.py:734
  37.0 1.5 %collective-permute-start.10 = (bf16[384,128]{1,0:T(8,128)(2,1)S(1)}, bf16[384,128]{1,0:T(8,128)(2,1)S(1)}, u32[]{:S(2)}, u32[]{:S(2)}) collective-permute-start(bf16[384,128]{1,0:T(8,128)(2,1)S(1)} %shard_map.72.after_ref.own_ref), channel_id=1, source_target_pairs={{0,4},{1,5},{2,6},{3,7},{4,0},{5,1},{6,2},{7,3},{8,12},{9,13},{10,... | collective-permute-start | bytes 294920 | tf_op jit(solution)/shard_map/ppermute | solution.py:734
  38.5 1.2 %collective-permute-start.11 = (bf16[384,128]{1,0:T(8,128)(2,1)S(1)}, bf16[384,128]{1,0:T(8,128)(2,1)S(1)}, u32[]{:S(2)}, u32[]{:S(2)}) collective-permute-start(bf16[384,128]{1,0:T(8,128)(2,1)S(1)} %shard_map.72.after_ref.own_ref), channel_id=1, source_target_pairs={{0,6},{1,7},{2,4},{3,5},{4,2},{5,3},{6,0},{7,1},{8,14},{9,15},{10,... | collective-permute-start | bytes 294920 | tf_op jit(solution)/shard_map/ppermute | solution.py:734
  40.5 6.4 %shard_map.74.after_ref.before_ref = f32[304,384]{1,0:T(8,128)S(1)} custom-call(s32[1]{0:T(128)} %bitcast.core_ref, f32[208,128]{1,0:T(8,128)S(1)} %shard_map.73.mine_ref, f32[208,128]{1,0:T(8,128)S(1)} %collective-permute-done.7.other_ref), custom_call_target="tpu_custom_call" | custom-call | flops 5500000256 | bytes 1000000 | tf_op jit(solution)/shard_map/pallas_call | solution.py:551
  47.9 1.9 %shard_map.77 = (f32[304,384]{1,0:T(8,128)S(1)}, f32[416,128]{1,0:T(8,128)S(1)}) custom-call(f32[304,384]{1,0:T(8,128)S(1)} %shard_map.74.after_ref.before_ref, f32[384,128]{1,0:T(8,128)S(1)} %get-tuple-element.21.after_ref), custom_call_target="tpu_custom_call" | custom-call | flops 4000000000 | bytes 100000 | tf_op jit(solution)/shard_map/pallas_call | solution.py:567
  49.9 1.3 %collective-permute-start.14 = (f32[384,128]{1,0:T(8,128)S(1)}, f32[384,128]{1,0:T(8,128)S(1)}, u32[]{:S(2)}, u32[]{:S(2)}) collective-permute-start(f32[384,128]{1,0:T(8,128)S(1)} %shard_map.80.left_ref), channel_id=1, source_target_pairs={{0,2},{1,5},{2,0},{3,7},{4,6},{5,1},{6,4},{7,3},{8,10},{9,13},{10,... | collective-permute-start | bytes 589832 | tf_op jit(solution)/shard_map/ppermute | solution.py:768
  51.2 3.4 %collective-permute-start.16 = (f32[416,128]{1,0:T(8,128)S(1)}, f32[416,128]{1,0:T(8,128)S(1)}, u32[]{:S(2)}, u32[]{:S(2)}) collective-permute-start(f32[416,128]{1,0:T(8,128)S(1)} %get-tuple-element.28), channel_id=1, source_target_pairs={{0,8},{8,16},{16,24},{1,9},{9,17},{17,25},{2,10},{10,18},{18,26},{... | collective-permute-start | bytes 638984 | tf_op jit(solution)/shard_map/ppermute | solution.py:712
  54.6 1.0 %collective-permute-done.14.right_ref = f32[384,128]{1,0:T(8,128)S(1)} collective-permute-done((f32[384,128]{1,0:T(8,128)S(1)}, f32[384,128]{1,0:T(8,128)S(1)}, u32[]{:S(2)}, u32[]{:S(2)}) %collective-permute-start.14) | collective-permute-done | bytes 196640 | tf_op jit(solution)/shard_map/ppermute | solution.py:768
  55.7 1.6 %collective-permute-start.15 = (f32[384,128]{1,0:T(8,128)S(1)}, f32[384,128]{1,0:T(8,128)S(1)}, u32[]{:S(2)}, u32[]{:S(2)}) collective-permute-start(f32[384,128]{1,0:T(8,128)S(1)} %shard_map.81.left_ref), channel_id=1, source_target_pairs={{0,4},{1,3},{2,6},{3,1},{4,0},{5,7},{6,2},{7,5},{8,12},{9,11},{10,... | collective-permute-start | bytes 589832 | tf_op jit(solution)/shard_map/ppermute | solution.py:769
  57.2 1.3 %collective-permute-done.12.other_ref = bf16[384,128]{1,0:T(8,128)(2,1)S(1)} collective-permute-done((bf16[384,128]{1,0:T(8,128)(2,1)S(1)}, bf16[384,128]{1,0:T(8,128)(2,1)S(1)}, u32[]{:S(2)}, u32[]{:S(2)}) %collective-permute-start.12) | collective-permute-done | bytes 98336 | tf_op jit(solution)/shard_map/ppermute | solution.py:716
  59.5 1.5 %shard_map.78 = (bf16[300,1280]{1,0:T(8,128)(2,1)}, f32[8,128]{1,0:T(8,128)S(1)}) custom-call(f32[304,384]{1,0:T(8,128)S(1)} %get-tuple-element.22.inverse_ref.refs_0_, bf16[300,1280]{1,0:T(8,128)(2,1)S(1)} %get-tuple-element.18.right_ref.y_ref), custom_call_target="tpu_custom_call" | custom-call | flops 100000 | bytes 100000 | tf_op jit(solution)/shard_map/pallas_call | solution.py:624
  61.4 1.3 %shard_map.83.left_ref = bf16[304,384]{1,0:T(8,128)(2,1)S(1)} custom-call(s32[1]{0:T(128)} %bitcast.core_ref, f32[384,128]{1,0:T(8,128)S(1)} %shard_map.82.mine_ref, f32[304,384]{1,0:T(8,128)S(1)} %get-tuple-element.22.inverse_ref.refs_0_, f32[416,128]{1,0:T(8,128)S(1)} %collective-permute-done.16.previous_ref), custom_call_target="tpu_custom_call" | custom-call | flops 100000 | bytes 100000 | tf_op jit(solution)/shard_map/pallas_call | solution.py:677
  62.8 1.5 %collective-permute-done.17.right_ref = bf16[304,384]{1,0:T(8,128)(2,1)S(1)} collective-permute-done((bf16[304,384]{1,0:T(8,128)(2,1)S(1)}, bf16[304,384]{1,0:T(8,128)(2,1)S(1)}, u32[]{:S(2)}, u32[]{:S(2)}) %collective-permute-start.17) | collective-permute-done | bytes 233504 | tf_op jit(solution)/shard_map/ppermute | solution.py:716
  (37 shorter events, 6.5 us)
Async XLA Ops:
  0.6 8.4 %copy-start = (bf16[1,1280,300]{1,2,0:T(8,128)(2,1)S(1)}, bf16[1,1280,300]{1,2,0:T(8,128)(2,1)}, u32[]{:S(2)}) copy-start(bf16[1,1280,300]{1,2,0:T(8,128)(2,1)} %param.4) | copy-start | bytes 2304004
  0.6 11.7 %collective-permute-start = (bf16[300,1280]{1,0:T(8,128)(2,1)}, bf16[300,1280]{1,0:T(8,128)(2,1)S(1)}, u32[]{:S(2)}, u32[]{:S(2)}) collective-permute-start(bf16[300,1280]{1,0:T(8,128)(2,1)} %bitcast.14), channel_id=1, source_target_pairs={{1,0},{2,1},{3,2},{4,3},{5,4},{6,5},{7,6},{9,8},{10,9},{11,10},{12... | collective-permute-start | bytes 2304008 | tf_op jit(solution)/shard_map/ppermute | solution.py:712
  2.1 0.7 %copy-start.1 = (s32[1,2,10,10]{3,1,2,0:T(2,128)S(1)}, s32[1,2,10,10]{3,1,2,0:T(2,128)}, u32[]{:S(2)}) copy-start(s32[1,2,10,10]{3,1,2,0:T(2,128)} %param.7) | copy-start | bytes 2404
  2.8 6.3 %copy-start.2 = (s32[1,2,10,10]{3,1,2,0:T(2,128)S(1)}, s32[1,2,10,10]{3,1,2,0:T(2,128)}, u32[]{:S(2)}) copy-start(s32[1,2,10,10]{3,1,2,0:T(2,128)} %param.7) | copy-start | bytes 2404
  5.9 9.6 %collective-permute-start.1 = (bf16[300,1280]{1,0:T(8,128)(2,1)S(1)}, bf16[300,1280]{1,0:T(8,128)(2,1)S(1)}, u32[]{:S(2)}, u32[]{:S(2)}) collective-permute-start(bf16[300,1280]{1,0:T(8,128)(2,1)S(1)} %shard_map.69), channel_id=1, source_target_pairs={{0,1},{1,2},{2,3},{3,4},{4,5},{5,6},{6,7},{8,9},{9,10},{10,11},{11... | collective-permute-start | bytes 2304008 | tf_op jit(solution)/shard_map/ppermute | solution.py:712
  16.1 8.4 %collective-permute-start.2 = (f32[208,128]{1,0:T(8,128)S(1)}, f32[208,128]{1,0:T(8,128)S(1)}, u32[]{:S(2)}, u32[]{:S(2)}) collective-permute-start(f32[208,128]{1,0:T(8,128)S(1)} %get-tuple-element.17), channel_id=1, source_target_pairs={{0,1},{1,0},{2,3},{3,2},{4,5},{5,4},{6,7},{7,6},{8,9},{9,8},{10,11... | collective-permute-start | bytes 319496 | tf_op jit(solution)/shard_map/ppermute | solution.py:716
  21.0 26.0 %collective-permute-start.8 = (bf16[300,1280]{1,0:T(8,128)(2,1)S(1)}, bf16[300,1280]{1,0:T(8,128)(2,1)S(1)}, u32[]{:S(2)}, u32[]{:S(2)}) collective-permute-start(bf16[300,1280]{1,0:T(8,128)(2,1)S(1)} %get-tuple-element.18.right_ref.y_ref), channel_id=1, source_target_pairs={{0,8},{8,16},{16,24},{1,9},{9,17},{17,25},{2,10},{10,18},{18,26},{... | collective-permute-start | bytes 2304008 | tf_op jit(solution)/shard_map/ppermute | solution.py:712
  24.5 8.9 %collective-permute-start.3 = (f32[208,128]{1,0:T(8,128)S(1)}, f32[208,128]{1,0:T(8,128)S(1)}, u32[]{:S(2)}, u32[]{:S(2)}) collective-permute-start(f32[208,128]{1,0:T(8,128)S(1)} %add.8.after_ref.own_ref), channel_id=1, source_target_pairs={{0,2},{1,3},{2,0},{3,1},{4,6},{5,7},{6,4},{7,5},{8,10},{9,11},{10,... | collective-permute-start | bytes 319496 | tf_op jit(solution)/shard_map/ppermute | solution.py:734
  28.0 7.9 %collective-permute-start.4 = (f32[208,128]{1,0:T(8,128)S(1)}, f32[208,128]{1,0:T(8,128)S(1)}, u32[]{:S(2)}, u32[]{:S(2)}) collective-permute-start(f32[208,128]{1,0:T(8,128)S(1)} %add.8.after_ref.own_ref), channel_id=1, source_target_pairs={{0,4},{1,5},{2,6},{3,7},{4,0},{5,1},{6,2},{7,3},{8,12},{9,13},{10,... | collective-permute-start | bytes 319496 | tf_op jit(solution)/shard_map/ppermute | solution.py:734
  31.2 5.6 %collective-permute-start.5 = (f32[208,128]{1,0:T(8,128)S(1)}, f32[208,128]{1,0:T(8,128)S(1)}, u32[]{:S(2)}, u32[]{:S(2)}) collective-permute-start(f32[208,128]{1,0:T(8,128)S(1)} %add.8.after_ref.own_ref), channel_id=1, source_target_pairs={{0,6},{1,7},{2,4},{3,5},{4,2},{5,3},{6,0},{7,1},{8,14},{9,15},{10,... | collective-permute-start | bytes 319496 | tf_op jit(solution)/shard_map/ppermute | solution.py:734
  32.1 1.4 %collective-permute-start.6 = (bf16[384,128]{1,0:T(8,128)(2,1)S(1)}, bf16[384,128]{1,0:T(8,128)(2,1)S(1)}, u32[]{:S(2)}, u32[]{:S(2)}) collective-permute-start(bf16[384,128]{1,0:T(8,128)(2,1)S(1)} %get-tuple-element.20), channel_id=1, source_target_pairs={{0,1},{1,0},{2,3},{3,2},{4,5},{5,4},{6,7},{7,6},{8,9},{9,8},{10,11... | collective-permute-start | bytes 294920 | tf_op jit(solution)/shard_map/ppermute | solution.py:716
  36.9 3.6 %collective-permute-start.7 = (f32[208,128]{1,0:T(8,128)S(1)}, f32[208,128]{1,0:T(8,128)S(1)}, u32[]{:S(2)}, u32[]{:S(2)}) collective-permute-start(f32[208,128]{1,0:T(8,128)S(1)} %shard_map.73.mine_ref), channel_id=1, source_target_pairs={{0,1},{1,0},{2,3},{3,2},{4,5},{5,4},{6,7},{7,6},{8,9},{9,8},{10,11... | collective-permute-start | bytes 319496 | tf_op jit(solution)/shard_map/ppermute | solution.py:716
  37.0 10.0 %collective-permute-start.10 = (bf16[384,128]{1,0:T(8,128)(2,1)S(1)}, bf16[384,128]{1,0:T(8,128)(2,1)S(1)}, u32[]{:S(2)}, u32[]{:S(2)}) collective-permute-start(bf16[384,128]{1,0:T(8,128)(2,1)S(1)} %shard_map.72.after_ref.own_ref), channel_id=1, source_target_pairs={{0,4},{1,5},{2,6},{3,7},{4,0},{5,1},{6,2},{7,3},{8,12},{9,13},{10,... | collective-permute-start | bytes 294920 | tf_op jit(solution)/shard_map/ppermute | solution.py:734
  38.5 8.4 %collective-permute-start.11 = (bf16[384,128]{1,0:T(8,128)(2,1)S(1)}, bf16[384,128]{1,0:T(8,128)(2,1)S(1)}, u32[]{:S(2)}, u32[]{:S(2)}) collective-permute-start(bf16[384,128]{1,0:T(8,128)(2,1)S(1)} %shard_map.72.after_ref.own_ref), channel_id=1, source_target_pairs={{0,6},{1,7},{2,4},{3,5},{4,2},{5,3},{6,0},{7,1},{8,14},{9,15},{10,... | collective-permute-start | bytes 294920 | tf_op jit(solution)/shard_map/ppermute | solution.py:734
  39.7 7.3 %collective-permute-start.9 = (bf16[384,128]{1,0:T(8,128)(2,1)S(1)}, bf16[384,128]{1,0:T(8,128)(2,1)S(1)}, u32[]{:S(2)}, u32[]{:S(2)}) collective-permute-start(bf16[384,128]{1,0:T(8,128)(2,1)S(1)} %shard_map.72.after_ref.own_ref), channel_id=1, source_target_pairs={{0,2},{1,3},{2,0},{3,1},{4,6},{5,7},{6,4},{7,5},{8,10},{9,11},{10,... | collective-permute-start | bytes 294920 | tf_op jit(solution)/shard_map/ppermute | solution.py:734
  47.8 2.0 %collective-permute-start.13 = (f32[384,128]{1,0:T(8,128)S(1)}, f32[384,128]{1,0:T(8,128)S(1)}, u32[]{:S(2)}, u32[]{:S(2)}) collective-permute-start(f32[384,128]{1,0:T(8,128)S(1)} %get-tuple-element.21.after_ref), channel_id=1, source_target_pairs={{0,1},{1,0},{2,3},{3,2},{4,5},{5,4},{6,7},{7,6},{8,9},{9,8},{10,11... | collective-permute-start | bytes 589832 | tf_op jit(solution)/shard_map/ppermute | solution.py:716
  49.9 5.7 %collective-permute-start.14 = (f32[384,128]{1,0:T(8,128)S(1)}, f32[384,128]{1,0:T(8,128)S(1)}, u32[]{:S(2)}, u32[]{:S(2)}) collective-permute-start(f32[384,128]{1,0:T(8,128)S(1)} %shard_map.80.left_ref), channel_id=1, source_target_pairs={{0,2},{1,5},{2,0},{3,7},{4,6},{5,1},{6,4},{7,3},{8,10},{9,13},{10,... | collective-permute-start | bytes 589832 | tf_op jit(solution)/shard_map/ppermute | solution.py:768
  51.2 10.3 %collective-permute-start.16 = (f32[416,128]{1,0:T(8,128)S(1)}, f32[416,128]{1,0:T(8,128)S(1)}, u32[]{:S(2)}, u32[]{:S(2)}) collective-permute-start(f32[416,128]{1,0:T(8,128)S(1)} %get-tuple-element.28), channel_id=1, source_target_pairs={{0,8},{8,16},{16,24},{1,9},{9,17},{17,25},{2,10},{10,18},{18,26},{... | collective-permute-start | bytes 638984 | tf_op jit(solution)/shard_map/ppermute | solution.py:712
  55.7 5.7 %collective-permute-start.15 = (f32[384,128]{1,0:T(8,128)S(1)}, f32[384,128]{1,0:T(8,128)S(1)}, u32[]{:S(2)}, u32[]{:S(2)}) collective-permute-start(f32[384,128]{1,0:T(8,128)S(1)} %shard_map.81.left_ref), channel_id=1, source_target_pairs={{0,4},{1,3},{2,6},{3,1},{4,0},{5,7},{6,2},{7,5},{8,12},{9,11},{10,... | collective-permute-start | bytes 589832 | tf_op jit(solution)/shard_map/ppermute | solution.py:769
  57.2 1.3 %collective-permute-start.12 = (bf16[384,128]{1,0:T(8,128)(2,1)S(1)}, bf16[384,128]{1,0:T(8,128)(2,1)S(1)}, u32[]{:S(2)}, u32[]{:S(2)}) collective-permute-start(bf16[384,128]{1,0:T(8,128)(2,1)S(1)} %shard_map.75.after_ref.mine_ref), channel_id=1, source_target_pairs={{0,1},{1,0},{2,3},{3,2},{4,5},{5,4},{6,7},{7,6},{8,9},{9,8},{10,11... | collective-permute-start | bytes 294920 | tf_op jit(solution)/shard_map/ppermute | solution.py:716
  62.7 1.6 %collective-permute-start.17 = (bf16[304,384]{1,0:T(8,128)(2,1)S(1)}, bf16[304,384]{1,0:T(8,128)(2,1)S(1)}, u32[]{:S(2)}, u32[]{:S(2)}) collective-permute-start(bf16[304,384]{1,0:T(8,128)(2,1)S(1)} %shard_map.83.left_ref), channel_id=1, source_target_pairs={{0,1},{1,0},{2,3},{3,2},{4,5},{5,4},{6,7},{7,6},{8,9},{9,8},{10,11... | collective-permute-start | bytes 700424 | tf_op jit(solution)/shard_map/ppermute | solution.py:716

commit v2 on v1

--- a/solution.py
+++ b/solution.py
@@ -15,8 +15,8 @@
 SCALARS = pl.BlockSpec(memory_space=pltpu.SMEM)
 ANYWHERE = pl.BlockSpec(memory_space=pl.ANY)
 MIB = 1024 * 1024
-FIRST_STAGE_FLOPS = 5500 * 10**6
-LAST_STAGES_FLOPS = 4 * 10**9
+FIRST_STAGE_FLOPS = 5000 * 10**6
+LAST_STAGES_FLOPS = 4000 * 10**6
 
 
 def params(mib=48):
@@ -756,16 +756,19 @@
     r_mine, r_other = cross(core, x_t, y_t, g_sum, jnp.bfloat16)
     r_sum = add_after(r_mine, other_core(r_other))
     g_sum = sum_chips(g_sum, r_sum)
+    r_first = lax.ppermute(r_sum, "rows", rounds[0])
     work = first_stage(core, g_sum, other_core(g_sum), channels, total_rows)
-    r_sum = sum_chips(r_sum, work)
-    m_mine, m_other = cross(core, previous_y, y_t, r_sum, jnp.float32)
+    r_sum = add_after(r_sum, r_first, work)
+    m_mine, m_other = cross(core, previous_y, y_t, work, jnp.float32)
     inverse, pack = last_stages(work, channels, m_other)
     m_sum = add_after(m_mine, other_core(m_other), inverse)
     previous = from_behind(pack, "sector", 1)
+    for pairs in rounds[1:]:
+        r_sum = add_after(r_sum, lax.ppermute(r_sum, "rows", pairs))
     rayleigh, token = unpack_ray(core, r_sum, other_core(r_sum), channels, total_rows)
     q_t, basis_token = basis(inverse, y_t)
     for pairs in rounds[:-1]:
-        m_sum = add_after(m_sum, lax.ppermute(m_sum, "rows", pairs))
+        m_sum = add_after(m_sum, lax.ppermute(m_sum, "rows", pairs), r_sum)
     m_sum = add_after(m_sum, lax.ppermute(m_sum, "rows", rounds[-1]), token, basis_token)
     part = correlation_part(core, m_sum, inverse, previous, channels, total_rows)
     correlation = both_parts(part, other_core(part), channels)

time: 65.5 us -> 65.7 us (level)
    ppermute x6 -> x3, starting transfers between devices: 10.3 us -> 6.72 us  [sum_chips(): lax.ppermute(value, 'rows', [(s, s ^ bits) for s in range(count)])]
    ppermute x1 -> x3, starting transfers between devices: 1.26 us -> 4.69 us  [the longest x1 2.42 us: shards(): r_sum = add_after(r_sum, lax.ppermute(r_sum, 'rows', pairs))]
    ppermute x1, waiting for transfers between devices: 0.37 us -> 1.5 us  [shards(): lax.ppermute(m_sum, 'rows', rounds[-1])]
    ppermute x1, starting transfers between devices: 1.55 us -> 0.43 us  [shards(): lax.ppermute(m_sum, 'rows', rounds[-1])]
    ppermute x1 -> x3, waiting for transfers between devices: 1.03 us -> 0.01 us  [the longest x1 0.01 us: shards(): r_first = lax.ppermute(r_sum, 'rows', rounds[0])]
    ppermute x4, starting transfers between devices: 11.5 us -> 12.4 us  [from_behind(): lax.ppermute(value, axis, [(source, source + steps) for source in range(l...]
    ppermute x6 -> x3, waiting for transfers between devices: 3.38 us -> 3.38 us  [sum_chips(): lax.ppermute(value, 'rows', [(s, s ^ bits) for s in range(count)])]
  transfers between devices with their start and end apart: 18 -> 17, of which waited for: 7 -> 6; matrix products, arithmetic and copies ran while one was open for 0% -> 0% of each run, Pallas kernels for 33% -> 34%
where the time goes in v2:
time: 65.7 us; the launch traced here: 65.4 us
  starting transfers between devices  29.8 us (45%)
  Pallas kernels  24.9 us (38%)
  waiting for transfers between devices  9.01 us (14%)
  between operations  0.92 us (1%)
  local copies, waits for them, and re-layouts  0.7 us (1%)
    ppermute x4, starting transfers between devices, from_behind(): lax.ppermute(value, axis, [(source, source + steps) for source in range(l...  12.4 us
    ppermute x3, starting transfers between devices, sum_chips(): lax.ppermute(value, 'rows', [(s, s ^ bits) for s in range(count)])  6.72 us
    pallas_call x2, Pallas kernels, tile_product(): pl.pallas_call(functools.partial(tile_kernel, which), in_specs=[WHOLE, AN...  6.41 us
    pallas_call x1, Pallas kernels, first_stage(): pl.pallas_call(functools.partial(first_stage_kernel, channels, 1.0 / tota...  6.39 us
    ppermute x6, starting transfers between devices, other_core(): lax.ppermute(value, 'rows', [(s, s ^ 1) for s in range(lax.axis_size('row...  5.59 us
    ppermute x6, waiting for transfers between devices, other_core(): lax.ppermute(value, 'rows', [(s, s ^ 1) for s in range(lax.axis_size('row...  4.11 us
    ppermute x3, waiting for transfers between devices, sum_chips(): lax.ppermute(value, 'rows', [(s, s ^ bits) for s in range(count)])  3.38 us
    pallas_call x1, Pallas kernels, later_product(): pl.pallas_call(later_kernel, in_specs=[WHOLE, WHOLE, ANYWHERE, WHOLE], ou...  3.15 us
  transfers between devices with their start and end apart: 17, of which 6 were waited for; matrix products, arithmetic and copies ran while one was open for 0% of the time, Pallas kernels for 34%

profile of v2, /device:TPU:0, one launch (start us, length us, event | category | flops | bytes accessed | tf_op | source)
XLA Modules:
  0.0 65.4 jit_solution(10683255651013737384)
XLA Ops:
  0.6 1.4 %collective-permute-start = (bf16[300,1280]{1,0:T(8,128)(2,1)}, bf16[300,1280]{1,0:T(8,128)(2,1)S(1)}, u32[]{:S(2)}, u32[]{:S(2)}) collective-permute-start(bf16[300,1280]{1,0:T(8,128)(2,1)} %bitcast.14), channel_id=1, source_target_pairs={{1,0},{2,1},{3,2},{4,3},{5,4},{6,5},{7,6},{9,8},{10,9},{11,10},{12... | collective-permute-start | bytes 2304008 | tf_op jit(solution)/shard_map/ppermute | solution.py:712
  2.8 3.1 %shard_map.69 = bf16[300,1280]{1,0:T(8,128)(2,1)S(1)} custom-call(s32[10,2,10]{2,1,0:T(2,128)S(1)} %bitcast.18, bf16[300,1280]{1,0:T(8,128)(2,1)} %bitcast.15, bf16[1280,1280]{1,0:T(8,128)(2,1)} %bitcast.21), custom_call_target="tpu_custom_call" | custom-call | flops 983040000 | bytes 3276800 | tf_op jit(solution)/shard_map/pallas_call | solution.py:107
  5.9 3.1 %collective-permute-start.1 = (bf16[300,1280]{1,0:T(8,128)(2,1)S(1)}, bf16[300,1280]{1,0:T(8,128)(2,1)S(1)}, u32[]{:S(2)}, u32[]{:S(2)}) collective-permute-start(bf16[300,1280]{1,0:T(8,128)(2,1)S(1)} %shard_map.69), channel_id=1, source_target_pairs={{0,1},{1,2},{2,3},{3,4},{4,5},{5,6},{6,7},{8,9},{9,10},{10,11},{11... | collective-permute-start | bytes 2304008 | tf_op jit(solution)/shard_map/ppermute | solution.py:712
  9.0 3.3 %shard_map.67.first_ref = f32[300,1280]{1,0:T(8,128)S(1)} custom-call(s32[10,2,10]{2,1,0:T(2,128)S(1)} %bitcast.19, bf16[300,1280]{1,0:T(8,128)(2,1)S(1)} %bitcast.16, bf16[1280,1280]{1,0:T(8,128)(2,1)} %bitcast.23), custom_call_target="tpu_custom_call" | custom-call | flops 983040000 | bytes 3276800 | tf_op jit(solution)/shard_map/pallas_call | solution.py:107
  12.3 3.1 %shard_map.68.part_ref = f32[300,1280]{1,0:T(8,128)S(1)} custom-call(s32[10,2,10]{2,1,0:T(2,128)S(1)} %bitcast.20, bf16[300,1280]{1,0:T(8,128)(2,1)S(1)} %collective-permute-done.later_ref, bf16[1280,1280]{1,0:T(8,128)(2,1)} %bitcast.22, f32[300,1280]{1,0:T(8,128)S(1)} %shard_map.67.first_ref), custom_call_target="tpu_custom_call" | custom-call | flops 983040000 | bytes 3276800 | tf_op jit(solution)/shard_map/pallas_call | solution.py:142
  16.1 4.9 %collective-permute-start.2 = (f32[208,128]{1,0:T(8,128)S(1)}, f32[208,128]{1,0:T(8,128)S(1)}, u32[]{:S(2)}, u32[]{:S(2)}) collective-permute-start(f32[208,128]{1,0:T(8,128)S(1)} %get-tuple-element.17), channel_id=1, source_target_pairs={{0,1},{1,0},{2,3},{3,2},{4,5},{5,4},{6,7},{7,6},{8,9},{9,8},{10,11... | collective-permute-start | bytes 319496 | tf_op jit(solution)/shard_map/ppermute | solution.py:716
  21.0 3.5 %collective-permute-start.8 = (bf16[300,1280]{1,0:T(8,128)(2,1)S(1)}, bf16[300,1280]{1,0:T(8,128)(2,1)S(1)}, u32[]{:S(2)}, u32[]{:S(2)}) collective-permute-start(bf16[300,1280]{1,0:T(8,128)(2,1)S(1)} %get-tuple-element.18.right_ref.y_ref), channel_id=1, source_target_pairs={{0,8},{8,16},{16,24},{1,9},{9,17},{17,25},{2,10},{10,18},{18,26},{... | collective-permute-start | bytes 2304008 | tf_op jit(solution)/shard_map/ppermute | solution.py:712
  24.5 3.4 %collective-permute-start.3 = (f32[208,128]{1,0:T(8,128)S(1)}, f32[208,128]{1,0:T(8,128)S(1)}, u32[]{:S(2)}, u32[]{:S(2)}) collective-permute-start(f32[208,128]{1,0:T(8,128)S(1)} %add.8.after_ref.own_ref), channel_id=1, source_target_pairs={{0,2},{1,3},{2,0},{3,1},{4,6},{5,7},{6,4},{7,5},{8,10},{9,11},{10,... | collective-permute-start | bytes 319496 | tf_op jit(solution)/shard_map/ppermute | solution.py:734
  28.0 3.3 %collective-permute-start.4 = (f32[208,128]{1,0:T(8,128)S(1)}, f32[208,128]{1,0:T(8,128)S(1)}, u32[]{:S(2)}, u32[]{:S(2)}) collective-permute-start(f32[208,128]{1,0:T(8,128)S(1)} %add.8.after_ref.own_ref), channel_id=1, source_target_pairs={{0,4},{1,5},{2,6},{3,7},{4,0},{5,1},{6,2},{7,3},{8,12},{9,13},{10,... | collective-permute-start | bytes 319496 | tf_op jit(solution)/shard_map/ppermute | solution.py:734
  32.1 1.3 %collective-permute-done.6.right_ref = bf16[384,128]{1,0:T(8,128)(2,1)S(1)} collective-permute-done((bf16[384,128]{1,0:T(8,128)(2,1)S(1)}, bf16[384,128]{1,0:T(8,128)(2,1)S(1)}, u32[]{:S(2)}, u32[]{:S(2)}) %collective-permute-start.6) | collective-permute-done | bytes 98336 | tf_op jit(solution)/shard_map/ppermute | solution.py:716
  33.5 2.4 %collective-permute-done.4.second_ref = f32[208,128]{1,0:T(8,128)S(1)} collective-permute-done((f32[208,128]{1,0:T(8,128)S(1)}, f32[208,128]{1,0:T(8,128)S(1)}, u32[]{:S(2)}, u32[]{:S(2)}) %collective-permute-start.4) | collective-permute-done | bytes 106528 | tf_op jit(solution)/shard_map/ppermute | solution.py:734
  35.8 1.0 %collective-permute-done.5.both_ref = f32[208,128]{1,0:T(8,128)S(1)} collective-permute-done((f32[208,128]{1,0:T(8,128)S(1)}, f32[208,128]{1,0:T(8,128)S(1)}, u32[]{:S(2)}, u32[]{:S(2)}) %collective-permute-start.5) | collective-permute-done | bytes 106528 | tf_op jit(solution)/shard_map/ppermute | solution.py:734
  37.0 1.3 %collective-permute-start.9 = (bf16[384,128]{1,0:T(8,128)(2,1)S(1)}, bf16[384,128]{1,0:T(8,128)(2,1)S(1)}, u32[]{:S(2)}, u32[]{:S(2)}) collective-permute-start(bf16[384,128]{1,0:T(8,128)(2,1)S(1)} %shard_map.72.after_ref.left_ref), channel_id=1, source_target_pairs={{0,2},{1,5},{2,0},{3,7},{4,6},{5,1},{6,4},{7,3},{8,10},{9,13},{10,... | collective-permute-start | bytes 294920 | tf_op jit(solution)/shard_map/ppermute | solution.py:759
  38.3 6.4 %shard_map.74.after_ref.before_ref.refs_0_ = f32[304,384]{1,0:T(8,128)S(1)} custom-call(s32[1]{0:T(128)} %bitcast.core_ref, f32[208,128]{1,0:T(8,128)S(1)} %shard_map.73.mine_ref, f32[208,128]{1,0:T(8,128)S(1)} %collective-permute-done.7.other_ref), custom_call_target="tpu_custom_call" | custom-call | flops 5000000000 | bytes 1000000 | tf_op jit(solution)/shard_map/pallas_call | solution.py:551
  45.9 1.9 %shard_map.76 = (f32[304,384]{1,0:T(8,128)S(1)}, f32[416,128]{1,0:T(8,128)S(1)}) custom-call(f32[304,384]{1,0:T(8,128)S(1)} %shard_map.74.after_ref.before_ref.refs_0_, f32[384,128]{1,0:T(8,128)S(1)} %get-tuple-element.21.after_ref), custom_call_target="tpu_custom_call" | custom-call | flops 4000000000 | bytes 100000 | tf_op jit(solution)/shard_map/pallas_call | solution.py:567
  47.9 1.0 %collective-permute-start.13 = (f32[384,128]{1,0:T(8,128)S(1)}, f32[384,128]{1,0:T(8,128)S(1)}, u32[]{:S(2)}, u32[]{:S(2)}) collective-permute-start(f32[384,128]{1,0:T(8,128)S(1)} %shard_map.81.left_ref), channel_id=1, source_target_pairs={{0,2},{1,5},{2,0},{3,7},{4,6},{5,1},{6,4},{7,3},{8,10},{9,13},{10,... | collective-permute-start | bytes 589832 | tf_op jit(solution)/shard_map/ppermute | solution.py:771
  49.0 2.4 %collective-permute-start.10 = (bf16[384,128]{1,0:T(8,128)(2,1)S(1)}, bf16[384,128]{1,0:T(8,128)(2,1)S(1)}, u32[]{:S(2)}, u32[]{:S(2)}) collective-permute-start(bf16[384,128]{1,0:T(8,128)(2,1)S(1)} %shard_map.78.left_ref), channel_id=1, source_target_pairs={{0,4},{1,3},{2,6},{3,1},{4,0},{5,7},{6,2},{7,5},{8,12},{9,11},{10,... | collective-permute-start | bytes 294920 | tf_op jit(solution)/shard_map/ppermute | solution.py:767
  51.4 4.4 %collective-permute-start.15 = (f32[416,128]{1,0:T(8,128)S(1)}, f32[416,128]{1,0:T(8,128)S(1)}, u32[]{:S(2)}, u32[]{:S(2)}) collective-permute-start(f32[416,128]{1,0:T(8,128)S(1)} %get-tuple-element.28), channel_id=1, source_target_pairs={{0,8},{8,16},{16,24},{1,9},{9,17},{17,25},{2,10},{10,18},{18,26},{... | collective-permute-start | bytes 638984 | tf_op jit(solution)/shard_map/ppermute | solution.py:712
  56.3 1.3 %collective-permute-done.11.other_ref = bf16[384,128]{1,0:T(8,128)(2,1)S(1)} collective-permute-done((bf16[384,128]{1,0:T(8,128)(2,1)S(1)}, bf16[384,128]{1,0:T(8,128)(2,1)S(1)}, u32[]{:S(2)}, u32[]{:S(2)}) %collective-permute-start.11) | collective-permute-done | bytes 98336 | tf_op jit(solution)/shard_map/ppermute | solution.py:716
  57.6 1.0 %shard_map.80 = (f32[300,1,300]{2,1,0:T(1,128)}, f32[8,128]{1,0:T(8,128)S(1)}) custom-call(s32[1]{0:T(128)} %bitcast.core_ref, bf16[384,128]{1,0:T(8,128)(2,1)S(1)} %shard_map.79.mine_ref.refs_0_, bf16[384,128]{1,0:T(8,128)(2,1)S(1)} %collective-permute-done.11.other_ref), custom_call_target="tpu_custom_call" | custom-call | flops 100000 | bytes 100000 | tf_op jit(solution)/shard_map/pallas_call | solution.py:649
  58.6 1.5 %shard_map.77 = (bf16[300,1280]{1,0:T(8,128)(2,1)}, f32[8,128]{1,0:T(8,128)S(1)}) custom-call(f32[304,384]{1,0:T(8,128)S(1)} %get-tuple-element.22.inverse_ref.refs_0_, bf16[300,1280]{1,0:T(8,128)(2,1)S(1)} %get-tuple-element.18.right_ref.y_ref), custom_call_target="tpu_custom_call" | custom-call | flops 100000 | bytes 100000 | tf_op jit(solution)/shard_map/pallas_call | solution.py:624
  60.1 1.5 %collective-permute-done.14.right_ref = f32[384,128]{1,0:T(8,128)S(1)} collective-permute-done((f32[384,128]{1,0:T(8,128)S(1)}, f32[384,128]{1,0:T(8,128)S(1)}, u32[]{:S(2)}, u32[]{:S(2)}) %collective-permute-start.14) | collective-permute-done | bytes 196640 | tf_op jit(solution)/shard_map/ppermute | solution.py:772
  61.6 1.3 %shard_map.84.left_ref = bf16[304,384]{1,0:T(8,128)(2,1)S(1)} custom-call(s32[1]{0:T(128)} %bitcast.core_ref, f32[384,128]{1,0:T(8,128)S(1)} %shard_map.83.mine_ref, f32[304,384]{1,0:T(8,128)S(1)} %get-tuple-element.22.inverse_ref.refs_0_, f32[416,128]{1,0:T(8,128)S(1)} %collective-permute-done.15.previous_ref), custom_call_target="tpu_custom_call" | custom-call | flops 100000 | bytes 100000 | tf_op jit(solution)/shard_map/pallas_call | solution.py:677
  63.0 1.5 %collective-permute-done.16.right_ref = bf16[304,384]{1,0:T(8,128)(2,1)S(1)} collective-permute-done((bf16[304,384]{1,0:T(8,128)(2,1)S(1)}, bf16[304,384]{1,0:T(8,128)(2,1)S(1)}, u32[]{:S(2)}, u32[]{:S(2)}) %collective-permute-start.16) | collective-permute-done | bytes 233504 | tf_op jit(solution)/shard_map/ppermute | solution.py:716
  (36 shorter events, 5.2 us)
Async XLA Ops:
  0.6 8.4 %copy-start = (bf16[1,1280,300]{1,2,0:T(8,128)(2,1)S(1)}, bf16[1,1280,300]{1,2,0:T(8,128)(2,1)}, u32[]{:S(2)}) copy-start(bf16[1,1280,300]{1,2,0:T(8,128)(2,1)} %param.4) | copy-start | bytes 2304004
  0.6 11.7 %collective-permute-start = (bf16[300,1280]{1,0:T(8,128)(2,1)}, bf16[300,1280]{1,0:T(8,128)(2,1)S(1)}, u32[]{:S(2)}, u32[]{:S(2)}) collective-permute-start(bf16[300,1280]{1,0:T(8,128)(2,1)} %bitcast.14), channel_id=1, source_target_pairs={{1,0},{2,1},{3,2},{4,3},{5,4},{6,5},{7,6},{9,8},{10,9},{11,10},{12... | collective-permute-start | bytes 2304008 | tf_op jit(solution)/shard_map/ppermute | solution.py:712
  2.1 0.7 %copy-start.1 = (s32[1,2,10,10]{3,1,2,0:T(2,128)S(1)}, s32[1,2,10,10]{3,1,2,0:T(2,128)}, u32[]{:S(2)}) copy-start(s32[1,2,10,10]{3,1,2,0:T(2,128)} %param.7) | copy-start | bytes 2404
  2.8 6.3 %copy-start.2 = (s32[1,2,10,10]{3,1,2,0:T(2,128)S(1)}, s32[1,2,10,10]{3,1,2,0:T(2,128)}, u32[]{:S(2)}) copy-start(s32[1,2,10,10]{3,1,2,0:T(2,128)} %param.7) | copy-start | bytes 2404
  5.9 9.6 %collective-permute-start.1 = (bf16[300,1280]{1,0:T(8,128)(2,1)S(1)}, bf16[300,1280]{1,0:T(8,128)(2,1)S(1)}, u32[]{:S(2)}, u32[]{:S(2)}) collective-permute-start(bf16[300,1280]{1,0:T(8,128)(2,1)S(1)} %shard_map.69), channel_id=1, source_target_pairs={{0,1},{1,2},{2,3},{3,4},{4,5},{5,6},{6,7},{8,9},{9,10},{10,11},{11... | collective-permute-start | bytes 2304008 | tf_op jit(solution)/shard_map/ppermute | solution.py:712
  16.1 8.4 %collective-permute-start.2 = (f32[208,128]{1,0:T(8,128)S(1)}, f32[208,128]{1,0:T(8,128)S(1)}, u32[]{:S(2)}, u32[]{:S(2)}) collective-permute-start(f32[208,128]{1,0:T(8,128)S(1)} %get-tuple-element.17), channel_id=1, source_target_pairs={{0,1},{1,0},{2,3},{3,2},{4,5},{5,4},{6,7},{7,6},{8,9},{9,8},{10,11... | collective-permute-start | bytes 319496 | tf_op jit(solution)/shard_map/ppermute | solution.py:716
  21.0 23.7 %collective-permute-start.8 = (bf16[300,1280]{1,0:T(8,128)(2,1)S(1)}, bf16[300,1280]{1,0:T(8,128)(2,1)S(1)}, u32[]{:S(2)}, u32[]{:S(2)}) collective-permute-start(bf16[300,1280]{1,0:T(8,128)(2,1)S(1)} %get-tuple-element.18.right_ref.y_ref), channel_id=1, source_target_pairs={{0,8},{8,16},{16,24},{1,9},{9,17},{17,25},{2,10},{10,18},{18,26},{... | collective-permute-start | bytes 2304008 | tf_op jit(solution)/shard_map/ppermute | solution.py:712
  24.5 8.9 %collective-permute-start.3 = (f32[208,128]{1,0:T(8,128)S(1)}, f32[208,128]{1,0:T(8,128)S(1)}, u32[]{:S(2)}, u32[]{:S(2)}) collective-permute-start(f32[208,128]{1,0:T(8,128)S(1)} %add.8.after_ref.own_ref), channel_id=1, source_target_pairs={{0,2},{1,3},{2,0},{3,1},{4,6},{5,7},{6,4},{7,5},{8,10},{9,11},{10,... | collective-permute-start | bytes 319496 | tf_op jit(solution)/shard_map/ppermute | solution.py:734
  28.0 7.9 %collective-permute-start.4 = (f32[208,128]{1,0:T(8,128)S(1)}, f32[208,128]{1,0:T(8,128)S(1)}, u32[]{:S(2)}, u32[]{:S(2)}) collective-permute-start(f32[208,128]{1,0:T(8,128)S(1)} %add.8.after_ref.own_ref), channel_id=1, source_target_pairs={{0,4},{1,5},{2,6},{3,7},{4,0},{5,1},{6,2},{7,3},{8,12},{9,13},{10,... | collective-permute-start | bytes 319496 | tf_op jit(solution)/shard_map/ppermute | solution.py:734
  31.2 5.6 %collective-permute-start.5 = (f32[208,128]{1,0:T(8,128)S(1)}, f32[208,128]{1,0:T(8,128)S(1)}, u32[]{:S(2)}, u32[]{:S(2)}) collective-permute-start(f32[208,128]{1,0:T(8,128)S(1)} %add.8.after_ref.own_ref), channel_id=1, source_target_pairs={{0,6},{1,7},{2,4},{3,5},{4,2},{5,3},{6,0},{7,1},{8,14},{9,15},{10,... | collective-permute-start | bytes 319496 | tf_op jit(solution)/shard_map/ppermute | solution.py:734
  32.1 1.4 %collective-permute-start.6 = (bf16[384,128]{1,0:T(8,128)(2,1)S(1)}, bf16[384,128]{1,0:T(8,128)(2,1)S(1)}, u32[]{:S(2)}, u32[]{:S(2)}) collective-permute-start(bf16[384,128]{1,0:T(8,128)(2,1)S(1)} %get-tuple-element.20), channel_id=1, source_target_pairs={{0,1},{1,0},{2,3},{3,2},{4,5},{5,4},{6,7},{7,6},{8,9},{9,8},{10,11... | collective-permute-start | bytes 294920 | tf_op jit(solution)/shard_map/ppermute | solution.py:716
  36.9 1.4 %collective-permute-start.7 = (f32[208,128]{1,0:T(8,128)S(1)}, f32[208,128]{1,0:T(8,128)S(1)}, u32[]{:S(2)}, u32[]{:S(2)}) collective-permute-start(f32[208,128]{1,0:T(8,128)S(1)} %shard_map.73.mine_ref), channel_id=1, source_target_pairs={{0,1},{1,0},{2,3},{3,2},{4,5},{5,4},{6,7},{7,6},{8,9},{9,8},{10,11... | collective-permute-start | bytes 319496 | tf_op jit(solution)/shard_map/ppermute | solution.py:716
  37.0 12.0 %collective-permute-start.9 = (bf16[384,128]{1,0:T(8,128)(2,1)S(1)}, bf16[384,128]{1,0:T(8,128)(2,1)S(1)}, u32[]{:S(2)}, u32[]{:S(2)}) collective-permute-start(bf16[384,128]{1,0:T(8,128)(2,1)S(1)} %shard_map.72.after_ref.left_ref), channel_id=1, source_target_pairs={{0,2},{1,5},{2,0},{3,7},{4,6},{5,1},{6,4},{7,3},{8,10},{9,13},{10,... | collective-permute-start | bytes 294920 | tf_op jit(solution)/shard_map/ppermute | solution.py:759
  45.5 2.4 %collective-permute-start.12 = (f32[384,128]{1,0:T(8,128)S(1)}, f32[384,128]{1,0:T(8,128)S(1)}, u32[]{:S(2)}, u32[]{:S(2)}) collective-permute-start(f32[384,128]{1,0:T(8,128)S(1)} %get-tuple-element.21.after_ref), channel_id=1, source_target_pairs={{0,1},{1,0},{2,3},{3,2},{4,5},{5,4},{6,7},{7,6},{8,9},{9,8},{10,11... | collective-permute-start | bytes 589832 | tf_op jit(solution)/shard_map/ppermute | solution.py:716
  47.9 7.9 %collective-permute-start.13 = (f32[384,128]{1,0:T(8,128)S(1)}, f32[384,128]{1,0:T(8,128)S(1)}, u32[]{:S(2)}, u32[]{:S(2)}) collective-permute-start(f32[384,128]{1,0:T(8,128)S(1)} %shard_map.81.left_ref), channel_id=1, source_target_pairs={{0,2},{1,5},{2,0},{3,7},{4,6},{5,1},{6,4},{7,3},{8,10},{9,13},{10,... | collective-permute-start | bytes 589832 | tf_op jit(solution)/shard_map/ppermute | solution.py:771
  49.0 6.8 %collective-permute-start.10 = (bf16[384,128]{1,0:T(8,128)(2,1)S(1)}, bf16[384,128]{1,0:T(8,128)(2,1)S(1)}, u32[]{:S(2)}, u32[]{:S(2)}) collective-permute-start(bf16[384,128]{1,0:T(8,128)(2,1)S(1)} %shard_map.78.left_ref), channel_id=1, source_target_pairs={{0,4},{1,3},{2,6},{3,1},{4,0},{5,7},{6,2},{7,5},{8,12},{9,11},{10,... | collective-permute-start | bytes 294920 | tf_op jit(solution)/shard_map/ppermute | solution.py:767
  51.4 10.2 %collective-permute-start.15 = (f32[416,128]{1,0:T(8,128)S(1)}, f32[416,128]{1,0:T(8,128)S(1)}, u32[]{:S(2)}, u32[]{:S(2)}) collective-permute-start(f32[416,128]{1,0:T(8,128)S(1)} %get-tuple-element.28), channel_id=1, source_target_pairs={{0,8},{8,16},{16,24},{1,9},{9,17},{17,25},{2,10},{10,18},{18,26},{... | collective-permute-start | bytes 638984 | tf_op jit(solution)/shard_map/ppermute | solution.py:712
  55.9 5.7 %collective-permute-start.14 = (f32[384,128]{1,0:T(8,128)S(1)}, f32[384,128]{1,0:T(8,128)S(1)}, u32[]{:S(2)}, u32[]{:S(2)}) collective-permute-start(f32[384,128]{1,0:T(8,128)S(1)} %shard_map.82.left_ref), channel_id=1, source_target_pairs={{0,4},{1,3},{2,6},{3,1},{4,0},{5,7},{6,2},{7,5},{8,12},{9,11},{10,... | collective-permute-start | bytes 589832 | tf_op jit(solution)/shard_map/ppermute | solution.py:772
  56.3 1.3 %collective-permute-start.11 = (bf16[384,128]{1,0:T(8,128)(2,1)S(1)}, bf16[384,128]{1,0:T(8,128)(2,1)S(1)}, u32[]{:S(2)}, u32[]{:S(2)}) collective-permute-start(bf16[384,128]{1,0:T(8,128)(2,1)S(1)} %shard_map.79.mine_ref.refs_0_), channel_id=1, source_target_pairs={{0,1},{1,0},{2,3},{3,2},{4,5},{5,4},{6,7},{7,6},{8,9},{9,8},{10,11... | collective-permute-start | bytes 294920 | tf_op jit(solution)/shard_map/ppermute | solution.py:716
  62.9 1.6 %collective-permute-start.16 = (bf16[304,384]{1,0:T(8,128)(2,1)S(1)}, bf16[304,384]{1,0:T(8,128)(2,1)S(1)}, u32[]{:S(2)}, u32[]{:S(2)}) collective-permute-start(bf16[304,384]{1,0:T(8,128)(2,1)S(1)} %shard_map.84.left_ref), channel_id=1, source_target_pairs={{0,1},{1,0},{2,3},{3,2},{4,5},{5,4},{6,7},{7,6},{8,9},{9,8},{10,11... | collective-permute-start | bytes 700424 | tf_op jit(solution)/shard_map/ppermute | solution.py:716

commit v3 on v2

--- a/solution.py
+++ b/solution.py
@@ -16,6 +16,7 @@
 ANYWHERE = pl.BlockSpec(memory_space=pl.ANY)
 MIB = 1024 * 1024
 FIRST_STAGE_FLOPS = 5000 * 10**6
+LAST_RAY_FLOPS = 3000 * 10**6
 LAST_STAGES_FLOPS = 4000 * 10**6
 
 
@@ -355,14 +356,14 @@
     )(own, first, second, both, after)
 
 
-def add_after(left, right, *after):
+def add_after(left, right, *after, flops=10**5):
     return pl.pallas_call(
         add_kernel,
         in_specs=[WHOLE] * 2 + [ANYWHERE] * len(after),
         out_specs=WHOLE,
         out_shape=jax.ShapeDtypeStruct(left.shape, left.dtype),
         compiler_params=params(),
-        cost_estimate=cost(10**5, 10**5),
+        cost_estimate=cost(flops, 10**5),
     )(left, right, *after)
 
 
@@ -638,25 +639,6 @@
     return jax.ShapeDtypeStruct((channels, 1, channels), jnp.float32)
 
 
-def ray_kernel(scale, core_ref, mine_ref, other_ref, out_ref, token_ref, pack_ref):
-    token_ref[...] = jnp.zeros_like(token_ref)
-    channels = out_ref.shape[0]
-    join(pack_ref, core_ref[0], mine_ref[...].astype(jnp.float32), other_ref[...].astype(jnp.float32))
-    out_ref[:, 0, :] = full_matrix(pack_ref, channels)[0:channels, 0:channels] * scale
-
-
-def unpack_ray(core, mine, other, channels, total_rows):
-    return pl.pallas_call(
-        functools.partial(ray_kernel, 1.0 / total_rows),
-        in_specs=[SCALARS] + [WHOLE] * 2,
-        out_specs=[WHOLE] * 2,
-        out_shape=[matrix_shape(channels), jax.ShapeDtypeStruct((8, LANES), jnp.float32)],
-        scratch_shapes=[pltpu.VMEM((full_rows(channels), LANES), jnp.float32)],
-        compiler_params=params(),
-        cost_estimate=cost(10**5, 10**5),
-    )(core, mine, other)
-
-
 def part_kernel(
     channels, scale, core_ref, mine_ref, inverse_ref, previous_ref, out_ref,
     pack_ref, lower_ref, before_ref,
@@ -689,21 +671,26 @@
     )(core, mine, inverse, previous)
 
 
-def both_kernel(left_ref, right_ref, out_ref):
+def both_kernel(
+    scale, core_ref, left_ref, right_ref, mine_ref, other_ref, out_ref, ray_ref, pack_ref
+):
     channels = out_ref.shape[0]
+    join(pack_ref, core_ref[0], mine_ref[...].astype(jnp.float32), other_ref[...].astype(jnp.float32))
+    ray_ref[:, 0, :] = full_matrix(pack_ref, channels)[0:channels, 0:channels] * scale
     total = left_ref[...].astype(jnp.float32) + right_ref[...].astype(jnp.float32)
     out_ref[:, 0, :] = total[0:channels, 0:channels]
 
 
-def both_parts(left, right, channels):
-    return pl.pallas_call(
-        both_kernel,
-        in_specs=[WHOLE] * 2,
-        out_specs=WHOLE,
-        out_shape=matrix_shape(channels),
+def both_parts(core, left, right, mine, other, channels, total_rows):
+    return pl.pallas_call(
+        functools.partial(both_kernel, 1.0 / total_rows),
+        in_specs=[SCALARS] + [WHOLE] * 4,
+        out_specs=[WHOLE] * 2,
+        out_shape=[matrix_shape(channels)] * 2,
+        scratch_shapes=[pltpu.VMEM((full_rows(channels), LANES), jnp.float32)],
         compiler_params=params(),
         cost_estimate=cost(10**5, 10**5),
-    )(left, right)
+    )(core, left, right, mine, other)
 
 
 def from_behind(value, axis, steps):
@@ -759,19 +746,20 @@
     r_first = lax.ppermute(r_sum, "rows", rounds[0])
     work = first_stage(core, g_sum, other_core(g_sum), channels, total_rows)
     r_sum = add_after(r_sum, r_first, work)
-    m_mine, m_other = cross(core, previous_y, y_t, work, jnp.float32)
+    m_mine, m_other = cross(core, previous_y, y_t, r_sum, jnp.float32)
     inverse, pack = last_stages(work, channels, m_other)
     m_sum = add_after(m_mine, other_core(m_other), inverse)
     previous = from_behind(pack, "sector", 1)
-    for pairs in rounds[1:]:
-        r_sum = add_after(r_sum, lax.ppermute(r_sum, "rows", pairs))
-    rayleigh, token = unpack_ray(core, r_sum, other_core(r_sum), channels, total_rows)
     q_t, basis_token = basis(inverse, y_t)
     for pairs in rounds[:-1]:
-        m_sum = add_after(m_sum, lax.ppermute(m_sum, "rows", pairs), r_sum)
-    m_sum = add_after(m_sum, lax.ppermute(m_sum, "rows", rounds[-1]), token, basis_token)
+        m_sum = add_after(m_sum, lax.ppermute(m_sum, "rows", pairs))
+    m_sum = add_after(m_sum, lax.ppermute(m_sum, "rows", rounds[-1]), basis_token)
     part = correlation_part(core, m_sum, inverse, previous, channels, total_rows)
-    correlation = both_parts(part, other_core(part), channels)
+    for pairs in rounds[1:]:
+        r_sum = add_after(r_sum, lax.ppermute(r_sum, "rows", pairs), flops=LAST_RAY_FLOPS)
+    correlation, rayleigh = both_parts(
+        core, part, other_core(part), r_sum, other_core(r_sum), channels, total_rows
+    )
     return (q_t.T[None], rayleigh.transpose(1, 0, 2), correlation.transpose(1, 0, 2))
 
 

time: 65.7 us -> 64.1 us (0.976)
  starting transfers between devices: 29.8 us -> 28.7 us
  Pallas kernels: 24.9 us -> 24.2 us
    ppermute x2, starting transfers between devices: 3.43 us -> 1.09 us  [the longest x1 1.01 us: shards(): m_sum = add_after(m_sum, lax.ppermute(m_sum, 'rows', pairs))]
    ppermute x6, waiting for transfers between devices: 4.11 us -> 2.36 us  [other_core(): lax.ppermute(value, 'rows', [(s, s ^ 1) for s in range(lax.axis_size('row...]
    ppermute x1, starting transfers between devices: 0.43 us -> 2.05 us  [shards(): lax.ppermute(m_sum, 'rows', rounds[-1])]
    ppermute x2, waiting for transfers between devices: 0.01 us -> 1.29 us  [the longest x1 1.29 us: shards(): m_sum = add_after(m_sum, lax.ppermute(m_sum, 'rows', pairs))]
    ppermute x4, starting transfers between devices: 12.4 us -> 11.5 us  [from_behind(): lax.ppermute(value, axis, [(source, source + steps) for source in range(l...]
    pallas_call x2 -> x1, Pallas kernels: 1.88 us -> 1.14 us  [both_parts(): pl.pallas_call(functools.partial(both_kernel, 1.0 / total_rows), in_specs...]
where the time goes in v3:
time: 64.1 us; the launch traced here: 63.6 us
  starting transfers between devices  28.7 us (45%)
  Pallas kernels  24.2 us (38%)
  waiting for transfers between devices  9.1 us (14%)
  between operations  0.91 us (1%)
  local copies, waits for them, and re-layouts  0.7 us (1%)
    ppermute x4, starting transfers between devices, from_behind(): lax.ppermute(value, axis, [(source, source + steps) for source in range(l...  11.5 us
    ppermute x3, starting transfers between devices, sum_chips(): lax.ppermute(value, 'rows', [(s, s ^ bits) for s in range(count)])  6.73 us
    pallas_call x2, Pallas kernels, tile_product(): pl.pallas_call(functools.partial(tile_kernel, which), in_specs=[WHOLE, AN...  6.41 us
    pallas_call x1, Pallas kernels, first_stage(): pl.pallas_call(functools.partial(first_stage_kernel, channels, 1.0 / tota...  6.39 us
    ppermute x6, starting transfers between devices, other_core(): lax.ppermute(value, 'rows', [(s, s ^ 1) for s in range(lax.axis_size('row...  6.14 us
    ppermute x3, waiting for transfers between devices, sum_chips(): lax.ppermute(value, 'rows', [(s, s ^ bits) for s in range(count)])  3.38 us
    pallas_call x1, Pallas kernels, later_product(): pl.pallas_call(later_kernel, in_specs=[WHOLE, WHOLE, ANYWHERE, WHOLE], ou...  3.15 us
    ppermute x6, waiting for transfers between devices, other_core(): lax.ppermute(value, 'rows', [(s, s ^ 1) for s in range(lax.axis_size('row...  2.36 us
  transfers between devices with their start and end apart: 17, of which 6 were waited for; matrix products, arithmetic and copies ran while one was open for 0% of the time, Pallas kernels for 34%

profile of v3, /device:TPU:0, one launch (start us, length us, event | category | flops | bytes accessed | tf_op | source)
XLA Modules:
  0.0 63.6 jit_solution(8893373701815872469)
XLA Ops:
  0.6 1.4 %collective-permute-start = (bf16[300,1280]{1,0:T(8,128)(2,1)}, bf16[300,1280]{1,0:T(8,128)(2,1)S(1)}, u32[]{:S(2)}, u32[]{:S(2)}) collective-permute-start(bf16[300,1280]{1,0:T(8,128)(2,1)} %bitcast.14), channel_id=1, source_target_pairs={{1,0},{2,1},{3,2},{4,3},{5,4},{6,5},{7,6},{9,8},{10,9},{11,10},{12... | collective-permute-start | bytes 2304008 | tf_op jit(solution)/shard_map/ppermute | solution.py:699
  2.8 3.1 %shard_map.69 = bf16[300,1280]{1,0:T(8,128)(2,1)S(1)} custom-call(s32[10,2,10]{2,1,0:T(2,128)S(1)} %bitcast.18, bf16[300,1280]{1,0:T(8,128)(2,1)} %bitcast.15, bf16[1280,1280]{1,0:T(8,128)(2,1)} %bitcast.21), custom_call_target="tpu_custom_call" | custom-call | flops 983040000 | bytes 3276800 | tf_op jit(solution)/shard_map/pallas_call | solution.py:108
  5.9 3.1 %collective-permute-start.1 = (bf16[300,1280]{1,0:T(8,128)(2,1)S(1)}, bf16[300,1280]{1,0:T(8,128)(2,1)S(1)}, u32[]{:S(2)}, u32[]{:S(2)}) collective-permute-start(bf16[300,1280]{1,0:T(8,128)(2,1)S(1)} %shard_map.69), channel_id=1, source_target_pairs={{0,1},{1,2},{2,3},{3,4},{4,5},{5,6},{6,7},{8,9},{9,10},{10,11},{11... | collective-permute-start | bytes 2304008 | tf_op jit(solution)/shard_map/ppermute | solution.py:699
  9.0 3.3 %shard_map.67.first_ref = f32[300,1280]{1,0:T(8,128)S(1)} custom-call(s32[10,2,10]{2,1,0:T(2,128)S(1)} %bitcast.19, bf16[300,1280]{1,0:T(8,128)(2,1)S(1)} %bitcast.16, bf16[1280,1280]{1,0:T(8,128)(2,1)} %bitcast.23), custom_call_target="tpu_custom_call" | custom-call | flops 983040000 | bytes 3276800 | tf_op jit(solution)/shard_map/pallas_call | solution.py:108
  12.3 3.1 %shard_map.68.part_ref = f32[300,1280]{1,0:T(8,128)S(1)} custom-call(s32[10,2,10]{2,1,0:T(2,128)S(1)} %bitcast.20, bf16[300,1280]{1,0:T(8,128)(2,1)S(1)} %collective-permute-done.later_ref, bf16[1280,1280]{1,0:T(8,128)(2,1)} %bitcast.22, f32[300,1280]{1,0:T(8,128)S(1)} %shard_map.67.first_ref), custom_call_target="tpu_custom_call" | custom-call | flops 983040000 | bytes 3276800 | tf_op jit(solution)/shard_map/pallas_call | solution.py:143
  16.1 4.9 %collective-permute-start.2 = (f32[208,128]{1,0:T(8,128)S(1)}, f32[208,128]{1,0:T(8,128)S(1)}, u32[]{:S(2)}, u32[]{:S(2)}) collective-permute-start(f32[208,128]{1,0:T(8,128)S(1)} %get-tuple-element.17), channel_id=1, source_target_pairs={{0,1},{1,0},{2,3},{3,2},{4,5},{5,4},{6,7},{7,6},{8,9},{9,8},{10,11... | collective-permute-start | bytes 319496 | tf_op jit(solution)/shard_map/ppermute | solution.py:703
  21.0 3.5 %collective-permute-start.8 = (bf16[300,1280]{1,0:T(8,128)(2,1)S(1)}, bf16[300,1280]{1,0:T(8,128)(2,1)S(1)}, u32[]{:S(2)}, u32[]{:S(2)}) collective-permute-start(bf16[300,1280]{1,0:T(8,128)(2,1)S(1)} %get-tuple-element.18.right_ref.y_ref), channel_id=1, source_target_pairs={{0,8},{8,16},{16,24},{1,9},{9,17},{17,25},{2,10},{10,18},{18,26},{... | collective-permute-start | bytes 2304008 | tf_op jit(solution)/shard_map/ppermute | solution.py:699
  24.5 3.4 %collective-permute-start.3 = (f32[208,128]{1,0:T(8,128)S(1)}, f32[208,128]{1,0:T(8,128)S(1)}, u32[]{:S(2)}, u32[]{:S(2)}) collective-permute-start(f32[208,128]{1,0:T(8,128)S(1)} %add.8.after_ref.own_ref), channel_id=1, source_target_pairs={{0,2},{1,3},{2,0},{3,1},{4,6},{5,7},{6,4},{7,5},{8,10},{9,11},{10,... | collective-permute-start | bytes 319496 | tf_op jit(solution)/shard_map/ppermute | solution.py:721
  28.0 3.3 %collective-permute-start.4 = (f32[208,128]{1,0:T(8,128)S(1)}, f32[208,128]{1,0:T(8,128)S(1)}, u32[]{:S(2)}, u32[]{:S(2)}) collective-permute-start(f32[208,128]{1,0:T(8,128)S(1)} %add.8.after_ref.own_ref), channel_id=1, source_target_pairs={{0,4},{1,5},{2,6},{3,7},{4,0},{5,1},{6,2},{7,3},{8,12},{9,13},{10,... | collective-permute-start | bytes 319496 | tf_op jit(solution)/shard_map/ppermute | solution.py:721
  32.1 1.3 %collective-permute-done.6.right_ref = bf16[384,128]{1,0:T(8,128)(2,1)S(1)} collective-permute-done((bf16[384,128]{1,0:T(8,128)(2,1)S(1)}, bf16[384,128]{1,0:T(8,128)(2,1)S(1)}, u32[]{:S(2)}, u32[]{:S(2)}) %collective-permute-start.6) | collective-permute-done | bytes 98336 | tf_op jit(solution)/shard_map/ppermute | solution.py:703
  33.5 2.4 %collective-permute-done.4.second_ref = f32[208,128]{1,0:T(8,128)S(1)} collective-permute-done((f32[208,128]{1,0:T(8,128)S(1)}, f32[208,128]{1,0:T(8,128)S(1)}, u32[]{:S(2)}, u32[]{:S(2)}) %collective-permute-start.4) | collective-permute-done | bytes 106528 | tf_op jit(solution)/shard_map/ppermute | solution.py:721
  35.8 1.0 %collective-permute-done.5.both_ref = f32[208,128]{1,0:T(8,128)S(1)} collective-permute-done((f32[208,128]{1,0:T(8,128)S(1)}, f32[208,128]{1,0:T(8,128)S(1)}, u32[]{:S(2)}, u32[]{:S(2)}) %collective-permute-start.5) | collective-permute-done | bytes 106528 | tf_op jit(solution)/shard_map/ppermute | solution.py:721
  37.0 1.3 %collective-permute-start.9 = (bf16[384,128]{1,0:T(8,128)(2,1)S(1)}, bf16[384,128]{1,0:T(8,128)(2,1)S(1)}, u32[]{:S(2)}, u32[]{:S(2)}) collective-permute-start(bf16[384,128]{1,0:T(8,128)(2,1)S(1)} %shard_map.72.after_ref.left_ref), channel_id=1, source_target_pairs={{0,2},{1,5},{2,0},{3,7},{4,6},{5,1},{6,4},{7,3},{8,10},{9,13},{10,... | collective-permute-start | bytes 294920 | tf_op jit(solution)/shard_map/ppermute | solution.py:746
  38.3 6.4 %shard_map.74.refs_0_.before_ref = f32[304,384]{1,0:T(8,128)S(1)} custom-call(s32[1]{0:T(128)} %bitcast.core_ref, f32[208,128]{1,0:T(8,128)S(1)} %shard_map.73.mine_ref, f32[208,128]{1,0:T(8,128)S(1)} %collective-permute-done.7.other_ref), custom_call_target="tpu_custom_call" | custom-call | flops 5000000000 | bytes 1000000 | tf_op jit(solution)/shard_map/pallas_call | solution.py:552
  46.0 1.9 %shard_map.77 = (f32[304,384]{1,0:T(8,128)S(1)}, f32[416,128]{1,0:T(8,128)S(1)}) custom-call(f32[304,384]{1,0:T(8,128)S(1)} %shard_map.74.refs_0_.before_ref, f32[384,128]{1,0:T(8,128)S(1)} %get-tuple-element.21.after_ref), custom_call_target="tpu_custom_call" | custom-call | flops 4000000000 | bytes 100000 | tf_op jit(solution)/shard_map/pallas_call | solution.py:568
  48.0 1.0 %collective-permute-start.11 = (f32[384,128]{1,0:T(8,128)S(1)}, f32[384,128]{1,0:T(8,128)S(1)}, u32[]{:S(2)}, u32[]{:S(2)}) collective-permute-start(f32[384,128]{1,0:T(8,128)S(1)} %shard_map.79.left_ref), channel_id=1, source_target_pairs={{0,2},{1,5},{2,0},{3,7},{4,6},{5,1},{6,4},{7,3},{8,10},{9,13},{10,... | collective-permute-start | bytes 589832 | tf_op jit(solution)/shard_map/ppermute | solution.py:755
  49.0 3.4 %collective-permute-start.13 = (f32[416,128]{1,0:T(8,128)S(1)}, f32[416,128]{1,0:T(8,128)S(1)}, u32[]{:S(2)}, u32[]{:S(2)}) collective-permute-start(f32[416,128]{1,0:T(8,128)S(1)} %get-tuple-element.26), channel_id=1, source_target_pairs={{0,8},{8,16},{16,24},{1,9},{9,17},{17,25},{2,10},{10,18},{18,26},{... | collective-permute-start | bytes 638984 | tf_op jit(solution)/shard_map/ppermute | solution.py:699
  52.4 1.3 %collective-permute-done.11.right_ref = f32[384,128]{1,0:T(8,128)S(1)} collective-permute-done((f32[384,128]{1,0:T(8,128)S(1)}, f32[384,128]{1,0:T(8,128)S(1)}, u32[]{:S(2)}, u32[]{:S(2)}) %collective-permute-start.11) | collective-permute-done | bytes 196640 | tf_op jit(solution)/shard_map/ppermute | solution.py:755
  53.7 2.0 %collective-permute-start.12 = (f32[384,128]{1,0:T(8,128)S(1)}, f32[384,128]{1,0:T(8,128)S(1)}, u32[]{:S(2)}, u32[]{:S(2)}) collective-permute-start(f32[384,128]{1,0:T(8,128)S(1)} %shard_map.80.left_ref), channel_id=1, source_target_pairs={{0,4},{1,3},{2,6},{3,1},{4,0},{5,7},{6,2},{7,5},{8,12},{9,11},{10,... | collective-permute-start | bytes 589832 | tf_op jit(solution)/shard_map/ppermute | solution.py:756
  55.9 1.5 %shard_map.78 = (bf16[300,1280]{1,0:T(8,128)(2,1)}, f32[8,128]{1,0:T(8,128)S(1)}) custom-call(f32[304,384]{1,0:T(8,128)S(1)} %get-tuple-element.22.inverse_ref.refs_0_, bf16[300,1280]{1,0:T(8,128)(2,1)S(1)} %get-tuple-element.18.right_ref.y_ref), custom_call_target="tpu_custom_call" | custom-call | flops 100000 | bytes 100000 | tf_op jit(solution)/shard_map/pallas_call | solution.py:625
  57.4 2.1 %collective-permute-done.12.right_ref = f32[384,128]{1,0:T(8,128)S(1)} collective-permute-done((f32[384,128]{1,0:T(8,128)S(1)}, f32[384,128]{1,0:T(8,128)S(1)}, u32[]{:S(2)}, u32[]{:S(2)}) %collective-permute-start.12) | collective-permute-done | bytes 196640 | tf_op jit(solution)/shard_map/ppermute | solution.py:756
  59.5 1.3 %shard_map.82.left_ref = bf16[304,384]{1,0:T(8,128)(2,1)S(1)} custom-call(s32[1]{0:T(128)} %bitcast.core_ref, f32[384,128]{1,0:T(8,128)S(1)} %shard_map.81.mine_ref, f32[304,384]{1,0:T(8,128)S(1)} %get-tuple-element.22.inverse_ref.refs_0_, f32[416,128]{1,0:T(8,128)S(1)} %collective-permute-done.13.previous_ref), custom_call_target="tpu_custom_call" | custom-call | flops 100000 | bytes 100000 | tf_op jit(solution)/shard_map/pallas_call | solution.py:659
  61.5 1.0 %collective-permute-done.16.other_ref = bf16[384,128]{1,0:T(8,128)(2,1)S(1)} collective-permute-done((bf16[384,128]{1,0:T(8,128)(2,1)S(1)}, bf16[384,128]{1,0:T(8,128)(2,1)S(1)}, u32[]{:S(2)}, u32[]{:S(2)}) %collective-permute-start.16) | collective-permute-done | bytes 98336 | tf_op jit(solution)/shard_map/ppermute | solution.py:703
  62.5 1.1 %shard_map.84 = (f32[300,1,300]{2,1,0:T(1,128)}, f32[300,1,300]{2,1,0:T(1,128)}) custom-call(s32[1]{0:T(128)} %bitcast.core_ref, bf16[304,384]{1,0:T(8,128)(2,1)S(1)} %shard_map.82.left_ref, bf16[304,384]{1,0:T(8,128)(2,1)S(1)} %collective-permute-done.14.right_ref, bf16[384,128]{1,0:T(8,128)(2,1)S(1)} %shard_map.83.mine_ref, ...), custom_call_target="tpu_custom_call" | custom-call | flops 100000 | bytes 100000 | tf_op jit(solution)/shard_map/pallas_call | solution.py:685
  (35 shorter events, 4.5 us)
Async XLA Ops:
  0.6 8.4 %copy-start = (bf16[1,1280,300]{1,2,0:T(8,128)(2,1)S(1)}, bf16[1,1280,300]{1,2,0:T(8,128)(2,1)}, u32[]{:S(2)}) copy-start(bf16[1,1280,300]{1,2,0:T(8,128)(2,1)} %param.4) | copy-start | bytes 2304004
  0.6 11.7 %collective-permute-start = (bf16[300,1280]{1,0:T(8,128)(2,1)}, bf16[300,1280]{1,0:T(8,128)(2,1)S(1)}, u32[]{:S(2)}, u32[]{:S(2)}) collective-permute-start(bf16[300,1280]{1,0:T(8,128)(2,1)} %bitcast.14), channel_id=1, source_target_pairs={{1,0},{2,1},{3,2},{4,3},{5,4},{6,5},{7,6},{9,8},{10,9},{11,10},{12... | collective-permute-start | bytes 2304008 | tf_op jit(solution)/shard_map/ppermute | solution.py:699
  2.1 0.7 %copy-start.1 = (s32[1,2,10,10]{3,1,2,0:T(2,128)S(1)}, s32[1,2,10,10]{3,1,2,0:T(2,128)}, u32[]{:S(2)}) copy-start(s32[1,2,10,10]{3,1,2,0:T(2,128)} %param.7) | copy-start | bytes 2404
  2.8 6.3 %copy-start.2 = (s32[1,2,10,10]{3,1,2,0:T(2,128)S(1)}, s32[1,2,10,10]{3,1,2,0:T(2,128)}, u32[]{:S(2)}) copy-start(s32[1,2,10,10]{3,1,2,0:T(2,128)} %param.7) | copy-start | bytes 2404
  5.9 9.6 %collective-permute-start.1 = (bf16[300,1280]{1,0:T(8,128)(2,1)S(1)}, bf16[300,1280]{1,0:T(8,128)(2,1)S(1)}, u32[]{:S(2)}, u32[]{:S(2)}) collective-permute-start(bf16[300,1280]{1,0:T(8,128)(2,1)S(1)} %shard_map.69), channel_id=1, source_target_pairs={{0,1},{1,2},{2,3},{3,4},{4,5},{5,6},{6,7},{8,9},{9,10},{10,11},{11... | collective-permute-start | bytes 2304008 | tf_op jit(solution)/shard_map/ppermute | solution.py:699
  16.1 8.4 %collective-permute-start.2 = (f32[208,128]{1,0:T(8,128)S(1)}, f32[208,128]{1,0:T(8,128)S(1)}, u32[]{:S(2)}, u32[]{:S(2)}) collective-permute-start(f32[208,128]{1,0:T(8,128)S(1)} %get-tuple-element.17), channel_id=1, source_target_pairs={{0,1},{1,0},{2,3},{3,2},{4,5},{5,4},{6,7},{7,6},{8,9},{9,8},{10,11... | collective-permute-start | bytes 319496 | tf_op jit(solution)/shard_map/ppermute | solution.py:703
  21.0 23.7 %collective-permute-start.8 = (bf16[300,1280]{1,0:T(8,128)(2,1)S(1)}, bf16[300,1280]{1,0:T(8,128)(2,1)S(1)}, u32[]{:S(2)}, u32[]{:S(2)}) collective-permute-start(bf16[300,1280]{1,0:T(8,128)(2,1)S(1)} %get-tuple-element.18.right_ref.y_ref), channel_id=1, source_target_pairs={{0,8},{8,16},{16,24},{1,9},{9,17},{17,25},{2,10},{10,18},{18,26},{... | collective-permute-start | bytes 2304008 | tf_op jit(solution)/shard_map/ppermute | solution.py:699
  24.5 8.9 %collective-permute-start.3 = (f32[208,128]{1,0:T(8,128)S(1)}, f32[208,128]{1,0:T(8,128)S(1)}, u32[]{:S(2)}, u32[]{:S(2)}) collective-permute-start(f32[208,128]{1,0:T(8,128)S(1)} %add.8.after_ref.own_ref), channel_id=1, source_target_pairs={{0,2},{1,3},{2,0},{3,1},{4,6},{5,7},{6,4},{7,5},{8,10},{9,11},{10,... | collective-permute-start | bytes 319496 | tf_op jit(solution)/shard_map/ppermute | solution.py:721
  28.0 7.9 %collective-permute-start.4 = (f32[208,128]{1,0:T(8,128)S(1)}, f32[208,128]{1,0:T(8,128)S(1)}, u32[]{:S(2)}, u32[]{:S(2)}) collective-permute-start(f32[208,128]{1,0:T(8,128)S(1)} %add.8.after_ref.own_ref), channel_id=1, source_target_pairs={{0,4},{1,5},{2,6},{3,7},{4,0},{5,1},{6,2},{7,3},{8,12},{9,13},{10,... | collective-permute-start | bytes 319496 | tf_op jit(solution)/shard_map/ppermute | solution.py:721
  31.2 5.6 %collective-permute-start.5 = (f32[208,128]{1,0:T(8,128)S(1)}, f32[208,128]{1,0:T(8,128)S(1)}, u32[]{:S(2)}, u32[]{:S(2)}) collective-permute-start(f32[208,128]{1,0:T(8,128)S(1)} %add.8.after_ref.own_ref), channel_id=1, source_target_pairs={{0,6},{1,7},{2,4},{3,5},{4,2},{5,3},{6,0},{7,1},{8,14},{9,15},{10,... | collective-permute-start | bytes 319496 | tf_op jit(solution)/shard_map/ppermute | solution.py:721
  32.1 1.4 %collective-permute-start.6 = (bf16[384,128]{1,0:T(8,128)(2,1)S(1)}, bf16[384,128]{1,0:T(8,128)(2,1)S(1)}, u32[]{:S(2)}, u32[]{:S(2)}) collective-permute-start(bf16[384,128]{1,0:T(8,128)(2,1)S(1)} %get-tuple-element.20), channel_id=1, source_target_pairs={{0,1},{1,0},{2,3},{3,2},{4,5},{5,4},{6,7},{7,6},{8,9},{9,8},{10,11... | collective-permute-start | bytes 294920 | tf_op jit(solution)/shard_map/ppermute | solution.py:703
  36.9 1.4 %collective-permute-start.7 = (f32[208,128]{1,0:T(8,128)S(1)}, f32[208,128]{1,0:T(8,128)S(1)}, u32[]{:S(2)}, u32[]{:S(2)}) collective-permute-start(f32[208,128]{1,0:T(8,128)S(1)} %shard_map.73.mine_ref), channel_id=1, source_target_pairs={{0,1},{1,0},{2,3},{3,2},{4,5},{5,4},{6,7},{7,6},{8,9},{9,8},{10,11... | collective-permute-start | bytes 319496 | tf_op jit(solution)/shard_map/ppermute | solution.py:703
  37.0 7.7 %collective-permute-start.9 = (bf16[384,128]{1,0:T(8,128)(2,1)S(1)}, bf16[384,128]{1,0:T(8,128)(2,1)S(1)}, u32[]{:S(2)}, u32[]{:S(2)}) collective-permute-start(bf16[384,128]{1,0:T(8,128)(2,1)S(1)} %shard_map.72.after_ref.left_ref), channel_id=1, source_target_pairs={{0,2},{1,5},{2,0},{3,7},{4,6},{5,1},{6,4},{7,3},{8,10},{9,13},{10,... | collective-permute-start | bytes 294920 | tf_op jit(solution)/shard_map/ppermute | solution.py:746
  45.5 2.4 %collective-permute-start.10 = (f32[384,128]{1,0:T(8,128)S(1)}, f32[384,128]{1,0:T(8,128)S(1)}, u32[]{:S(2)}, u32[]{:S(2)}) collective-permute-start(f32[384,128]{1,0:T(8,128)S(1)} %get-tuple-element.21.after_ref), channel_id=1, source_target_pairs={{0,1},{1,0},{2,3},{3,2},{4,5},{5,4},{6,7},{7,6},{8,9},{9,8},{10,11... | collective-permute-start | bytes 589832 | tf_op jit(solution)/shard_map/ppermute | solution.py:703
  48.0 5.7 %collective-permute-start.11 = (f32[384,128]{1,0:T(8,128)S(1)}, f32[384,128]{1,0:T(8,128)S(1)}, u32[]{:S(2)}, u32[]{:S(2)}) collective-permute-start(f32[384,128]{1,0:T(8,128)S(1)} %shard_map.79.left_ref), channel_id=1, source_target_pairs={{0,2},{1,5},{2,0},{3,7},{4,6},{5,1},{6,4},{7,3},{8,10},{9,13},{10,... | collective-permute-start | bytes 589832 | tf_op jit(solution)/shard_map/ppermute | solution.py:755
  49.0 10.5 %collective-permute-start.13 = (f32[416,128]{1,0:T(8,128)S(1)}, f32[416,128]{1,0:T(8,128)S(1)}, u32[]{:S(2)}, u32[]{:S(2)}) collective-permute-start(f32[416,128]{1,0:T(8,128)S(1)} %get-tuple-element.26), channel_id=1, source_target_pairs={{0,8},{8,16},{16,24},{1,9},{9,17},{17,25},{2,10},{10,18},{18,26},{... | collective-permute-start | bytes 638984 | tf_op jit(solution)/shard_map/ppermute | solution.py:699
  53.7 5.7 %collective-permute-start.12 = (f32[384,128]{1,0:T(8,128)S(1)}, f32[384,128]{1,0:T(8,128)S(1)}, u32[]{:S(2)}, u32[]{:S(2)}) collective-permute-start(f32[384,128]{1,0:T(8,128)S(1)} %shard_map.80.left_ref), channel_id=1, source_target_pairs={{0,4},{1,3},{2,6},{3,1},{4,0},{5,7},{6,2},{7,5},{8,12},{9,11},{10,... | collective-permute-start | bytes 589832 | tf_op jit(solution)/shard_map/ppermute | solution.py:756
  55.8 5.1 %collective-permute-start.15 = (bf16[384,128]{1,0:T(8,128)(2,1)S(1)}, bf16[384,128]{1,0:T(8,128)(2,1)S(1)}, u32[]{:S(2)}, u32[]{:S(2)}) collective-permute-start(bf16[384,128]{1,0:T(8,128)(2,1)S(1)} %shard_map.75.after_ref.left_ref), channel_id=1, source_target_pairs={{0,4},{1,3},{2,6},{3,1},{4,0},{5,7},{6,2},{7,5},{8,12},{9,11},{10,... | collective-permute-start | bytes 294920 | tf_op jit(solution)/shard_map/ppermute | solution.py:759
  60.8 1.7 %collective-permute-start.14 = (bf16[304,384]{1,0:T(8,128)(2,1)S(1)}, bf16[304,384]{1,0:T(8,128)(2,1)S(1)}, u32[]{:S(2)}, u32[]{:S(2)}) collective-permute-start(bf16[304,384]{1,0:T(8,128)(2,1)S(1)} %shard_map.82.left_ref), channel_id=1, source_target_pairs={{0,1},{1,0},{2,3},{3,2},{4,5},{5,4},{6,7},{7,6},{8,9},{9,8},{10,11... | collective-permute-start | bytes 700424 | tf_op jit(solution)/shard_map/ppermute | solution.py:703
  60.9 1.6 %collective-permute-start.16 = (bf16[384,128]{1,0:T(8,128)(2,1)S(1)}, bf16[384,128]{1,0:T(8,128)(2,1)S(1)}, u32[]{:S(2)}, u32[]{:S(2)}) collective-permute-start(bf16[384,128]{1,0:T(8,128)(2,1)S(1)} %shard_map.83.mine_ref), channel_id=1, source_target_pairs={{0,1},{1,0},{2,3},{3,2},{4,5},{5,4},{6,7},{7,6},{8,9},{9,8},{10,11... | collective-permute-start | bytes 294920 | tf_op jit(solution)/shard_map/ppermute | solution.py:703

commit v4 on v3

--- a/solution.py
+++ b/solution.py
@@ -10,7 +10,7 @@
 SUBBLOCK = 128
 LANES = 128
 PANEL = 16
-EARLY_PANELS = 6
+EARLY_PANELS = 7
 WHOLE = pl.BlockSpec(memory_space=pltpu.VMEM)
 SCALARS = pl.BlockSpec(memory_space=pltpu.SMEM)
 ANYWHERE = pl.BlockSpec(memory_space=pl.ANY)
@@ -38,19 +38,21 @@
     )
 
 
-def block_mask(mask_ref, which, cols):
+def block_mask(mask_ref, which, cols, dtype):
     blocks = mask_ref[:, which, :].astype(jnp.float32)
     col = lax.broadcasted_iota(jnp.int32, (blocks.shape[1], cols), 1)
     block = lax.broadcasted_iota(jnp.int32, (blocks.shape[1], cols), 0)
-    return dot(blocks, jnp.where(col // SUBBLOCK == block, 1.0, 0.0), ((1,), (0,)))
+    wide = dot(blocks, jnp.where(col // SUBBLOCK == block, 1.0, 0.0), ((1,), (0,)))
+    return [
+        jnp.broadcast_to(wide[i : i + 1, :], (PANEL, cols)).astype(dtype)
+        for i in range(blocks.shape[0])
+    ]
 
 
 def mask_rows(tile_ref, mask, start, size):
-    cols = tile_ref.shape[1]
     for i in range(start // SUBBLOCK, (start + size) // SUBBLOCK):
-        keep = jnp.broadcast_to(mask[i : i + 1, :], (PANEL, cols)).astype(tile_ref.dtype)
         for row in range(i * SUBBLOCK, (i + 1) * SUBBLOCK, PANEL):
-            tile_ref[row : row + PANEL, :] = tile_ref[row : row + PANEL, :] * keep
+            tile_ref[row : row + PANEL, :] = tile_ref[row : row + PANEL, :] * mask[i]
 
 
 def strips(rows, width):
@@ -74,6 +76,8 @@
     rows = tile_ref.shape[0]
     for n, (start, size) in enumerate(halves(rows)):
         copies[n].wait()
+        if n + 1 < len(copies):
+            copies[n + 1].start()
         mask_rows(tile_ref, mask, start, size)
         last = n + 1 == len(copies)
         for col, cols in strips(rows, 2 * SUBBLOCK):
@@ -95,10 +99,9 @@
     rows = tile_ref.shape[0]
     copies = copies_of(tile_hbm, tile_ref, sems)
     copy_x = pltpu.make_async_copy(x_hbm, x_ref, x_sem)
+    copies[0].start()
     copy_x.start()
-    for copy in copies:
-        copy.start()
-    mask = block_mask(mask_ref, which, rows)
+    mask = block_mask(mask_ref, which, rows, tile_ref.dtype)
     copy_x.wait()
     product(x_ref, tile_ref, copies, mask, sum_ref, out_ref)
 
@@ -127,7 +130,7 @@
     copies = copies_of(tile_hbm, tile_ref, sems)
     for copy in copies:
         copy.start()
-    mask = block_mask(mask_ref, 1, rows)
+    mask = block_mask(mask_ref, 1, rows, tile_ref.dtype)
     for n, (start, size) in enumerate(halves(rows)):
         copies[n].wait()
         mask_rows(tile_ref, mask, start, size)

time: 64.1 us -> 64.1 us (level)
  Pallas kernels: 24.2 us -> 25.6 us
  starting transfers between devices: 28.7 us -> 27.3 us
    pallas_call x2, Pallas kernels: 6.41 us -> 7.78 us  [tile_product(): pl.pallas_call(functools.partial(tile_kernel, which), in_specs=[WHOLE, AN...]
    ppermute x3, starting transfers between devices: 6.73 us -> 5.86 us  [sum_chips(): lax.ppermute(value, 'rows', [(s, s ^ bits) for s in range(count)])]
  transfers between devices with their start and end apart: 17 -> 17, of which waited for: 6 -> 6; matrix products, arithmetic and copies ran while one was open for 0% -> 0% of each run, Pallas kernels for 34% -> 36%
where the time goes in v4:
time: 64.1 us; the launch traced here: 63.7 us
  starting transfers between devices  27.3 us (43%)
  Pallas kernels  25.6 us (40%)
  waiting for transfers between devices  9.14 us (14%)
  between operations  0.9 us (1%)
  local copies, waits for them, and re-layouts  0.7 us (1%)
    ppermute x4, starting transfers between devices, from_behind(): lax.ppermute(value, axis, [(source, source + steps) for source in range(l...  11.5 us
    pallas_call x2, Pallas kernels, tile_product(): pl.pallas_call(functools.partial(tile_kernel, which), in_specs=[WHOLE, AN...  7.78 us
    pallas_call x1, Pallas kernels, first_stage(): pl.pallas_call(functools.partial(first_stage_kernel, channels, 1.0 / tota...  6.82 us
    ppermute x3, starting transfers between devices, sum_chips(): lax.ppermute(value, 'rows', [(s, s ^ bits) for s in range(count)])  5.86 us
    ppermute x6, starting transfers between devices, other_core(): lax.ppermute(value, 'rows', [(s, s ^ 1) for s in range(lax.axis_size('row...  5.64 us
    ppermute x3, waiting for transfers between devices, sum_chips(): lax.ppermute(value, 'rows', [(s, s ^ bits) for s in range(count)])  3.38 us
    pallas_call x1, Pallas kernels, later_product(): pl.pallas_call(later_kernel, in_specs=[WHOLE, WHOLE, ANYWHERE, WHOLE], ou...  3.15 us
    ppermute x6, waiting for transfers between devices, other_core(): lax.ppermute(value, 'rows', [(s, s ^ 1) for s in range(lax.axis_size('row...  2.36 us
  transfers between devices with their start and end apart: 17, of which 6 were waited for; matrix products, arithmetic and copies ran while one was open for 0% of the time, Pallas kernels for 36%

profile of v4, /device:TPU:0, one launch (start us, length us, event | category | flops | bytes accessed | tf_op | source)
XLA Modules:
  0.0 63.7 jit_solution(2926747679485863816)
XLA Ops:
  0.6 1.4 %collective-permute-start = (bf16[300,1280]{1,0:T(8,128)(2,1)}, bf16[300,1280]{1,0:T(8,128)(2,1)S(1)}, u32[]{:S(2)}, u32[]{:S(2)}) collective-permute-start(bf16[300,1280]{1,0:T(8,128)(2,1)} %bitcast.14), channel_id=1, source_target_pairs={{1,0},{2,1},{3,2},{4,3},{5,4},{6,5},{7,6},{9,8},{10,9},{11,10},{12... | collective-permute-start | bytes 2304008 | tf_op jit(solution)/shard_map/ppermute | solution.py:702
  2.8 4.0 %shard_map.69 = bf16[300,1280]{1,0:T(8,128)(2,1)S(1)} custom-call(s32[10,2,10]{2,1,0:T(2,128)S(1)} %bitcast.18, bf16[300,1280]{1,0:T(8,128)(2,1)} %bitcast.15, bf16[1280,1280]{1,0:T(8,128)(2,1)} %bitcast.21), custom_call_target="tpu_custom_call" | custom-call | flops 983040000 | bytes 3276800 | tf_op jit(solution)/shard_map/pallas_call | solution.py:111
  6.8 3.1 %collective-permute-start.1 = (bf16[300,1280]{1,0:T(8,128)(2,1)S(1)}, bf16[300,1280]{1,0:T(8,128)(2,1)S(1)}, u32[]{:S(2)}, u32[]{:S(2)}) collective-permute-start(bf16[300,1280]{1,0:T(8,128)(2,1)S(1)} %shard_map.69), channel_id=1, source_target_pairs={{0,1},{1,2},{2,3},{3,4},{4,5},{5,6},{6,7},{8,9},{9,10},{10,11},{11... | collective-permute-start | bytes 2304008 | tf_op jit(solution)/shard_map/ppermute | solution.py:702
  9.9 3.8 %shard_map.67.first_ref = f32[300,1280]{1,0:T(8,128)S(1)} custom-call(s32[10,2,10]{2,1,0:T(2,128)S(1)} %bitcast.19, bf16[300,1280]{1,0:T(8,128)(2,1)S(1)} %bitcast.16, bf16[1280,1280]{1,0:T(8,128)(2,1)} %bitcast.23), custom_call_target="tpu_custom_call" | custom-call | flops 983040000 | bytes 3276800 | tf_op jit(solution)/shard_map/pallas_call | solution.py:111
  13.7 3.1 %shard_map.68.part_ref = f32[300,1280]{1,0:T(8,128)S(1)} custom-call(s32[10,2,10]{2,1,0:T(2,128)S(1)} %bitcast.20, bf16[300,1280]{1,0:T(8,128)(2,1)S(1)} %collective-permute-done.later_ref, bf16[1280,1280]{1,0:T(8,128)(2,1)} %bitcast.22, f32[300,1280]{1,0:T(8,128)S(1)} %shard_map.67.first_ref), custom_call_target="tpu_custom_call" | custom-call | flops 983040000 | bytes 3276800 | tf_op jit(solution)/shard_map/pallas_call | solution.py:146
  17.4 4.4 %collective-permute-start.2 = (f32[208,128]{1,0:T(8,128)S(1)}, f32[208,128]{1,0:T(8,128)S(1)}, u32[]{:S(2)}, u32[]{:S(2)}) collective-permute-start(f32[208,128]{1,0:T(8,128)S(1)} %get-tuple-element.17), channel_id=1, source_target_pairs={{0,1},{1,0},{2,3},{3,2},{4,5},{5,4},{6,7},{7,6},{8,9},{9,8},{10,11... | collective-permute-start | bytes 319496 | tf_op jit(solution)/shard_map/ppermute | solution.py:706
  21.8 3.5 %collective-permute-start.8 = (bf16[300,1280]{1,0:T(8,128)(2,1)S(1)}, bf16[300,1280]{1,0:T(8,128)(2,1)S(1)}, u32[]{:S(2)}, u32[]{:S(2)}) collective-permute-start(bf16[300,1280]{1,0:T(8,128)(2,1)S(1)} %get-tuple-element.18.right_ref.y_ref), channel_id=1, source_target_pairs={{0,8},{8,16},{16,24},{1,9},{9,17},{17,25},{2,10},{10,18},{18,26},{... | collective-permute-start | bytes 2304008 | tf_op jit(solution)/shard_map/ppermute | solution.py:702
  25.4 2.6 %collective-permute-start.3 = (f32[208,128]{1,0:T(8,128)S(1)}, f32[208,128]{1,0:T(8,128)S(1)}, u32[]{:S(2)}, u32[]{:S(2)}) collective-permute-start(f32[208,128]{1,0:T(8,128)S(1)} %add.8.after_ref.own_ref), channel_id=1, source_target_pairs={{0,2},{1,3},{2,0},{3,1},{4,6},{5,7},{6,4},{7,5},{8,10},{9,11},{10,... | collective-permute-start | bytes 319496 | tf_op jit(solution)/shard_map/ppermute | solution.py:724
  28.0 3.3 %collective-permute-start.4 = (f32[208,128]{1,0:T(8,128)S(1)}, f32[208,128]{1,0:T(8,128)S(1)}, u32[]{:S(2)}, u32[]{:S(2)}) collective-permute-start(f32[208,128]{1,0:T(8,128)S(1)} %add.8.after_ref.own_ref), channel_id=1, source_target_pairs={{0,4},{1,5},{2,6},{3,7},{4,0},{5,1},{6,2},{7,3},{8,12},{9,13},{10,... | collective-permute-start | bytes 319496 | tf_op jit(solution)/shard_map/ppermute | solution.py:724
  32.1 1.3 %collective-permute-done.6.right_ref = bf16[384,128]{1,0:T(8,128)(2,1)S(1)} collective-permute-done((bf16[384,128]{1,0:T(8,128)(2,1)S(1)}, bf16[384,128]{1,0:T(8,128)(2,1)S(1)}, u32[]{:S(2)}, u32[]{:S(2)}) %collective-permute-start.6) | collective-permute-done | bytes 98336 | tf_op jit(solution)/shard_map/ppermute | solution.py:706
  33.5 2.4 %collective-permute-done.4.second_ref = f32[208,128]{1,0:T(8,128)S(1)} collective-permute-done((f32[208,128]{1,0:T(8,128)S(1)}, f32[208,128]{1,0:T(8,128)S(1)}, u32[]{:S(2)}, u32[]{:S(2)}) %collective-permute-start.4) | collective-permute-done | bytes 106528 | tf_op jit(solution)/shard_map/ppermute | solution.py:724
  35.8 1.0 %collective-permute-done.5.both_ref = f32[208,128]{1,0:T(8,128)S(1)} collective-permute-done((f32[208,128]{1,0:T(8,128)S(1)}, f32[208,128]{1,0:T(8,128)S(1)}, u32[]{:S(2)}, u32[]{:S(2)}) %collective-permute-start.5) | collective-permute-done | bytes 106528 | tf_op jit(solution)/shard_map/ppermute | solution.py:724
  37.0 1.3 %collective-permute-start.9 = (bf16[384,128]{1,0:T(8,128)(2,1)S(1)}, bf16[384,128]{1,0:T(8,128)(2,1)S(1)}, u32[]{:S(2)}, u32[]{:S(2)}) collective-permute-start(bf16[384,128]{1,0:T(8,128)(2,1)S(1)} %shard_map.72.after_ref.left_ref), channel_id=1, source_target_pairs={{0,2},{1,5},{2,0},{3,7},{4,6},{5,1},{6,4},{7,3},{8,10},{9,13},{10,... | collective-permute-start | bytes 294920 | tf_op jit(solution)/shard_map/ppermute | solution.py:749
  38.3 6.8 %shard_map.74.refs_0_.before_ref = f32[304,384]{1,0:T(8,128)S(1)} custom-call(s32[1]{0:T(128)} %bitcast.core_ref, f32[208,128]{1,0:T(8,128)S(1)} %shard_map.73.mine_ref, f32[208,128]{1,0:T(8,128)S(1)} %collective-permute-done.7.other_ref), custom_call_target="tpu_custom_call" | custom-call | flops 5000000000 | bytes 1000000 | tf_op jit(solution)/shard_map/pallas_call | solution.py:555
  46.4 1.5 %shard_map.77 = (f32[304,384]{1,0:T(8,128)S(1)}, f32[416,128]{1,0:T(8,128)S(1)}) custom-call(f32[304,384]{1,0:T(8,128)S(1)} %shard_map.74.refs_0_.before_ref, f32[384,128]{1,0:T(8,128)S(1)} %get-tuple-element.21.after_ref), custom_call_target="tpu_custom_call" | custom-call | flops 4000000000 | bytes 100000 | tf_op jit(solution)/shard_map/pallas_call | solution.py:571
  48.0 1.0 %collective-permute-start.11 = (f32[384,128]{1,0:T(8,128)S(1)}, f32[384,128]{1,0:T(8,128)S(1)}, u32[]{:S(2)}, u32[]{:S(2)}) collective-permute-start(f32[384,128]{1,0:T(8,128)S(1)} %shard_map.79.left_ref), channel_id=1, source_target_pairs={{0,2},{1,5},{2,0},{3,7},{4,6},{5,1},{6,4},{7,3},{8,10},{9,13},{10,... | collective-permute-start | bytes 589832 | tf_op jit(solution)/shard_map/ppermute | solution.py:758
  49.0 3.4 %collective-permute-start.13 = (f32[416,128]{1,0:T(8,128)S(1)}, f32[416,128]{1,0:T(8,128)S(1)}, u32[]{:S(2)}, u32[]{:S(2)}) collective-permute-start(f32[416,128]{1,0:T(8,128)S(1)} %get-tuple-element.26), channel_id=1, source_target_pairs={{0,8},{8,16},{16,24},{1,9},{9,17},{17,25},{2,10},{10,18},{18,26},{... | collective-permute-start | bytes 638984 | tf_op jit(solution)/shard_map/ppermute | solution.py:702
  52.5 1.3 %collective-permute-done.11.right_ref = f32[384,128]{1,0:T(8,128)S(1)} collective-permute-done((f32[384,128]{1,0:T(8,128)S(1)}, f32[384,128]{1,0:T(8,128)S(1)}, u32[]{:S(2)}, u32[]{:S(2)}) %collective-permute-start.11) | collective-permute-done | bytes 196640 | tf_op jit(solution)/shard_map/ppermute | solution.py:758
  53.8 1.6 %collective-permute-start.12 = (f32[384,128]{1,0:T(8,128)S(1)}, f32[384,128]{1,0:T(8,128)S(1)}, u32[]{:S(2)}, u32[]{:S(2)}) collective-permute-start(f32[384,128]{1,0:T(8,128)S(1)} %shard_map.80.left_ref), channel_id=1, source_target_pairs={{0,4},{1,3},{2,6},{3,1},{4,0},{5,7},{6,2},{7,5},{8,12},{9,11},{10,... | collective-permute-start | bytes 589832 | tf_op jit(solution)/shard_map/ppermute | solution.py:759
  55.9 1.5 %shard_map.78 = (bf16[300,1280]{1,0:T(8,128)(2,1)}, f32[8,128]{1,0:T(8,128)S(1)}) custom-call(f32[304,384]{1,0:T(8,128)S(1)} %get-tuple-element.22.inverse_ref.refs_0_, bf16[300,1280]{1,0:T(8,128)(2,1)S(1)} %get-tuple-element.18.right_ref.y_ref), custom_call_target="tpu_custom_call" | custom-call | flops 100000 | bytes 100000 | tf_op jit(solution)/shard_map/pallas_call | solution.py:628
  57.4 2.1 %collective-permute-done.12.right_ref = f32[384,128]{1,0:T(8,128)S(1)} collective-permute-done((f32[384,128]{1,0:T(8,128)S(1)}, f32[384,128]{1,0:T(8,128)S(1)}, u32[]{:S(2)}, u32[]{:S(2)}) %collective-permute-start.12) | collective-permute-done | bytes 196640 | tf_op jit(solution)/shard_map/ppermute | solution.py:759
  59.6 1.3 %shard_map.82.left_ref = bf16[304,384]{1,0:T(8,128)(2,1)S(1)} custom-call(s32[1]{0:T(128)} %bitcast.core_ref, f32[384,128]{1,0:T(8,128)S(1)} %shard_map.81.mine_ref, f32[304,384]{1,0:T(8,128)S(1)} %get-tuple-element.22.inverse_ref.refs_0_, f32[416,128]{1,0:T(8,128)S(1)} %collective-permute-done.13.previous_ref), custom_call_target="tpu_custom_call" | custom-call | flops 100000 | bytes 100000 | tf_op jit(solution)/shard_map/pallas_call | solution.py:662
  61.5 1.0 %collective-permute-done.16.other_ref = bf16[384,128]{1,0:T(8,128)(2,1)S(1)} collective-permute-done((bf16[384,128]{1,0:T(8,128)(2,1)S(1)}, bf16[384,128]{1,0:T(8,128)(2,1)S(1)}, u32[]{:S(2)}, u32[]{:S(2)}) %collective-permute-start.16) | collective-permute-done | bytes 98336 | tf_op jit(solution)/shard_map/ppermute | solution.py:706
  62.5 1.1 %shard_map.84 = (f32[300,1,300]{2,1,0:T(1,128)}, f32[300,1,300]{2,1,0:T(1,128)}) custom-call(s32[1]{0:T(128)} %bitcast.core_ref, bf16[304,384]{1,0:T(8,128)(2,1)S(1)} %shard_map.82.left_ref, bf16[304,384]{1,0:T(8,128)(2,1)S(1)} %collective-permute-done.14.right_ref, bf16[384,128]{1,0:T(8,128)(2,1)S(1)} %shard_map.83.mine_ref, ...), custom_call_target="tpu_custom_call" | custom-call | flops 100000 | bytes 100000 | tf_op jit(solution)/shard_map/pallas_call | solution.py:688
  (35 shorter events, 4.9 us)
Async XLA Ops:
  0.6 9.3 %copy-start = (bf16[1,1280,300]{1,2,0:T(8,128)(2,1)S(1)}, bf16[1,1280,300]{1,2,0:T(8,128)(2,1)}, u32[]{:S(2)}) copy-start(bf16[1,1280,300]{1,2,0:T(8,128)(2,1)} %param.4) | copy-start | bytes 2304004
  0.6 13.0 %collective-permute-start = (bf16[300,1280]{1,0:T(8,128)(2,1)}, bf16[300,1280]{1,0:T(8,128)(2,1)S(1)}, u32[]{:S(2)}, u32[]{:S(2)}) collective-permute-start(bf16[300,1280]{1,0:T(8,128)(2,1)} %bitcast.14), channel_id=1, source_target_pairs={{1,0},{2,1},{3,2},{4,3},{5,4},{6,5},{7,6},{9,8},{10,9},{11,10},{12... | collective-permute-start | bytes 2304008 | tf_op jit(solution)/shard_map/ppermute | solution.py:702
  2.1 0.7 %copy-start.1 = (s32[1,2,10,10]{3,1,2,0:T(2,128)S(1)}, s32[1,2,10,10]{3,1,2,0:T(2,128)}, u32[]{:S(2)}) copy-start(s32[1,2,10,10]{3,1,2,0:T(2,128)} %param.7) | copy-start | bytes 2404
  2.8 7.1 %copy-start.2 = (s32[1,2,10,10]{3,1,2,0:T(2,128)S(1)}, s32[1,2,10,10]{3,1,2,0:T(2,128)}, u32[]{:S(2)}) copy-start(s32[1,2,10,10]{3,1,2,0:T(2,128)} %param.7) | copy-start | bytes 2404
  6.8 10.1 %collective-permute-start.1 = (bf16[300,1280]{1,0:T(8,128)(2,1)S(1)}, bf16[300,1280]{1,0:T(8,128)(2,1)S(1)}, u32[]{:S(2)}, u32[]{:S(2)}) collective-permute-start(bf16[300,1280]{1,0:T(8,128)(2,1)S(1)} %shard_map.69), channel_id=1, source_target_pairs={{0,1},{1,2},{2,3},{3,4},{4,5},{5,6},{6,7},{8,9},{9,10},{10,11},{11... | collective-permute-start | bytes 2304008 | tf_op jit(solution)/shard_map/ppermute | solution.py:702
  17.4 7.9 %collective-permute-start.2 = (f32[208,128]{1,0:T(8,128)S(1)}, f32[208,128]{1,0:T(8,128)S(1)}, u32[]{:S(2)}, u32[]{:S(2)}) collective-permute-start(f32[208,128]{1,0:T(8,128)S(1)} %get-tuple-element.17), channel_id=1, source_target_pairs={{0,1},{1,0},{2,3},{3,2},{4,5},{5,4},{6,7},{7,6},{8,9},{9,8},{10,11... | collective-permute-start | bytes 319496 | tf_op jit(solution)/shard_map/ppermute | solution.py:706
  21.8 23.3 %collective-permute-start.8 = (bf16[300,1280]{1,0:T(8,128)(2,1)S(1)}, bf16[300,1280]{1,0:T(8,128)(2,1)S(1)}, u32[]{:S(2)}, u32[]{:S(2)}) collective-permute-start(bf16[300,1280]{1,0:T(8,128)(2,1)S(1)} %get-tuple-element.18.right_ref.y_ref), channel_id=1, source_target_pairs={{0,8},{8,16},{16,24},{1,9},{9,17},{17,25},{2,10},{10,18},{18,26},{... | collective-permute-start | bytes 2304008 | tf_op jit(solution)/shard_map/ppermute | solution.py:702
  25.4 8.1 %collective-permute-start.3 = (f32[208,128]{1,0:T(8,128)S(1)}, f32[208,128]{1,0:T(8,128)S(1)}, u32[]{:S(2)}, u32[]{:S(2)}) collective-permute-start(f32[208,128]{1,0:T(8,128)S(1)} %add.8.after_ref.own_ref), channel_id=1, source_target_pairs={{0,2},{1,3},{2,0},{3,1},{4,6},{5,7},{6,4},{7,5},{8,10},{9,11},{10,... | collective-permute-start | bytes 319496 | tf_op jit(solution)/shard_map/ppermute | solution.py:724
  28.0 7.9 %collective-permute-start.4 = (f32[208,128]{1,0:T(8,128)S(1)}, f32[208,128]{1,0:T(8,128)S(1)}, u32[]{:S(2)}, u32[]{:S(2)}) collective-permute-start(f32[208,128]{1,0:T(8,128)S(1)} %add.8.after_ref.own_ref), channel_id=1, source_target_pairs={{0,4},{1,5},{2,6},{3,7},{4,0},{5,1},{6,2},{7,3},{8,12},{9,13},{10,... | collective-permute-start | bytes 319496 | tf_op jit(solution)/shard_map/ppermute | solution.py:724
  31.2 5.6 %collective-permute-start.5 = (f32[208,128]{1,0:T(8,128)S(1)}, f32[208,128]{1,0:T(8,128)S(1)}, u32[]{:S(2)}, u32[]{:S(2)}) collective-permute-start(f32[208,128]{1,0:T(8,128)S(1)} %add.8.after_ref.own_ref), channel_id=1, source_target_pairs={{0,6},{1,7},{2,4},{3,5},{4,2},{5,3},{6,0},{7,1},{8,14},{9,15},{10,... | collective-permute-start | bytes 319496 | tf_op jit(solution)/shard_map/ppermute | solution.py:724
  32.1 1.4 %collective-permute-start.6 = (bf16[384,128]{1,0:T(8,128)(2,1)S(1)}, bf16[384,128]{1,0:T(8,128)(2,1)S(1)}, u32[]{:S(2)}, u32[]{:S(2)}) collective-permute-start(bf16[384,128]{1,0:T(8,128)(2,1)S(1)} %get-tuple-element.20), channel_id=1, source_target_pairs={{0,1},{1,0},{2,3},{3,2},{4,5},{5,4},{6,7},{7,6},{8,9},{9,8},{10,11... | collective-permute-start | bytes 294920 | tf_op jit(solution)/shard_map/ppermute | solution.py:706
  36.9 1.4 %collective-permute-start.7 = (f32[208,128]{1,0:T(8,128)S(1)}, f32[208,128]{1,0:T(8,128)S(1)}, u32[]{:S(2)}, u32[]{:S(2)}) collective-permute-start(f32[208,128]{1,0:T(8,128)S(1)} %shard_map.73.mine_ref), channel_id=1, source_target_pairs={{0,1},{1,0},{2,3},{3,2},{4,5},{5,4},{6,7},{7,6},{8,9},{9,8},{10,11... | collective-permute-start | bytes 319496 | tf_op jit(solution)/shard_map/ppermute | solution.py:706
  37.0 8.1 %collective-permute-start.9 = (bf16[384,128]{1,0:T(8,128)(2,1)S(1)}, bf16[384,128]{1,0:T(8,128)(2,1)S(1)}, u32[]{:S(2)}, u32[]{:S(2)}) collective-permute-start(bf16[384,128]{1,0:T(8,128)(2,1)S(1)} %shard_map.72.after_ref.left_ref), channel_id=1, source_target_pairs={{0,2},{1,5},{2,0},{3,7},{4,6},{5,1},{6,4},{7,3},{8,10},{9,13},{10,... | collective-permute-start | bytes 294920 | tf_op jit(solution)/shard_map/ppermute | solution.py:749
  46.0 2.0 %collective-permute-start.10 = (f32[384,128]{1,0:T(8,128)S(1)}, f32[384,128]{1,0:T(8,128)S(1)}, u32[]{:S(2)}, u32[]{:S(2)}) collective-permute-start(f32[384,128]{1,0:T(8,128)S(1)} %get-tuple-element.21.after_ref), channel_id=1, source_target_pairs={{0,1},{1,0},{2,3},{3,2},{4,5},{5,4},{6,7},{7,6},{8,9},{9,8},{10,11... | collective-permute-start | bytes 589832 | tf_op jit(solution)/shard_map/ppermute | solution.py:706
  48.0 5.7 %collective-permute-start.11 = (f32[384,128]{1,0:T(8,128)S(1)}, f32[384,128]{1,0:T(8,128)S(1)}, u32[]{:S(2)}, u32[]{:S(2)}) collective-permute-start(f32[384,128]{1,0:T(8,128)S(1)} %shard_map.79.left_ref), channel_id=1, source_target_pairs={{0,2},{1,5},{2,0},{3,7},{4,6},{5,1},{6,4},{7,3},{8,10},{9,13},{10,... | collective-permute-start | bytes 589832 | tf_op jit(solution)/shard_map/ppermute | solution.py:758
  49.0 10.5 %collective-permute-start.13 = (f32[416,128]{1,0:T(8,128)S(1)}, f32[416,128]{1,0:T(8,128)S(1)}, u32[]{:S(2)}, u32[]{:S(2)}) collective-permute-start(f32[416,128]{1,0:T(8,128)S(1)} %get-tuple-element.26), channel_id=1, source_target_pairs={{0,8},{8,16},{16,24},{1,9},{9,17},{17,25},{2,10},{10,18},{18,26},{... | collective-permute-start | bytes 638984 | tf_op jit(solution)/shard_map/ppermute | solution.py:702
  53.8 5.7 %collective-permute-start.12 = (f32[384,128]{1,0:T(8,128)S(1)}, f32[384,128]{1,0:T(8,128)S(1)}, u32[]{:S(2)}, u32[]{:S(2)}) collective-permute-start(f32[384,128]{1,0:T(8,128)S(1)} %shard_map.80.left_ref), channel_id=1, source_target_pairs={{0,4},{1,3},{2,6},{3,1},{4,0},{5,7},{6,2},{7,5},{8,12},{9,11},{10,... | collective-permute-start | bytes 589832 | tf_op jit(solution)/shard_map/ppermute | solution.py:759
  55.4 5.5 %collective-permute-start.15 = (bf16[384,128]{1,0:T(8,128)(2,1)S(1)}, bf16[384,128]{1,0:T(8,128)(2,1)S(1)}, u32[]{:S(2)}, u32[]{:S(2)}) collective-permute-start(bf16[384,128]{1,0:T(8,128)(2,1)S(1)} %shard_map.75.after_ref.left_ref), channel_id=1, source_target_pairs={{0,4},{1,3},{2,6},{3,1},{4,0},{5,7},{6,2},{7,5},{8,12},{9,11},{10,... | collective-permute-start | bytes 294920 | tf_op jit(solution)/shard_map/ppermute | solution.py:762
  60.8 1.7 %collective-permute-start.14 = (bf16[304,384]{1,0:T(8,128)(2,1)S(1)}, bf16[304,384]{1,0:T(8,128)(2,1)S(1)}, u32[]{:S(2)}, u32[]{:S(2)}) collective-permute-start(bf16[304,384]{1,0:T(8,128)(2,1)S(1)} %shard_map.82.left_ref), channel_id=1, source_target_pairs={{0,1},{1,0},{2,3},{3,2},{4,5},{5,4},{6,7},{7,6},{8,9},{9,8},{10,11... | collective-permute-start | bytes 700424 | tf_op jit(solution)/shard_map/ppermute | solution.py:706
  61.0 1.6 %collective-permute-start.16 = (bf16[384,128]{1,0:T(8,128)(2,1)S(1)}, bf16[384,128]{1,0:T(8,128)(2,1)S(1)}, u32[]{:S(2)}, u32[]{:S(2)}) collective-permute-start(bf16[384,128]{1,0:T(8,128)(2,1)S(1)} %shard_map.83.mine_ref), channel_id=1, source_target_pairs={{0,1},{1,0},{2,3},{3,2},{4,5},{5,4},{6,7},{7,6},{8,9},{9,8},{10,11... | collective-permute-start | bytes 294920 | tf_op jit(solution)/shard_map/ppermute | solution.py:706

commit v5 on v4

--- a/solution.py
+++ b/solution.py
@@ -76,8 +76,6 @@
     rows = tile_ref.shape[0]
     for n, (start, size) in enumerate(halves(rows)):
         copies[n].wait()
-        if n + 1 < len(copies):
-            copies[n + 1].start()
         mask_rows(tile_ref, mask, start, size)
         last = n + 1 == len(copies)
         for col, cols in strips(rows, 2 * SUBBLOCK):
@@ -99,8 +97,9 @@
     rows = tile_ref.shape[0]
     copies = copies_of(tile_hbm, tile_ref, sems)
     copy_x = pltpu.make_async_copy(x_hbm, x_ref, x_sem)
-    copies[0].start()
     copy_x.start()
+    for copy in copies:
+        copy.start()
     mask = block_mask(mask_ref, which, rows, tile_ref.dtype)
     copy_x.wait()
     product(x_ref, tile_ref, copies, mask, sum_ref, out_ref)
@@ -169,8 +168,8 @@
     return round_up(whole * rows + rest * (wide // LANES), 4 * PANEL)
 
 
-def lower_products(ref, out_ref):
-    channels = ref.shape[0]
+def lower_products(left_ref, right_ref, out_ref):
+    channels = left_ref.shape[0]
     rows = round_up(channels, PANEL)
     offset = 0
     for start, size in strips(channels, LANES):
@@ -182,7 +181,7 @@
                 (rows - channels, LANES), jnp.float32
             )
         out_ref[offset : offset + channels - start, 0:size] = dot(
-            ref[start:channels, :], ref[start : start + size, :], ((1,), (1,))
+            left_ref[start:channels, :], right_ref[start : start + size, :], ((1,), (1,))
         )
         offset += tall
 
@@ -294,7 +293,7 @@
 def gram_kernel(core_ref, part_ref, carried_ref, y_ref, g_mine, g_other, gram_ref, folded_ref):
     image = part_ref[...] + carried_ref[...].astype(jnp.float32)
     y_ref[...] = image.astype(y_ref.dtype)
-    lower_products(y_ref, gram_ref)
+    lower_products(y_ref, y_ref, gram_ref)
     fold(gram_ref, folded_ref, y_ref.shape[0], True)
     cut(folded_ref, core_ref[0], g_mine, g_other)
 
@@ -315,6 +314,47 @@
         compiler_params=params(),
         cost_estimate=cost(2 * channels * channels * rows, 8 * channels * rows),
     )(core, part, carried)
+
+
+def symmetric_matrix(pack_ref, out_ref):
+    rows, wide = out_ref.shape
+    offset = 0
+    for top in range(0, wide, LANES):
+        size = min(LANES, rows - top)
+        column = pack_ref[offset : offset + rows - top, :]
+        offset += rows - top
+        out_ref[top:rows, top : top + LANES] = column
+        for below in range(top + LANES, wide, LANES):
+            count = min(LANES, rows - below)
+            block = column[below - top : below - top + count, :]
+            if count < LANES:
+                block = jnp.concatenate(
+                    [block, jnp.zeros((LANES - count, LANES), block.dtype)], axis=0
+                )
+            out_ref[top : top + size, below : below + LANES] = block.T
+
+
+def ray_kernel(core_ref, x_ref, y_ref, after_ref, mine_ref, other_ref, pack_ref, folded_ref):
+    lower_products(x_ref, y_ref, pack_ref)
+    fold(pack_ref, folded_ref, x_ref.shape[0], True)
+    cut(folded_ref, core_ref[0], mine_ref, other_ref)
+
+
+def ray(core, x_t, y_t, after):
+    channels, rows = x_t.shape
+    lower, folded = lower_rows(channels), folded_rows(channels)
+    return pl.pallas_call(
+        ray_kernel,
+        in_specs=[SCALARS, WHOLE, WHOLE, ANYWHERE],
+        out_specs=[WHOLE] * 2,
+        out_shape=[jax.ShapeDtypeStruct((folded // 2, LANES), jnp.bfloat16)] * 2,
+        scratch_shapes=[
+            pltpu.VMEM((lower, LANES), jnp.float32),
+            pltpu.VMEM((folded, LANES), jnp.float32),
+        ],
+        compiler_params=params(),
+        cost_estimate=cost(2 * channels * channels * rows, 4 * channels * rows),
+    )(core, x_t, y_t, after)
 
 
 def cross_kernel(core_ref, left_ref, right_ref, after_ref, mine_ref, other_ref, pack_ref):
@@ -591,13 +631,11 @@
 
 
 def dot3(left, right, dims):
+    rows = left.shape[0]
     left_high, left_low = split2(left)
     right_high, right_low = split2(right)
-    return (
-        dot(left_high, right_high, dims)
-        + dot(left_high, right_low, dims)
-        + dot(left_low, right_high, dims)
-    )
+    both = dot(jnp.concatenate([left_high, left_low], axis=0), right_high, dims)
+    return both[0:rows, :] + both[rows:, :] + dot(left_high, right_low, dims)
 
 
 def lower_matrix(pack_ref, out_ref):
@@ -675,11 +713,15 @@
 
 
 def both_kernel(
-    scale, core_ref, left_ref, right_ref, mine_ref, other_ref, out_ref, ray_ref, pack_ref
+    scale, core_ref, left_ref, right_ref, mine_ref, other_ref, out_ref, ray_ref,
+    folded_ref, pack_ref, full_ref,
 ):
     channels = out_ref.shape[0]
-    join(pack_ref, core_ref[0], mine_ref[...].astype(jnp.float32), other_ref[...].astype(jnp.float32))
-    ray_ref[:, 0, :] = full_matrix(pack_ref, channels)[0:channels, 0:channels] * scale
+    mine, other = mine_ref[...].astype(jnp.float32), other_ref[...].astype(jnp.float32)
+    join(folded_ref, core_ref[0], mine, other)
+    unfold(folded_ref, pack_ref, channels, True)
+    symmetric_matrix(pack_ref, full_ref)
+    ray_ref[:, 0, :] = full_ref[0:channels, 0:channels] * scale
     total = left_ref[...].astype(jnp.float32) + right_ref[...].astype(jnp.float32)
     out_ref[:, 0, :] = total[0:channels, 0:channels]
 
@@ -690,7 +732,11 @@
         in_specs=[SCALARS] + [WHOLE] * 4,
         out_specs=[WHOLE] * 2,
         out_shape=[matrix_shape(channels)] * 2,
-        scratch_shapes=[pltpu.VMEM((full_rows(channels), LANES), jnp.float32)],
+        scratch_shapes=[
+            pltpu.VMEM((folded_rows(channels), LANES), jnp.float32),
+            pltpu.VMEM((lower_rows(channels), LANES), jnp.float32),
+            pltpu.VMEM((round_up(channels, PANEL), round_up(channels, LANES)), jnp.float32),
+        ],
         compiler_params=params(),
         cost_estimate=cost(10**5, 10**5),
     )(core, left, right, mine, other)
@@ -743,7 +789,7 @@
     previous_y = from_behind(y_t, "sector", 1)
     rounds = chip_rounds()
     g_sum = g_mine + other_core(g_other)
-    r_mine, r_other = cross(core, x_t, y_t, g_sum, jnp.bfloat16)
+    r_mine, r_other = ray(core, x_t, y_t, g_sum)
     r_sum = add_after(r_mine, other_core(r_other))
     g_sum = sum_chips(g_sum, r_sum)
     r_first = lax.ppermute(r_sum, "rows", rounds[0])

time: 64.1 us -> 63.9 us (level)
  Pallas kernels: 25.6 us -> 23.9 us
  starting transfers between devices: 27.3 us -> 28.7 us
    pallas_call x2, Pallas kernels: 7.78 us -> 6.41 us  [tile_product(): pl.pallas_call(functools.partial(tile_kernel, which), in_specs=[WHOLE, AN...]
    ppermute x3, starting transfers between devices: 5.86 us -> 6.72 us  [sum_chips(): lax.ppermute(value, 'rows', [(s, s ^ bits) for s in range(count)])]
    pallas_call x2 -> x1, Pallas kernels: 1.6 us -> 0.8 us  [cross(): pl.pallas_call(cross_kernel, in_specs=[SCALARS, WHOLE, WHOLE, ANYWHERE],...]
  transfers between devices with their start and end apart: 17 -> 17, of which waited for: 6 -> 6; matrix products, arithmetic and copies ran while one was open for 0% -> 0% of each run, Pallas kernels for 36% -> 34%
where the time goes in v5:
time: 63.9 us; the launch traced here: 63.6 us
  starting transfers between devices  28.7 us (45%)
  Pallas kernels  23.9 us (37%)
  waiting for transfers between devices  9.36 us (15%)
  between operations  0.91 us (1%)
  local copies, waits for them, and re-layouts  0.7 us (1%)
    ppermute x4, starting transfers between devices, from_behind(): lax.ppermute(value, axis, [(source, source + steps) for source in range(l...  11.5 us
    pallas_call x1, Pallas kernels, first_stage(): pl.pallas_call(functools.partial(first_stage_kernel, channels, 1.0 / tota...  6.82 us
    ppermute x3, starting transfers between devices, sum_chips(): lax.ppermute(value, 'rows', [(s, s ^ bits) for s in range(count)])  6.72 us
    pallas_call x2, Pallas kernels, tile_product(): pl.pallas_call(functools.partial(tile_kernel, which), in_specs=[WHOLE, AN...  6.41 us
    ppermute x6, starting transfers between devices, other_core(): lax.ppermute(value, 'rows', [(s, s ^ 1) for s in range(lax.axis_size('row...  6.14 us
    ppermute x3, waiting for transfers between devices, sum_chips(): lax.ppermute(value, 'rows', [(s, s ^ bits) for s in range(count)])  3.71 us
    pallas_call x1, Pallas kernels, later_product(): pl.pallas_call(later_kernel, in_specs=[WHOLE, WHOLE, ANYWHERE, WHOLE], ou...  3.15 us
    ppermute x6, waiting for transfers between devices, other_core(): lax.ppermute(value, 'rows', [(s, s ^ 1) for s in range(lax.axis_size('row...  2.24 us
  transfers between devices with their start and end apart: 17, of which 6 were waited for; matrix products, arithmetic and copies ran while one was open for 0% of the time, Pallas kernels for 34%

profile of v5, /device:TPU:0, one launch (start us, length us, event | category | flops | bytes accessed | tf_op | source)
XLA Modules:
  0.0 63.6 jit_solution(14399672176530204424)
XLA Ops:
  0.6 1.4 %collective-permute-start = (bf16[300,1280]{1,0:T(8,128)(2,1)}, bf16[300,1280]{1,0:T(8,128)(2,1)S(1)}, u32[]{:S(2)}, u32[]{:S(2)}) collective-permute-start(bf16[300,1280]{1,0:T(8,128)(2,1)} %bitcast.14), channel_id=1, source_target_pairs={{1,0},{2,1},{3,2},{4,3},{5,4},{6,5},{7,6},{9,8},{10,9},{11,10},{12... | collective-permute-start | bytes 2304008 | tf_op jit(solution)/shard_map/ppermute | solution.py:748
  2.8 3.1 %shard_map.69 = bf16[300,1280]{1,0:T(8,128)(2,1)S(1)} custom-call(s32[10,2,10]{2,1,0:T(2,128)S(1)} %bitcast.18, bf16[300,1280]{1,0:T(8,128)(2,1)} %bitcast.15, bf16[1280,1280]{1,0:T(8,128)(2,1)} %bitcast.21), custom_call_target="tpu_custom_call" | custom-call | flops 983040000 | bytes 3276800 | tf_op jit(solution)/shard_map/pallas_call | solution.py:110
  5.9 3.1 %collective-permute-start.1 = (bf16[300,1280]{1,0:T(8,128)(2,1)S(1)}, bf16[300,1280]{1,0:T(8,128)(2,1)S(1)}, u32[]{:S(2)}, u32[]{:S(2)}) collective-permute-start(bf16[300,1280]{1,0:T(8,128)(2,1)S(1)} %shard_map.69), channel_id=1, source_target_pairs={{0,1},{1,2},{2,3},{3,4},{4,5},{5,6},{6,7},{8,9},{9,10},{10,11},{11... | collective-permute-start | bytes 2304008 | tf_op jit(solution)/shard_map/ppermute | solution.py:748
  9.0 3.3 %shard_map.67.first_ref = f32[300,1280]{1,0:T(8,128)S(1)} custom-call(s32[10,2,10]{2,1,0:T(2,128)S(1)} %bitcast.19, bf16[300,1280]{1,0:T(8,128)(2,1)S(1)} %bitcast.16, bf16[1280,1280]{1,0:T(8,128)(2,1)} %bitcast.23), custom_call_target="tpu_custom_call" | custom-call | flops 983040000 | bytes 3276800 | tf_op jit(solution)/shard_map/pallas_call | solution.py:110
  12.3 3.1 %shard_map.68.part_ref = f32[300,1280]{1,0:T(8,128)S(1)} custom-call(s32[10,2,10]{2,1,0:T(2,128)S(1)} %bitcast.20, bf16[300,1280]{1,0:T(8,128)(2,1)S(1)} %collective-permute-done.later_ref, bf16[1280,1280]{1,0:T(8,128)(2,1)} %bitcast.22, f32[300,1280]{1,0:T(8,128)S(1)} %shard_map.67.first_ref), custom_call_target="tpu_custom_call" | custom-call | flops 983040000 | bytes 3276800 | tf_op jit(solution)/shard_map/pallas_call | solution.py:145
  16.1 4.9 %collective-permute-start.2 = (f32[208,128]{1,0:T(8,128)S(1)}, f32[208,128]{1,0:T(8,128)S(1)}, u32[]{:S(2)}, u32[]{:S(2)}) collective-permute-start(f32[208,128]{1,0:T(8,128)S(1)} %get-tuple-element.17), channel_id=1, source_target_pairs={{0,1},{1,0},{2,3},{3,2},{4,5},{5,4},{6,7},{7,6},{8,9},{9,8},{10,11... | collective-permute-start | bytes 319496 | tf_op jit(solution)/shard_map/ppermute | solution.py:752
  21.0 3.5 %collective-permute-start.8 = (bf16[300,1280]{1,0:T(8,128)(2,1)S(1)}, bf16[300,1280]{1,0:T(8,128)(2,1)S(1)}, u32[]{:S(2)}, u32[]{:S(2)}) collective-permute-start(bf16[300,1280]{1,0:T(8,128)(2,1)S(1)} %get-tuple-element.18.y_ref.right_ref), channel_id=1, source_target_pairs={{0,8},{8,16},{16,24},{1,9},{9,17},{17,25},{2,10},{10,18},{18,26},{... | collective-permute-start | bytes 2304008 | tf_op jit(solution)/shard_map/ppermute | solution.py:748
  24.5 3.4 %collective-permute-start.3 = (f32[208,128]{1,0:T(8,128)S(1)}, f32[208,128]{1,0:T(8,128)S(1)}, u32[]{:S(2)}, u32[]{:S(2)}) collective-permute-start(f32[208,128]{1,0:T(8,128)S(1)} %add.8.after_ref.own_ref), channel_id=1, source_target_pairs={{0,2},{1,3},{2,0},{3,1},{4,6},{5,7},{6,4},{7,5},{8,10},{9,11},{10,... | collective-permute-start | bytes 319496 | tf_op jit(solution)/shard_map/ppermute | solution.py:770
  28.0 3.3 %collective-permute-start.4 = (f32[208,128]{1,0:T(8,128)S(1)}, f32[208,128]{1,0:T(8,128)S(1)}, u32[]{:S(2)}, u32[]{:S(2)}) collective-permute-start(f32[208,128]{1,0:T(8,128)S(1)} %add.8.after_ref.own_ref), channel_id=1, source_target_pairs={{0,4},{1,5},{2,6},{3,7},{4,0},{5,1},{6,2},{7,3},{8,12},{9,13},{10,... | collective-permute-start | bytes 319496 | tf_op jit(solution)/shard_map/ppermute | solution.py:770
  31.9 1.2 %collective-permute-done.6.right_ref = bf16[208,128]{1,0:T(8,128)(2,1)S(1)} collective-permute-done((bf16[208,128]{1,0:T(8,128)(2,1)S(1)}, bf16[208,128]{1,0:T(8,128)(2,1)S(1)}, u32[]{:S(2)}, u32[]{:S(2)}) %collective-permute-start.6) | collective-permute-done | bytes 53280 | tf_op jit(solution)/shard_map/ppermute | solution.py:752
  33.1 2.7 %collective-permute-done.4.second_ref = f32[208,128]{1,0:T(8,128)S(1)} collective-permute-done((f32[208,128]{1,0:T(8,128)S(1)}, f32[208,128]{1,0:T(8,128)S(1)}, u32[]{:S(2)}, u32[]{:S(2)}) %collective-permute-start.4) | collective-permute-done | bytes 106528 | tf_op jit(solution)/shard_map/ppermute | solution.py:770
  35.8 1.0 %collective-permute-done.5.both_ref = f32[208,128]{1,0:T(8,128)S(1)} collective-permute-done((f32[208,128]{1,0:T(8,128)S(1)}, f32[208,128]{1,0:T(8,128)S(1)}, u32[]{:S(2)}, u32[]{:S(2)}) %collective-permute-start.5) | collective-permute-done | bytes 106528 | tf_op jit(solution)/shard_map/ppermute | solution.py:770
  37.0 1.3 %collective-permute-start.9 = (bf16[208,128]{1,0:T(8,128)(2,1)S(1)}, bf16[208,128]{1,0:T(8,128)(2,1)S(1)}, u32[]{:S(2)}, u32[]{:S(2)}) collective-permute-start(bf16[208,128]{1,0:T(8,128)(2,1)S(1)} %shard_map.72.after_ref.left_ref), channel_id=1, source_target_pairs={{0,2},{1,5},{2,0},{3,7},{4,6},{5,1},{6,4},{7,3},{8,10},{9,13},{10,... | collective-permute-start | bytes 159752 | tf_op jit(solution)/shard_map/ppermute | solution.py:795
  38.3 6.8 %shard_map.74.refs_0_.before_ref = f32[304,384]{1,0:T(8,128)S(1)} custom-call(s32[1]{0:T(128)} %bitcast.core_ref, f32[208,128]{1,0:T(8,128)S(1)} %shard_map.73.mine_ref, f32[208,128]{1,0:T(8,128)S(1)} %collective-permute-done.7.other_ref), custom_call_target="tpu_custom_call" | custom-call | flops 5000000000 | bytes 1000000 | tf_op jit(solution)/shard_map/pallas_call | solution.py:595
  46.4 1.5 %shard_map.77 = (f32[304,384]{1,0:T(8,128)S(1)}, f32[416,128]{1,0:T(8,128)S(1)}) custom-call(f32[304,384]{1,0:T(8,128)S(1)} %shard_map.74.refs_0_.before_ref, f32[384,128]{1,0:T(8,128)S(1)} %get-tuple-element.21.after_ref), custom_call_target="tpu_custom_call" | custom-call | flops 4000000000 | bytes 100000 | tf_op jit(solution)/shard_map/pallas_call | solution.py:611
  48.0 1.0 %collective-permute-start.11 = (f32[384,128]{1,0:T(8,128)S(1)}, f32[384,128]{1,0:T(8,128)S(1)}, u32[]{:S(2)}, u32[]{:S(2)}) collective-permute-start(f32[384,128]{1,0:T(8,128)S(1)} %shard_map.79.left_ref), channel_id=1, source_target_pairs={{0,2},{1,5},{2,0},{3,7},{4,6},{5,1},{6,4},{7,3},{8,10},{9,13},{10,... | collective-permute-start | bytes 589832 | tf_op jit(solution)/shard_map/ppermute | solution.py:804
  49.0 3.4 %collective-permute-start.13 = (f32[416,128]{1,0:T(8,128)S(1)}, f32[416,128]{1,0:T(8,128)S(1)}, u32[]{:S(2)}, u32[]{:S(2)}) collective-permute-start(f32[416,128]{1,0:T(8,128)S(1)} %get-tuple-element.26), channel_id=1, source_target_pairs={{0,8},{8,16},{16,24},{1,9},{9,17},{17,25},{2,10},{10,18},{18,26},{... | collective-permute-start | bytes 638984 | tf_op jit(solution)/shard_map/ppermute | solution.py:748
  52.5 1.3 %collective-permute-done.11.right_ref = f32[384,128]{1,0:T(8,128)S(1)} collective-permute-done((f32[384,128]{1,0:T(8,128)S(1)}, f32[384,128]{1,0:T(8,128)S(1)}, u32[]{:S(2)}, u32[]{:S(2)}) %collective-permute-start.11) | collective-permute-done | bytes 196640 | tf_op jit(solution)/shard_map/ppermute | solution.py:804
  53.8 1.6 %collective-permute-start.12 = (f32[384,128]{1,0:T(8,128)S(1)}, f32[384,128]{1,0:T(8,128)S(1)}, u32[]{:S(2)}, u32[]{:S(2)}) collective-permute-start(f32[384,128]{1,0:T(8,128)S(1)} %shard_map.80.left_ref), channel_id=1, source_target_pairs={{0,4},{1,3},{2,6},{3,1},{4,0},{5,7},{6,2},{7,5},{8,12},{9,11},{10,... | collective-permute-start | bytes 589832 | tf_op jit(solution)/shard_map/ppermute | solution.py:805
  55.9 1.5 %shard_map.78 = (bf16[300,1280]{1,0:T(8,128)(2,1)}, f32[8,128]{1,0:T(8,128)S(1)}) custom-call(f32[304,384]{1,0:T(8,128)S(1)} %get-tuple-element.22.inverse_ref.refs_0_, bf16[300,1280]{1,0:T(8,128)(2,1)S(1)} %get-tuple-element.18.y_ref.right_ref), custom_call_target="tpu_custom_call" | custom-call | flops 100000 | bytes 100000 | tf_op jit(solution)/shard_map/pallas_call | solution.py:666
  57.4 2.1 %collective-permute-done.12.right_ref = f32[384,128]{1,0:T(8,128)S(1)} collective-permute-done((f32[384,128]{1,0:T(8,128)S(1)}, f32[384,128]{1,0:T(8,128)S(1)}, u32[]{:S(2)}, u32[]{:S(2)}) %collective-permute-start.12) | collective-permute-done | bytes 196640 | tf_op jit(solution)/shard_map/ppermute | solution.py:805
  59.6 1.3 %shard_map.82.left_ref = bf16[304,384]{1,0:T(8,128)(2,1)S(1)} custom-call(s32[1]{0:T(128)} %bitcast.core_ref, f32[384,128]{1,0:T(8,128)S(1)} %shard_map.81.mine_ref, f32[304,384]{1,0:T(8,128)S(1)} %get-tuple-element.22.inverse_ref.refs_0_, f32[416,128]{1,0:T(8,128)S(1)} %collective-permute-done.13.previous_ref), custom_call_target="tpu_custom_call" | custom-call | flops 100000 | bytes 100000 | tf_op jit(solution)/shard_map/pallas_call | solution.py:700
  61.5 1.0 %collective-permute-done.16.other_ref = bf16[208,128]{1,0:T(8,128)(2,1)S(1)} collective-permute-done((bf16[208,128]{1,0:T(8,128)(2,1)S(1)}, bf16[208,128]{1,0:T(8,128)(2,1)S(1)}, u32[]{:S(2)}, u32[]{:S(2)}) %collective-permute-start.16) | collective-permute-done | bytes 53280 | tf_op jit(solution)/shard_map/ppermute | solution.py:752
  62.5 1.2 %shard_map.84 = (f32[300,1,300]{2,1,0:T(1,128)}, f32[300,1,300]{2,1,0:T(1,128)}) custom-call(s32[1]{0:T(128)} %bitcast.core_ref, bf16[304,384]{1,0:T(8,128)(2,1)S(1)} %shard_map.82.left_ref, bf16[304,384]{1,0:T(8,128)(2,1)S(1)} %collective-permute-done.14.right_ref, bf16[208,128]{1,0:T(8,128)(2,1)S(1)} %shard_map.83.mine_ref, ...), custom_call_target="tpu_custom_call" | custom-call | flops 100000 | bytes 100000 | tf_op jit(solution)/shard_map/pallas_call | solution.py:730
  (35 shorter events, 4.6 us)
Async XLA Ops:
  0.6 8.4 %copy-start = (bf16[1,1280,300]{1,2,0:T(8,128)(2,1)S(1)}, bf16[1,1280,300]{1,2,0:T(8,128)(2,1)}, u32[]{:S(2)}) copy-start(bf16[1,1280,300]{1,2,0:T(8,128)(2,1)} %param.4) | copy-start | bytes 2304004
  0.6 11.7 %collective-permute-start = (bf16[300,1280]{1,0:T(8,128)(2,1)}, bf16[300,1280]{1,0:T(8,128)(2,1)S(1)}, u32[]{:S(2)}, u32[]{:S(2)}) collective-permute-start(bf16[300,1280]{1,0:T(8,128)(2,1)} %bitcast.14), channel_id=1, source_target_pairs={{1,0},{2,1},{3,2},{4,3},{5,4},{6,5},{7,6},{9,8},{10,9},{11,10},{12... | collective-permute-start | bytes 2304008 | tf_op jit(solution)/shard_map/ppermute | solution.py:748
  2.1 0.7 %copy-start.1 = (s32[1,2,10,10]{3,1,2,0:T(2,128)S(1)}, s32[1,2,10,10]{3,1,2,0:T(2,128)}, u32[]{:S(2)}) copy-start(s32[1,2,10,10]{3,1,2,0:T(2,128)} %param.7) | copy-start | bytes 2404
  2.8 6.3 %copy-start.2 = (s32[1,2,10,10]{3,1,2,0:T(2,128)S(1)}, s32[1,2,10,10]{3,1,2,0:T(2,128)}, u32[]{:S(2)}) copy-start(s32[1,2,10,10]{3,1,2,0:T(2,128)} %param.7) | copy-start | bytes 2404
  5.9 9.6 %collective-permute-start.1 = (bf16[300,1280]{1,0:T(8,128)(2,1)S(1)}, bf16[300,1280]{1,0:T(8,128)(2,1)S(1)}, u32[]{:S(2)}, u32[]{:S(2)}) collective-permute-start(bf16[300,1280]{1,0:T(8,128)(2,1)S(1)} %shard_map.69), channel_id=1, source_target_pairs={{0,1},{1,2},{2,3},{3,4},{4,5},{5,6},{6,7},{8,9},{9,10},{10,11},{11... | collective-permute-start | bytes 2304008 | tf_op jit(solution)/shard_map/ppermute | solution.py:748
  16.1 8.4 %collective-permute-start.2 = (f32[208,128]{1,0:T(8,128)S(1)}, f32[208,128]{1,0:T(8,128)S(1)}, u32[]{:S(2)}, u32[]{:S(2)}) collective-permute-start(f32[208,128]{1,0:T(8,128)S(1)} %get-tuple-element.17), channel_id=1, source_target_pairs={{0,1},{1,0},{2,3},{3,2},{4,5},{5,4},{6,7},{7,6},{8,9},{9,8},{10,11... | collective-permute-start | bytes 319496 | tf_op jit(solution)/shard_map/ppermute | solution.py:752
  21.0 24.1 %collective-permute-start.8 = (bf16[300,1280]{1,0:T(8,128)(2,1)S(1)}, bf16[300,1280]{1,0:T(8,128)(2,1)S(1)}, u32[]{:S(2)}, u32[]{:S(2)}) collective-permute-start(bf16[300,1280]{1,0:T(8,128)(2,1)S(1)} %get-tuple-element.18.y_ref.right_ref), channel_id=1, source_target_pairs={{0,8},{8,16},{16,24},{1,9},{9,17},{17,25},{2,10},{10,18},{18,26},{... | collective-permute-start | bytes 2304008 | tf_op jit(solution)/shard_map/ppermute | solution.py:748
  24.5 8.6 %collective-permute-start.3 = (f32[208,128]{1,0:T(8,128)S(1)}, f32[208,128]{1,0:T(8,128)S(1)}, u32[]{:S(2)}, u32[]{:S(2)}) collective-permute-start(f32[208,128]{1,0:T(8,128)S(1)} %add.8.after_ref.own_ref), channel_id=1, source_target_pairs={{0,2},{1,3},{2,0},{3,1},{4,6},{5,7},{6,4},{7,5},{8,10},{9,11},{10,... | collective-permute-start | bytes 319496 | tf_op jit(solution)/shard_map/ppermute | solution.py:770
  28.0 7.9 %collective-permute-start.4 = (f32[208,128]{1,0:T(8,128)S(1)}, f32[208,128]{1,0:T(8,128)S(1)}, u32[]{:S(2)}, u32[]{:S(2)}) collective-permute-start(f32[208,128]{1,0:T(8,128)S(1)} %add.8.after_ref.own_ref), channel_id=1, source_target_pairs={{0,4},{1,5},{2,6},{3,7},{4,0},{5,1},{6,2},{7,3},{8,12},{9,13},{10,... | collective-permute-start | bytes 319496 | tf_op jit(solution)/shard_map/ppermute | solution.py:770
  31.2 5.6 %collective-permute-start.5 = (f32[208,128]{1,0:T(8,128)S(1)}, f32[208,128]{1,0:T(8,128)S(1)}, u32[]{:S(2)}, u32[]{:S(2)}) collective-permute-start(f32[208,128]{1,0:T(8,128)S(1)} %add.8.after_ref.own_ref), channel_id=1, source_target_pairs={{0,6},{1,7},{2,4},{3,5},{4,2},{5,3},{6,0},{7,1},{8,14},{9,15},{10,... | collective-permute-start | bytes 319496 | tf_op jit(solution)/shard_map/ppermute | solution.py:770
  31.8 1.3 %collective-permute-start.6 = (bf16[208,128]{1,0:T(8,128)(2,1)S(1)}, bf16[208,128]{1,0:T(8,128)(2,1)S(1)}, u32[]{:S(2)}, u32[]{:S(2)}) collective-permute-start(bf16[208,128]{1,0:T(8,128)(2,1)S(1)} %get-tuple-element.20), channel_id=1, source_target_pairs={{0,1},{1,0},{2,3},{3,2},{4,5},{5,4},{6,7},{7,6},{8,9},{9,8},{10,11... | collective-permute-start | bytes 159752 | tf_op jit(solution)/shard_map/ppermute | solution.py:752
  36.9 1.4 %collective-permute-start.7 = (f32[208,128]{1,0:T(8,128)S(1)}, f32[208,128]{1,0:T(8,128)S(1)}, u32[]{:S(2)}, u32[]{:S(2)}) collective-permute-start(f32[208,128]{1,0:T(8,128)S(1)} %shard_map.73.mine_ref), channel_id=1, source_target_pairs={{0,1},{1,0},{2,3},{3,2},{4,5},{5,4},{6,7},{7,6},{8,9},{9,8},{10,11... | collective-permute-start | bytes 319496 | tf_op jit(solution)/shard_map/ppermute | solution.py:752
  37.0 8.1 %collective-permute-start.9 = (bf16[208,128]{1,0:T(8,128)(2,1)S(1)}, bf16[208,128]{1,0:T(8,128)(2,1)S(1)}, u32[]{:S(2)}, u32[]{:S(2)}) collective-permute-start(bf16[208,128]{1,0:T(8,128)(2,1)S(1)} %shard_map.72.after_ref.left_ref), channel_id=1, source_target_pairs={{0,2},{1,5},{2,0},{3,7},{4,6},{5,1},{6,4},{7,3},{8,10},{9,13},{10,... | collective-permute-start | bytes 159752 | tf_op jit(solution)/shard_map/ppermute | solution.py:795
  45.9 2.0 %collective-permute-start.10 = (f32[384,128]{1,0:T(8,128)S(1)}, f32[384,128]{1,0:T(8,128)S(1)}, u32[]{:S(2)}, u32[]{:S(2)}) collective-permute-start(f32[384,128]{1,0:T(8,128)S(1)} %get-tuple-element.21.after_ref), channel_id=1, source_target_pairs={{0,1},{1,0},{2,3},{3,2},{4,5},{5,4},{6,7},{7,6},{8,9},{9,8},{10,11... | collective-permute-start | bytes 589832 | tf_op jit(solution)/shard_map/ppermute | solution.py:752
  48.0 5.7 %collective-permute-start.11 = (f32[384,128]{1,0:T(8,128)S(1)}, f32[384,128]{1,0:T(8,128)S(1)}, u32[]{:S(2)}, u32[]{:S(2)}) collective-permute-start(f32[384,128]{1,0:T(8,128)S(1)} %shard_map.79.left_ref), channel_id=1, source_target_pairs={{0,2},{1,5},{2,0},{3,7},{4,6},{5,1},{6,4},{7,3},{8,10},{9,13},{10,... | collective-permute-start | bytes 589832 | tf_op jit(solution)/shard_map/ppermute | solution.py:804
  49.0 10.5 %collective-permute-start.13 = (f32[416,128]{1,0:T(8,128)S(1)}, f32[416,128]{1,0:T(8,128)S(1)}, u32[]{:S(2)}, u32[]{:S(2)}) collective-permute-start(f32[416,128]{1,0:T(8,128)S(1)} %get-tuple-element.26), channel_id=1, source_target_pairs={{0,8},{8,16},{16,24},{1,9},{9,17},{17,25},{2,10},{10,18},{18,26},{... | collective-permute-start | bytes 638984 | tf_op jit(solution)/shard_map/ppermute | solution.py:748
  53.8 5.7 %collective-permute-start.12 = (f32[384,128]{1,0:T(8,128)S(1)}, f32[384,128]{1,0:T(8,128)S(1)}, u32[]{:S(2)}, u32[]{:S(2)}) collective-permute-start(f32[384,128]{1,0:T(8,128)S(1)} %shard_map.80.left_ref), channel_id=1, source_target_pairs={{0,4},{1,3},{2,6},{3,1},{4,0},{5,7},{6,2},{7,5},{8,12},{9,11},{10,... | collective-permute-start | bytes 589832 | tf_op jit(solution)/shard_map/ppermute | solution.py:805
  55.4 5.5 %collective-permute-start.15 = (bf16[208,128]{1,0:T(8,128)(2,1)S(1)}, bf16[208,128]{1,0:T(8,128)(2,1)S(1)}, u32[]{:S(2)}, u32[]{:S(2)}) collective-permute-start(bf16[208,128]{1,0:T(8,128)(2,1)S(1)} %shard_map.75.after_ref.left_ref), channel_id=1, source_target_pairs={{0,4},{1,3},{2,6},{3,1},{4,0},{5,7},{6,2},{7,5},{8,12},{9,11},{10,... | collective-permute-start | bytes 159752 | tf_op jit(solution)/shard_map/ppermute | solution.py:808
  60.8 1.6 %collective-permute-start.14 = (bf16[304,384]{1,0:T(8,128)(2,1)S(1)}, bf16[304,384]{1,0:T(8,128)(2,1)S(1)}, u32[]{:S(2)}, u32[]{:S(2)}) collective-permute-start(bf16[304,384]{1,0:T(8,128)(2,1)S(1)} %shard_map.82.left_ref), channel_id=1, source_target_pairs={{0,1},{1,0},{2,3},{3,2},{4,5},{5,4},{6,7},{7,6},{8,9},{9,8},{10,11... | collective-permute-start | bytes 700424 | tf_op jit(solution)/shard_map/ppermute | solution.py:752
  60.9 1.5 %collective-permute-start.16 = (bf16[208,128]{1,0:T(8,128)(2,1)S(1)}, bf16[208,128]{1,0:T(8,128)(2,1)S(1)}, u32[]{:S(2)}, u32[]{:S(2)}) collective-permute-start(bf16[208,128]{1,0:T(8,128)(2,1)S(1)} %shard_map.83.mine_ref), channel_id=1, source_target_pairs={{0,1},{1,0},{2,3},{3,2},{4,5},{5,4},{6,7},{7,6},{8,9},{9,8},{10,11... | collective-permute-start | bytes 159752 | tf_op jit(solution)/shard_map/ppermute | solution.py:752

commit v6 on v5

--- a/solution.py
+++ b/solution.py
@@ -10,7 +10,7 @@
 SUBBLOCK = 128
 LANES = 128
 PANEL = 16
-EARLY_PANELS = 7
+EARLY_PANELS = 8
 WHOLE = pl.BlockSpec(memory_space=pltpu.VMEM)
 SCALARS = pl.BlockSpec(memory_space=pltpu.SMEM)
 ANYWHERE = pl.BlockSpec(memory_space=pl.ANY)
@@ -72,10 +72,12 @@
     return copies
 
 
-def product(x_ref, tile_ref, copies, mask, sum_ref, out_ref):
+def product(x_ref, tile_ref, copies, in_turn, mask, sum_ref, out_ref):
     rows = tile_ref.shape[0]
     for n, (start, size) in enumerate(halves(rows)):
         copies[n].wait()
+        if in_turn and n + 1 < len(copies):
+            copies[n + 1].start()
         mask_rows(tile_ref, mask, start, size)
         last = n + 1 == len(copies)
         for col, cols in strips(rows, 2 * SUBBLOCK):
@@ -93,22 +95,22 @@
                 sum_ref[here] = term
 
 
-def tile_kernel(which, mask_ref, x_hbm, tile_hbm, out_ref, x_ref, tile_ref, sum_ref, x_sem, sems):
+def tile_kernel(which, in_turn, mask_ref, x_hbm, tile_hbm, out_ref, x_ref, tile_ref, sum_ref, x_sem, sems):
     rows = tile_ref.shape[0]
     copies = copies_of(tile_hbm, tile_ref, sems)
     copy_x = pltpu.make_async_copy(x_hbm, x_ref, x_sem)
     copy_x.start()
-    for copy in copies:
+    for copy in copies[:1] if in_turn else copies:
         copy.start()
     mask = block_mask(mask_ref, which, rows, tile_ref.dtype)
     copy_x.wait()
-    product(x_ref, tile_ref, copies, mask, sum_ref, out_ref)
-
-
-def tile_product(which, masks, x_t, tile, dtype, mib):
+    product(x_ref, tile_ref, copies, in_turn, mask, sum_ref, out_ref)
+
+
+def tile_product(which, masks, x_t, tile, dtype, mib, in_turn):
     channels, rows = x_t.shape
     return pl.pallas_call(
-        functools.partial(tile_kernel, which),
+        functools.partial(tile_kernel, which, in_turn),
         in_specs=[WHOLE, ANYWHERE, ANYWHERE],
         out_specs=WHOLE,
         out_shape=jax.ShapeDtypeStruct((channels, rows), dtype),
@@ -381,14 +383,14 @@
     refs[-1][...] = total.astype(refs[-1].dtype)
 
 
-def add_four_kernel(own_ref, first_ref, second_ref, both_ref, after_ref, out_ref):
-    own, first, second, both = (
-        ref[...].astype(jnp.float32) for ref in (own_ref, first_ref, second_ref, both_ref)
+def add_four_kernel(both_ref, own_ref, first_ref, second_ref, after_ref, out_ref):
+    both, own, first, second = (
+        ref[...].astype(jnp.float32) for ref in (both_ref, own_ref, first_ref, second_ref)
     )
     out_ref[...] = ((own + first) + (second + both)).astype(out_ref.dtype)
 
 
-def add_four(own, first, second, both, after):
+def add_four(both, own, first, second, after):
     return pl.pallas_call(
         add_four_kernel,
         in_specs=[WHOLE] * 4 + [ANYWHERE],
@@ -396,7 +398,7 @@
         out_shape=jax.ShapeDtypeStruct(own.shape, own.dtype),
         compiler_params=params(),
         cost_estimate=cost(10**5, 10**5),
-    )(own, first, second, both, after)
+    )(both, own, first, second, after)
 
 
 def add_after(left, right, *after, flops=10**5):
@@ -573,7 +575,7 @@
 ):
     work_ref[...] = before_ref[...]
     rows, wide = work_ref.shape
-    for g in range(1, wide // LANES):
+    for g in range(1 if EARLY_PANELS * PANEL < LANES else 2, wide // LANES):
         eliminate_group(g, work_ref, turned_ref, EARLY_PANELS if g == 1 else 0)
     offset = 0
     for q in range(wide // LANES):
@@ -766,10 +768,10 @@
 def sum_chips(value, after):
     count = lax.axis_size("rows")
     if count == 8:
-        others = [
-            lax.ppermute(value, "rows", [(s, s ^ bits) for s in range(count)]) for bits in (2, 4, 6)
+        both, first, second = [
+            lax.ppermute(value, "rows", [(s, s ^ bits) for s in range(count)]) for bits in (6, 2, 4)
         ]
-        return add_four(value, *others, after)
+        return add_four(both, value, first, second, after)
     for pairs in chip_rounds():
         value = add_after(value, lax.ppermute(value, "rows", pairs), after)
     return value
@@ -782,8 +784,8 @@
     total_rows = lax.axis_size("rows") * block_rows
     core = (lax.axis_index("rows") % 2).astype(jnp.int32).reshape(1)
     later = from_behind(x_t, "rows", -1)
-    carried = from_behind(tile_product(1, masks, x_t, h_right[0], x_t.dtype, 53), "rows", 1)
-    first = tile_product(0, masks, x_t, h_diag[0], jnp.float32, 50)
+    carried = from_behind(tile_product(1, masks, x_t, h_right[0], x_t.dtype, 53, True), "rows", 1)
+    first = tile_product(0, masks, x_t, h_diag[0], jnp.float32, 50, False)
     part = later_product(masks, later, h_right[0], first)
     y_t, g_mine, g_other = gram(core, part, carried)
     previous_y = from_behind(y_t, "sector", 1)

time: 63.9 us -> 63.8 us (level)
  Pallas kernels: 23.9 us -> 24.9 us
    pallas_call x2, Pallas kernels: 6.41 us -> 7.31 us  [tile_product(): pl.pallas_call(functools.partial(tile_kernel, which, in_turn), in_specs=[...]
    ppermute x3, starting transfers between devices: 6.72 us -> 5.89 us  [sum_chips(): lax.ppermute(value, 'rows', [(s, s ^ bits) for s in range(count)])]
  transfers between devices with their start and end apart: 17 -> 17, of which waited for: 6 -> 7; matrix products, arithmetic and copies ran while one was open for 0% -> 0% of each run, Pallas kernels for 34% -> 35%
where the time goes in v6:
time: 63.8 us; the launch traced here: 63.5 us
  starting transfers between devices  28.2 us (44%)
  Pallas kernels  24.9 us (39%)
  waiting for transfers between devices  8.75 us (14%)
  between operations  0.9 us (1%)
  local copies, waits for them, and re-layouts  0.7 us (1%)
    ppermute x4, starting transfers between devices, from_behind(): lax.ppermute(value, axis, [(source, source + steps) for source in range(l...  11.5 us
    pallas_call x2, Pallas kernels, tile_product(): pl.pallas_call(functools.partial(tile_kernel, which, in_turn), in_specs=[...  7.31 us
    pallas_call x1, Pallas kernels, first_stage(): pl.pallas_call(functools.partial(first_stage_kernel, channels, 1.0 / tota...  7.25 us
    ppermute x6, starting transfers between devices, other_core(): lax.ppermute(value, 'rows', [(s, s ^ 1) for s in range(lax.axis_size('row...  5.9 us
    ppermute x3, starting transfers between devices, sum_chips(): lax.ppermute(value, 'rows', [(s, s ^ bits) for s in range(count)])  5.89 us
    ppermute x3, waiting for transfers between devices, sum_chips(): lax.ppermute(value, 'rows', [(s, s ^ bits) for s in range(count)])  3.41 us
    pallas_call x1, Pallas kernels, later_product(): pl.pallas_call(later_kernel, in_specs=[WHOLE, WHOLE, ANYWHERE, WHOLE], ou...  3.14 us
    ppermute x6, waiting for transfers between devices, other_core(): lax.ppermute(value, 'rows', [(s, s ^ 1) for s in range(lax.axis_size('row...  2.33 us
  transfers between devices with their start and end apart: 17, of which 7 were waited for; matrix products, arithmetic and copies ran while one was open for 0% of the time, Pallas kernels for 35%

profile of v6, /device:TPU:0, one launch (start us, length us, event | category | flops | bytes accessed | tf_op | source)
XLA Modules:
  0.0 63.5 jit_solution(13978945236989676217)
XLA Ops:
  0.6 1.4 %collective-permute-start = (bf16[300,1280]{1,0:T(8,128)(2,1)}, bf16[300,1280]{1,0:T(8,128)(2,1)S(1)}, u32[]{:S(2)}, u32[]{:S(2)}) collective-permute-start(bf16[300,1280]{1,0:T(8,128)(2,1)} %bitcast.14), channel_id=1, source_target_pairs={{1,0},{2,1},{3,2},{4,3},{5,4},{6,5},{7,6},{9,8},{10,9},{11,10},{12... | collective-permute-start | bytes 2304008 | tf_op jit(solution)/shard_map/ppermute | solution.py:750
  2.8 4.0 %shard_map.69 = bf16[300,1280]{1,0:T(8,128)(2,1)S(1)} custom-call(s32[10,2,10]{2,1,0:T(2,128)S(1)} %bitcast.18, bf16[300,1280]{1,0:T(8,128)(2,1)} %bitcast.15, bf16[1280,1280]{1,0:T(8,128)(2,1)} %bitcast.21), custom_call_target="tpu_custom_call" | custom-call | flops 983040000 | bytes 3276800 | tf_op jit(solution)/shard_map/pallas_call | solution.py:112
  6.8 3.1 %collective-permute-start.1 = (bf16[300,1280]{1,0:T(8,128)(2,1)S(1)}, bf16[300,1280]{1,0:T(8,128)(2,1)S(1)}, u32[]{:S(2)}, u32[]{:S(2)}) collective-permute-start(bf16[300,1280]{1,0:T(8,128)(2,1)S(1)} %shard_map.69), channel_id=1, source_target_pairs={{0,1},{1,2},{2,3},{3,4},{4,5},{5,6},{6,7},{8,9},{9,10},{10,11},{11... | collective-permute-start | bytes 2304008 | tf_op jit(solution)/shard_map/ppermute | solution.py:750
  9.9 3.3 %shard_map.67.first_ref = f32[300,1280]{1,0:T(8,128)S(1)} custom-call(s32[10,2,10]{2,1,0:T(2,128)S(1)} %bitcast.19, bf16[300,1280]{1,0:T(8,128)(2,1)S(1)} %bitcast.16, bf16[1280,1280]{1,0:T(8,128)(2,1)} %bitcast.23), custom_call_target="tpu_custom_call" | custom-call | flops 983040000 | bytes 3276800 | tf_op jit(solution)/shard_map/pallas_call | solution.py:112
  13.2 3.1 %shard_map.68.part_ref = f32[300,1280]{1,0:T(8,128)S(1)} custom-call(s32[10,2,10]{2,1,0:T(2,128)S(1)} %bitcast.20, bf16[300,1280]{1,0:T(8,128)(2,1)S(1)} %collective-permute-done.later_ref, bf16[1280,1280]{1,0:T(8,128)(2,1)} %bitcast.22, f32[300,1280]{1,0:T(8,128)S(1)} %shard_map.67.first_ref), custom_call_target="tpu_custom_call" | custom-call | flops 983040000 | bytes 3276800 | tf_op jit(solution)/shard_map/pallas_call | solution.py:147
  17.0 4.9 %collective-permute-start.2 = (f32[208,128]{1,0:T(8,128)S(1)}, f32[208,128]{1,0:T(8,128)S(1)}, u32[]{:S(2)}, u32[]{:S(2)}) collective-permute-start(f32[208,128]{1,0:T(8,128)S(1)} %get-tuple-element.17), channel_id=1, source_target_pairs={{0,1},{1,0},{2,3},{3,2},{4,5},{5,4},{6,7},{7,6},{8,9},{9,8},{10,11... | collective-permute-start | bytes 319496 | tf_op jit(solution)/shard_map/ppermute | solution.py:754
  21.9 3.5 %collective-permute-start.8 = (bf16[300,1280]{1,0:T(8,128)(2,1)S(1)}, bf16[300,1280]{1,0:T(8,128)(2,1)S(1)}, u32[]{:S(2)}, u32[]{:S(2)}) collective-permute-start(bf16[300,1280]{1,0:T(8,128)(2,1)S(1)} %get-tuple-element.18.y_ref.right_ref), channel_id=1, source_target_pairs={{0,8},{8,16},{16,24},{1,9},{9,17},{17,25},{2,10},{10,18},{18,26},{... | collective-permute-start | bytes 2304008 | tf_op jit(solution)/shard_map/ppermute | solution.py:750
  25.4 5.3 %collective-permute-start.3 = (f32[208,128]{1,0:T(8,128)S(1)}, f32[208,128]{1,0:T(8,128)S(1)}, u32[]{:S(2)}, u32[]{:S(2)}) collective-permute-start(f32[208,128]{1,0:T(8,128)S(1)} %add.8.after_ref.own_ref), channel_id=1, source_target_pairs={{0,6},{1,7},{2,4},{3,5},{4,2},{5,3},{6,0},{7,1},{8,14},{9,15},{10,... | collective-permute-start | bytes 319496 | tf_op jit(solution)/shard_map/ppermute | solution.py:772
  31.9 1.2 %collective-permute-done.6.right_ref = bf16[208,128]{1,0:T(8,128)(2,1)S(1)} collective-permute-done((bf16[208,128]{1,0:T(8,128)(2,1)S(1)}, bf16[208,128]{1,0:T(8,128)(2,1)S(1)}, u32[]{:S(2)}, u32[]{:S(2)}) %collective-permute-start.6) | collective-permute-done | bytes 53280 | tf_op jit(solution)/shard_map/ppermute | solution.py:754
  33.2 1.2 %collective-permute-done.3.both_ref = f32[208,128]{1,0:T(8,128)S(1)} collective-permute-done((f32[208,128]{1,0:T(8,128)S(1)}, f32[208,128]{1,0:T(8,128)S(1)}, u32[]{:S(2)}, u32[]{:S(2)}) %collective-permute-start.3) | collective-permute-done | bytes 106528 | tf_op jit(solution)/shard_map/ppermute | solution.py:772
  34.4 2.2 %collective-permute-done.4.first_ref = f32[208,128]{1,0:T(8,128)S(1)} collective-permute-done((f32[208,128]{1,0:T(8,128)S(1)}, f32[208,128]{1,0:T(8,128)S(1)}, u32[]{:S(2)}, u32[]{:S(2)}) %collective-permute-start.4) | collective-permute-done | bytes 106528 | tf_op jit(solution)/shard_map/ppermute | solution.py:772
  36.7 1.5 %collective-permute-start.9 = (bf16[208,128]{1,0:T(8,128)(2,1)S(1)}, bf16[208,128]{1,0:T(8,128)(2,1)S(1)}, u32[]{:S(2)}, u32[]{:S(2)}) collective-permute-start(bf16[208,128]{1,0:T(8,128)(2,1)S(1)} %shard_map.72.after_ref.left_ref), channel_id=1, source_target_pairs={{0,2},{1,5},{2,0},{3,7},{4,6},{5,1},{6,4},{7,3},{8,10},{9,13},{10,... | collective-permute-start | bytes 159752 | tf_op jit(solution)/shard_map/ppermute | solution.py:797
  38.2 7.2 %shard_map.74.refs_0_.before_ref = f32[304,384]{1,0:T(8,128)S(1)} custom-call(s32[1]{0:T(128)} %bitcast.core_ref, f32[208,128]{1,0:T(8,128)S(1)} %shard_map.73.mine_ref, f32[208,128]{1,0:T(8,128)S(1)} %collective-permute-done.7.other_ref), custom_call_target="tpu_custom_call" | custom-call | flops 5000000000 | bytes 1000000 | tf_op jit(solution)/shard_map/pallas_call | solution.py:597
  45.5 0.8 %shard_map.76 = (f32[384,128]{1,0:T(8,128)S(1)}, f32[384,128]{1,0:T(8,128)S(1)}) custom-call(s32[1]{0:T(128)} %bitcast.core_ref, bf16[300,1280]{1,0:T(8,128)(2,1)S(1)} %collective-permute-done.8.left_ref, bf16[300,1280]{1,0:T(8,128)(2,1)S(1)} %get-tuple-element.18.y_ref.right_ref, bf16[208,128]{1,0:T(8,128)(2,1)S(1)} %shard_map.75.after_ref.left_ref), custom_call_target="tpu_custom_call" | custom-call | flops 230400000 | bytes 1536000 | tf_op jit(solution)/shard_map/pallas_call | solution.py:370
  46.6 1.1 %shard_map.77 = (f32[304,384]{1,0:T(8,128)S(1)}, f32[416,128]{1,0:T(8,128)S(1)}) custom-call(f32[304,384]{1,0:T(8,128)S(1)} %shard_map.74.refs_0_.before_ref, f32[384,128]{1,0:T(8,128)S(1)} %get-tuple-element.21.after_ref), custom_call_target="tpu_custom_call" | custom-call | flops 4000000000 | bytes 100000 | tf_op jit(solution)/shard_map/pallas_call | solution.py:613
  47.9 1.4 %collective-permute-start.11 = (f32[384,128]{1,0:T(8,128)S(1)}, f32[384,128]{1,0:T(8,128)S(1)}, u32[]{:S(2)}, u32[]{:S(2)}) collective-permute-start(f32[384,128]{1,0:T(8,128)S(1)} %shard_map.79.left_ref), channel_id=1, source_target_pairs={{0,2},{1,5},{2,0},{3,7},{4,6},{5,1},{6,4},{7,3},{8,10},{9,13},{10,... | collective-permute-start | bytes 589832 | tf_op jit(solution)/shard_map/ppermute | solution.py:806
  49.3 3.4 %collective-permute-start.13 = (f32[416,128]{1,0:T(8,128)S(1)}, f32[416,128]{1,0:T(8,128)S(1)}, u32[]{:S(2)}, u32[]{:S(2)}) collective-permute-start(f32[416,128]{1,0:T(8,128)S(1)} %get-tuple-element.26), channel_id=1, source_target_pairs={{0,8},{8,16},{16,24},{1,9},{9,17},{17,25},{2,10},{10,18},{18,26},{... | collective-permute-start | bytes 638984 | tf_op jit(solution)/shard_map/ppermute | solution.py:750
  52.7 0.9 %collective-permute-done.11.right_ref = f32[384,128]{1,0:T(8,128)S(1)} collective-permute-done((f32[384,128]{1,0:T(8,128)S(1)}, f32[384,128]{1,0:T(8,128)S(1)}, u32[]{:S(2)}, u32[]{:S(2)}) %collective-permute-start.11) | collective-permute-done | bytes 196640 | tf_op jit(solution)/shard_map/ppermute | solution.py:806
  53.6 1.6 %collective-permute-start.12 = (f32[384,128]{1,0:T(8,128)S(1)}, f32[384,128]{1,0:T(8,128)S(1)}, u32[]{:S(2)}, u32[]{:S(2)}) collective-permute-start(f32[384,128]{1,0:T(8,128)S(1)} %shard_map.80.left_ref), channel_id=1, source_target_pairs={{0,4},{1,3},{2,6},{3,1},{4,0},{5,7},{6,2},{7,5},{8,12},{9,11},{10,... | collective-permute-start | bytes 589832 | tf_op jit(solution)/shard_map/ppermute | solution.py:807
  55.7 1.5 %shard_map.78 = (bf16[300,1280]{1,0:T(8,128)(2,1)}, f32[8,128]{1,0:T(8,128)S(1)}) custom-call(f32[304,384]{1,0:T(8,128)S(1)} %get-tuple-element.22.inverse_ref.refs_0_, bf16[300,1280]{1,0:T(8,128)(2,1)S(1)} %get-tuple-element.18.y_ref.right_ref), custom_call_target="tpu_custom_call" | custom-call | flops 100000 | bytes 100000 | tf_op jit(solution)/shard_map/pallas_call | solution.py:668
  57.3 2.1 %collective-permute-done.12.right_ref = f32[384,128]{1,0:T(8,128)S(1)} collective-permute-done((f32[384,128]{1,0:T(8,128)S(1)}, f32[384,128]{1,0:T(8,128)S(1)}, u32[]{:S(2)}, u32[]{:S(2)}) %collective-permute-start.12) | collective-permute-done | bytes 196640 | tf_op jit(solution)/shard_map/ppermute | solution.py:807
  59.4 1.3 %shard_map.82.left_ref = bf16[304,384]{1,0:T(8,128)(2,1)S(1)} custom-call(s32[1]{0:T(128)} %bitcast.core_ref, f32[384,128]{1,0:T(8,128)S(1)} %shard_map.81.mine_ref, f32[304,384]{1,0:T(8,128)S(1)} %get-tuple-element.22.inverse_ref.refs_0_, f32[416,128]{1,0:T(8,128)S(1)} %collective-permute-done.13.previous_ref), custom_call_target="tpu_custom_call" | custom-call | flops 100000 | bytes 100000 | tf_op jit(solution)/shard_map/pallas_call | solution.py:702
  61.3 1.0 %collective-permute-done.16.other_ref = bf16[208,128]{1,0:T(8,128)(2,1)S(1)} collective-permute-done((bf16[208,128]{1,0:T(8,128)(2,1)S(1)}, bf16[208,128]{1,0:T(8,128)(2,1)S(1)}, u32[]{:S(2)}, u32[]{:S(2)}) %collective-permute-start.16) | collective-permute-done | bytes 53280 | tf_op jit(solution)/shard_map/ppermute | solution.py:754
  62.3 1.2 %shard_map.84 = (f32[300,1,300]{2,1,0:T(1,128)}, f32[300,1,300]{2,1,0:T(1,128)}) custom-call(s32[1]{0:T(128)} %bitcast.core_ref, bf16[304,384]{1,0:T(8,128)(2,1)S(1)} %shard_map.82.left_ref, bf16[304,384]{1,0:T(8,128)(2,1)S(1)} %collective-permute-done.14.right_ref, bf16[208,128]{1,0:T(8,128)(2,1)S(1)} %shard_map.83.mine_ref, ...), custom_call_target="tpu_custom_call" | custom-call | flops 100000 | bytes 100000 | tf_op jit(solution)/shard_map/pallas_call | solution.py:732
  (35 shorter events, 4.2 us)
Async XLA Ops:
  0.6 9.3 %copy-start = (bf16[1,1280,300]{1,2,0:T(8,128)(2,1)S(1)}, bf16[1,1280,300]{1,2,0:T(8,128)(2,1)}, u32[]{:S(2)}) copy-start(bf16[1,1280,300]{1,2,0:T(8,128)(2,1)} %param.4) | copy-start | bytes 2304004
  0.6 12.6 %collective-permute-start = (bf16[300,1280]{1,0:T(8,128)(2,1)}, bf16[300,1280]{1,0:T(8,128)(2,1)S(1)}, u32[]{:S(2)}, u32[]{:S(2)}) collective-permute-start(bf16[300,1280]{1,0:T(8,128)(2,1)} %bitcast.14), channel_id=1, source_target_pairs={{1,0},{2,1},{3,2},{4,3},{5,4},{6,5},{7,6},{9,8},{10,9},{11,10},{12... | collective-permute-start | bytes 2304008 | tf_op jit(solution)/shard_map/ppermute | solution.py:750
  2.1 0.7 %copy-start.1 = (s32[1,2,10,10]{3,1,2,0:T(2,128)S(1)}, s32[1,2,10,10]{3,1,2,0:T(2,128)}, u32[]{:S(2)}) copy-start(s32[1,2,10,10]{3,1,2,0:T(2,128)} %param.7) | copy-start | bytes 2404
  2.8 7.1 %copy-start.2 = (s32[1,2,10,10]{3,1,2,0:T(2,128)S(1)}, s32[1,2,10,10]{3,1,2,0:T(2,128)}, u32[]{:S(2)}) copy-start(s32[1,2,10,10]{3,1,2,0:T(2,128)} %param.7) | copy-start | bytes 2404
  6.8 9.6 %collective-permute-start.1 = (bf16[300,1280]{1,0:T(8,128)(2,1)S(1)}, bf16[300,1280]{1,0:T(8,128)(2,1)S(1)}, u32[]{:S(2)}, u32[]{:S(2)}) collective-permute-start(bf16[300,1280]{1,0:T(8,128)(2,1)S(1)} %shard_map.69), channel_id=1, source_target_pairs={{0,1},{1,2},{2,3},{3,4},{4,5},{5,6},{6,7},{8,9},{9,10},{10,11},{11... | collective-permute-start | bytes 2304008 | tf_op jit(solution)/shard_map/ppermute | solution.py:750
  17.0 8.4 %collective-permute-start.2 = (f32[208,128]{1,0:T(8,128)S(1)}, f32[208,128]{1,0:T(8,128)S(1)}, u32[]{:S(2)}, u32[]{:S(2)}) collective-permute-start(f32[208,128]{1,0:T(8,128)S(1)} %get-tuple-element.17), channel_id=1, source_target_pairs={{0,1},{1,0},{2,3},{3,2},{4,5},{5,4},{6,7},{7,6},{8,9},{9,8},{10,11... | collective-permute-start | bytes 319496 | tf_op jit(solution)/shard_map/ppermute | solution.py:754
  21.9 23.6 %collective-permute-start.8 = (bf16[300,1280]{1,0:T(8,128)(2,1)S(1)}, bf16[300,1280]{1,0:T(8,128)(2,1)S(1)}, u32[]{:S(2)}, u32[]{:S(2)}) collective-permute-start(bf16[300,1280]{1,0:T(8,128)(2,1)S(1)} %get-tuple-element.18.y_ref.right_ref), channel_id=1, source_target_pairs={{0,8},{8,16},{16,24},{1,9},{9,17},{17,25},{2,10},{10,18},{18,26},{... | collective-permute-start | bytes 2304008 | tf_op jit(solution)/shard_map/ppermute | solution.py:750
  25.4 9.0 %collective-permute-start.3 = (f32[208,128]{1,0:T(8,128)S(1)}, f32[208,128]{1,0:T(8,128)S(1)}, u32[]{:S(2)}, u32[]{:S(2)}) collective-permute-start(f32[208,128]{1,0:T(8,128)S(1)} %add.8.after_ref.own_ref), channel_id=1, source_target_pairs={{0,6},{1,7},{2,4},{3,5},{4,2},{5,3},{6,0},{7,1},{8,14},{9,15},{10,... | collective-permute-start | bytes 319496 | tf_op jit(solution)/shard_map/ppermute | solution.py:772
  30.7 5.9 %collective-permute-start.4 = (f32[208,128]{1,0:T(8,128)S(1)}, f32[208,128]{1,0:T(8,128)S(1)}, u32[]{:S(2)}, u32[]{:S(2)}) collective-permute-start(f32[208,128]{1,0:T(8,128)S(1)} %add.8.after_ref.own_ref), channel_id=1, source_target_pairs={{0,2},{1,3},{2,0},{3,1},{4,6},{5,7},{6,4},{7,5},{8,10},{9,11},{10,... | collective-permute-start | bytes 319496 | tf_op jit(solution)/shard_map/ppermute | solution.py:772
  31.3 5.3 %collective-permute-start.5 = (f32[208,128]{1,0:T(8,128)S(1)}, f32[208,128]{1,0:T(8,128)S(1)}, u32[]{:S(2)}, u32[]{:S(2)}) collective-permute-start(f32[208,128]{1,0:T(8,128)S(1)} %add.8.after_ref.own_ref), channel_id=1, source_target_pairs={{0,4},{1,5},{2,6},{3,7},{4,0},{5,1},{6,2},{7,3},{8,12},{9,13},{10,... | collective-permute-start | bytes 319496 | tf_op jit(solution)/shard_map/ppermute | solution.py:772
  31.9 1.3 %collective-permute-start.6 = (bf16[208,128]{1,0:T(8,128)(2,1)S(1)}, bf16[208,128]{1,0:T(8,128)(2,1)S(1)}, u32[]{:S(2)}, u32[]{:S(2)}) collective-permute-start(bf16[208,128]{1,0:T(8,128)(2,1)S(1)} %get-tuple-element.20), channel_id=1, source_target_pairs={{0,1},{1,0},{2,3},{3,2},{4,5},{5,4},{6,7},{7,6},{8,9},{9,8},{10,11... | collective-permute-start | bytes 159752 | tf_op jit(solution)/shard_map/ppermute | solution.py:754
  36.6 1.6 %collective-permute-start.7 = (f32[208,128]{1,0:T(8,128)S(1)}, f32[208,128]{1,0:T(8,128)S(1)}, u32[]{:S(2)}, u32[]{:S(2)}) collective-permute-start(f32[208,128]{1,0:T(8,128)S(1)} %shard_map.73.mine_ref), channel_id=1, source_target_pairs={{0,1},{1,0},{2,3},{3,2},{4,5},{5,4},{6,7},{7,6},{8,9},{9,8},{10,11... | collective-permute-start | bytes 319496 | tf_op jit(solution)/shard_map/ppermute | solution.py:754
  36.7 8.8 %collective-permute-start.9 = (bf16[208,128]{1,0:T(8,128)(2,1)S(1)}, bf16[208,128]{1,0:T(8,128)(2,1)S(1)}, u32[]{:S(2)}, u32[]{:S(2)}) collective-permute-start(bf16[208,128]{1,0:T(8,128)(2,1)S(1)} %shard_map.72.after_ref.left_ref), channel_id=1, source_target_pairs={{0,2},{1,5},{2,0},{3,7},{4,6},{5,1},{6,4},{7,3},{8,10},{9,13},{10,... | collective-permute-start | bytes 159752 | tf_op jit(solution)/shard_map/ppermute | solution.py:797
  46.3 1.5 %collective-permute-start.10 = (f32[384,128]{1,0:T(8,128)S(1)}, f32[384,128]{1,0:T(8,128)S(1)}, u32[]{:S(2)}, u32[]{:S(2)}) collective-permute-start(f32[384,128]{1,0:T(8,128)S(1)} %get-tuple-element.21.after_ref), channel_id=1, source_target_pairs={{0,1},{1,0},{2,3},{3,2},{4,5},{5,4},{6,7},{7,6},{8,9},{9,8},{10,11... | collective-permute-start | bytes 589832 | tf_op jit(solution)/shard_map/ppermute | solution.py:754
  47.9 5.7 %collective-permute-start.11 = (f32[384,128]{1,0:T(8,128)S(1)}, f32[384,128]{1,0:T(8,128)S(1)}, u32[]{:S(2)}, u32[]{:S(2)}) collective-permute-start(f32[384,128]{1,0:T(8,128)S(1)} %shard_map.79.left_ref), channel_id=1, source_target_pairs={{0,2},{1,5},{2,0},{3,7},{4,6},{5,1},{6,4},{7,3},{8,10},{9,13},{10,... | collective-permute-start | bytes 589832 | tf_op jit(solution)/shard_map/ppermute | solution.py:806
  49.3 10.1 %collective-permute-start.13 = (f32[416,128]{1,0:T(8,128)S(1)}, f32[416,128]{1,0:T(8,128)S(1)}, u32[]{:S(2)}, u32[]{:S(2)}) collective-permute-start(f32[416,128]{1,0:T(8,128)S(1)} %get-tuple-element.26), channel_id=1, source_target_pairs={{0,8},{8,16},{16,24},{1,9},{9,17},{17,25},{2,10},{10,18},{18,26},{... | collective-permute-start | bytes 638984 | tf_op jit(solution)/shard_map/ppermute | solution.py:750
  53.6 5.7 %collective-permute-start.12 = (f32[384,128]{1,0:T(8,128)S(1)}, f32[384,128]{1,0:T(8,128)S(1)}, u32[]{:S(2)}, u32[]{:S(2)}) collective-permute-start(f32[384,128]{1,0:T(8,128)S(1)} %shard_map.80.left_ref), channel_id=1, source_target_pairs={{0,4},{1,3},{2,6},{3,1},{4,0},{5,7},{6,2},{7,5},{8,12},{9,11},{10,... | collective-permute-start | bytes 589832 | tf_op jit(solution)/shard_map/ppermute | solution.py:807
  55.3 5.5 %collective-permute-start.15 = (bf16[208,128]{1,0:T(8,128)(2,1)S(1)}, bf16[208,128]{1,0:T(8,128)(2,1)S(1)}, u32[]{:S(2)}, u32[]{:S(2)}) collective-permute-start(bf16[208,128]{1,0:T(8,128)(2,1)S(1)} %shard_map.75.after_ref.left_ref), channel_id=1, source_target_pairs={{0,4},{1,3},{2,6},{3,1},{4,0},{5,7},{6,2},{7,5},{8,12},{9,11},{10,... | collective-permute-start | bytes 159752 | tf_op jit(solution)/shard_map/ppermute | solution.py:810
  60.7 1.6 %collective-permute-start.14 = (bf16[304,384]{1,0:T(8,128)(2,1)S(1)}, bf16[304,384]{1,0:T(8,128)(2,1)S(1)}, u32[]{:S(2)}, u32[]{:S(2)}) collective-permute-start(bf16[304,384]{1,0:T(8,128)(2,1)S(1)} %shard_map.82.left_ref), channel_id=1, source_target_pairs={{0,1},{1,0},{2,3},{3,2},{4,5},{5,4},{6,7},{7,6},{8,9},{9,8},{10,11... | collective-permute-start | bytes 700424 | tf_op jit(solution)/shard_map/ppermute | solution.py:754
  60.8 1.5 %collective-permute-start.16 = (bf16[208,128]{1,0:T(8,128)(2,1)S(1)}, bf16[208,128]{1,0:T(8,128)(2,1)S(1)}, u32[]{:S(2)}, u32[]{:S(2)}) collective-permute-start(bf16[208,128]{1,0:T(8,128)(2,1)S(1)} %shard_map.83.mine_ref), channel_id=1, source_target_pairs={{0,1},{1,0},{2,3},{3,2},{4,5},{5,4},{6,7},{7,6},{8,9},{9,8},{10,11... | collective-permute-start | bytes 159752 | tf_op jit(solution)/shard_map/ppermute | solution.py:754

commit v7 on v6

--- a/solution.py
+++ b/solution.py
@@ -10,7 +10,7 @@
 SUBBLOCK = 128
 LANES = 128
 PANEL = 16
-EARLY_PANELS = 8
+EARLY_PANELS = 7
 WHOLE = pl.BlockSpec(memory_space=pltpu.VMEM)
 SCALARS = pl.BlockSpec(memory_space=pltpu.SMEM)
 ANYWHERE = pl.BlockSpec(memory_space=pl.ANY)
@@ -174,18 +174,20 @@
     channels = left_ref.shape[0]
     rows = round_up(channels, PANEL)
     offset = 0
-    for start, size in strips(channels, LANES):
-        tall = rows - start
-        if size < LANES:
-            out_ref[offset : offset + tall, :] = jnp.zeros((tall, LANES), jnp.float32)
-        elif rows > channels:
-            out_ref[offset + channels - start : offset + tall, :] = jnp.zeros(
-                (rows - channels, LANES), jnp.float32
-            )
-        out_ref[offset : offset + channels - start, 0:size] = dot(
-            left_ref[start:channels, :], right_ref[start : start + size, :], ((1,), (1,))
-        )
-        offset += tall
+    for start, size in strips(channels, 2 * LANES):
+        product = dot(left_ref[start:channels, :], right_ref[start : start + size, :], ((1,), (1,)))
+        for skip in range(0, size, LANES):
+            width = min(LANES, size - skip)
+            top = start + skip
+            tall = rows - top
+            if width < LANES:
+                out_ref[offset : offset + tall, :] = jnp.zeros((tall, LANES), jnp.float32)
+            elif rows > channels:
+                out_ref[offset + channels - top : offset + tall, :] = jnp.zeros(
+                    (rows - channels, LANES), jnp.float32
+                )
+            out_ref[offset : offset + channels - top, 0:width] = product[skip:, skip : skip + width]
+            offset += tall
 
 
 def full_products(left_ref, right_ref, out_ref):

time: 63.8 us -> 63.6 us (level)
  transfers between devices with their start and end apart: 17 -> 17, of which waited for: 7 -> 6; matrix products, arithmetic and copies ran while one was open for 0% -> 0% of each run, Pallas kernels for 35% -> 35%
where the time goes in v7:
time: 63.6 us; the launch traced here: 63.3 us
  starting transfers between devices  28.4 us (45%)
  Pallas kernels  24.7 us (39%)
  waiting for transfers between devices  8.58 us (13%)
  between operations  0.9 us (1%)
  local copies, waits for them, and re-layouts  0.7 us (1%)
    ppermute x4, starting transfers between devices, from_behind(): lax.ppermute(value, axis, [(source, source + steps) for source in range(l...  11.5 us
    pallas_call x2, Pallas kernels, tile_product(): pl.pallas_call(functools.partial(tile_kernel, which, in_turn), in_specs=[...  7.31 us
    pallas_call x1, Pallas kernels, first_stage(): pl.pallas_call(functools.partial(first_stage_kernel, channels, 1.0 / tota...  6.82 us
    ppermute x3, starting transfers between devices, sum_chips(): lax.ppermute(value, 'rows', [(s, s ^ bits) for s in range(count)])  5.89 us
    ppermute x6, starting transfers between devices, other_core(): lax.ppermute(value, 'rows', [(s, s ^ 1) for s in range(lax.axis_size('row...  5.89 us
    ppermute x3, waiting for transfers between devices, sum_chips(): lax.ppermute(value, 'rows', [(s, s ^ bits) for s in range(count)])  3.49 us
    pallas_call x1, Pallas kernels, later_product(): pl.pallas_call(later_kernel, in_specs=[WHOLE, WHOLE, ANYWHERE, WHOLE], ou...  3.14 us
    ppermute x6, waiting for transfers between devices, other_core(): lax.ppermute(value, 'rows', [(s, s ^ 1) for s in range(lax.axis_size('row...  2.21 us
  transfers between devices with their start and end apart: 17, of which 6 were waited for; matrix products, arithmetic and copies ran while one was open for 0% of the time, Pallas kernels for 35%

profile of v7, /device:TPU:0, one launch (start us, length us, event | category | flops | bytes accessed | tf_op | source)
XLA Modules:
  0.0 63.3 jit_solution(2989154900692310247)
XLA Ops:
  0.6 1.4 %collective-permute-start = (bf16[300,1280]{1,0:T(8,128)(2,1)}, bf16[300,1280]{1,0:T(8,128)(2,1)S(1)}, u32[]{:S(2)}, u32[]{:S(2)}) collective-permute-start(bf16[300,1280]{1,0:T(8,128)(2,1)} %bitcast.14), channel_id=1, source_target_pairs={{1,0},{2,1},{3,2},{4,3},{5,4},{6,5},{7,6},{9,8},{10,9},{11,10},{12... | collective-permute-start | bytes 2304008 | tf_op jit(solution)/shard_map/ppermute | solution.py:752
  2.8 4.0 %shard_map.69 = bf16[300,1280]{1,0:T(8,128)(2,1)S(1)} custom-call(s32[10,2,10]{2,1,0:T(2,128)S(1)} %bitcast.18, bf16[300,1280]{1,0:T(8,128)(2,1)} %bitcast.15, bf16[1280,1280]{1,0:T(8,128)(2,1)} %bitcast.21), custom_call_target="tpu_custom_call" | custom-call | flops 983040000 | bytes 3276800 | tf_op jit(solution)/shard_map/pallas_call | solution.py:112
  6.8 3.1 %collective-permute-start.1 = (bf16[300,1280]{1,0:T(8,128)(2,1)S(1)}, bf16[300,1280]{1,0:T(8,128)(2,1)S(1)}, u32[]{:S(2)}, u32[]{:S(2)}) collective-permute-start(bf16[300,1280]{1,0:T(8,128)(2,1)S(1)} %shard_map.69), channel_id=1, source_target_pairs={{0,1},{1,2},{2,3},{3,4},{4,5},{5,6},{6,7},{8,9},{9,10},{10,11},{11... | collective-permute-start | bytes 2304008 | tf_op jit(solution)/shard_map/ppermute | solution.py:752
  9.9 3.3 %shard_map.67.first_ref = f32[300,1280]{1,0:T(8,128)S(1)} custom-call(s32[10,2,10]{2,1,0:T(2,128)S(1)} %bitcast.19, bf16[300,1280]{1,0:T(8,128)(2,1)S(1)} %bitcast.16, bf16[1280,1280]{1,0:T(8,128)(2,1)} %bitcast.23), custom_call_target="tpu_custom_call" | custom-call | flops 983040000 | bytes 3276800 | tf_op jit(solution)/shard_map/pallas_call | solution.py:112
  13.2 3.1 %shard_map.68.part_ref = f32[300,1280]{1,0:T(8,128)S(1)} custom-call(s32[10,2,10]{2,1,0:T(2,128)S(1)} %bitcast.20, bf16[300,1280]{1,0:T(8,128)(2,1)S(1)} %collective-permute-done.later_ref, bf16[1280,1280]{1,0:T(8,128)(2,1)} %bitcast.22, f32[300,1280]{1,0:T(8,128)S(1)} %shard_map.67.first_ref), custom_call_target="tpu_custom_call" | custom-call | flops 983040000 | bytes 3276800 | tf_op jit(solution)/shard_map/pallas_call | solution.py:147
  16.9 4.9 %collective-permute-start.2 = (f32[208,128]{1,0:T(8,128)S(1)}, f32[208,128]{1,0:T(8,128)S(1)}, u32[]{:S(2)}, u32[]{:S(2)}) collective-permute-start(f32[208,128]{1,0:T(8,128)S(1)} %get-tuple-element.17), channel_id=1, source_target_pairs={{0,1},{1,0},{2,3},{3,2},{4,5},{5,4},{6,7},{7,6},{8,9},{9,8},{10,11... | collective-permute-start | bytes 319496 | tf_op jit(solution)/shard_map/ppermute | solution.py:756
  21.8 3.5 %collective-permute-start.8 = (bf16[300,1280]{1,0:T(8,128)(2,1)S(1)}, bf16[300,1280]{1,0:T(8,128)(2,1)S(1)}, u32[]{:S(2)}, u32[]{:S(2)}) collective-permute-start(bf16[300,1280]{1,0:T(8,128)(2,1)S(1)} %get-tuple-element.18.y_ref.right_ref), channel_id=1, source_target_pairs={{0,8},{8,16},{16,24},{1,9},{9,17},{17,25},{2,10},{10,18},{18,26},{... | collective-permute-start | bytes 2304008 | tf_op jit(solution)/shard_map/ppermute | solution.py:752
  25.4 5.2 %collective-permute-start.3 = (f32[208,128]{1,0:T(8,128)S(1)}, f32[208,128]{1,0:T(8,128)S(1)}, u32[]{:S(2)}, u32[]{:S(2)}) collective-permute-start(f32[208,128]{1,0:T(8,128)S(1)} %add.8.after_ref.own_ref), channel_id=1, source_target_pairs={{0,6},{1,7},{2,4},{3,5},{4,2},{5,3},{6,0},{7,1},{8,14},{9,15},{10,... | collective-permute-start | bytes 319496 | tf_op jit(solution)/shard_map/ppermute | solution.py:774
  31.8 1.2 %collective-permute-done.6.right_ref = bf16[208,128]{1,0:T(8,128)(2,1)S(1)} collective-permute-done((bf16[208,128]{1,0:T(8,128)(2,1)S(1)}, bf16[208,128]{1,0:T(8,128)(2,1)S(1)}, u32[]{:S(2)}, u32[]{:S(2)}) %collective-permute-start.6) | collective-permute-done | bytes 53280 | tf_op jit(solution)/shard_map/ppermute | solution.py:756
  33.0 1.3 %collective-permute-done.3.both_ref = f32[208,128]{1,0:T(8,128)S(1)} collective-permute-done((f32[208,128]{1,0:T(8,128)S(1)}, f32[208,128]{1,0:T(8,128)S(1)}, u32[]{:S(2)}, u32[]{:S(2)}) %collective-permute-start.3) | collective-permute-done | bytes 106528 | tf_op jit(solution)/shard_map/ppermute | solution.py:774
  34.4 2.2 %collective-permute-done.4.first_ref = f32[208,128]{1,0:T(8,128)S(1)} collective-permute-done((f32[208,128]{1,0:T(8,128)S(1)}, f32[208,128]{1,0:T(8,128)S(1)}, u32[]{:S(2)}, u32[]{:S(2)}) %collective-permute-start.4) | collective-permute-done | bytes 106528 | tf_op jit(solution)/shard_map/ppermute | solution.py:774
  36.6 1.5 %collective-permute-start.9 = (bf16[208,128]{1,0:T(8,128)(2,1)S(1)}, bf16[208,128]{1,0:T(8,128)(2,1)S(1)}, u32[]{:S(2)}, u32[]{:S(2)}) collective-permute-start(bf16[208,128]{1,0:T(8,128)(2,1)S(1)} %shard_map.72.after_ref.left_ref), channel_id=1, source_target_pairs={{0,2},{1,5},{2,0},{3,7},{4,6},{5,1},{6,4},{7,3},{8,10},{9,13},{10,... | collective-permute-start | bytes 159752 | tf_op jit(solution)/shard_map/ppermute | solution.py:799
  38.2 6.8 %shard_map.74.refs_0_.before_ref = f32[304,384]{1,0:T(8,128)S(1)} custom-call(s32[1]{0:T(128)} %bitcast.core_ref, f32[208,128]{1,0:T(8,128)S(1)} %shard_map.73.mine_ref, f32[208,128]{1,0:T(8,128)S(1)} %collective-permute-done.7.other_ref), custom_call_target="tpu_custom_call" | custom-call | flops 5000000000 | bytes 1000000 | tf_op jit(solution)/shard_map/pallas_call | solution.py:599
  45.0 0.8 %shard_map.76 = (f32[384,128]{1,0:T(8,128)S(1)}, f32[384,128]{1,0:T(8,128)S(1)}) custom-call(s32[1]{0:T(128)} %bitcast.core_ref, bf16[300,1280]{1,0:T(8,128)(2,1)S(1)} %collective-permute-done.8.left_ref, bf16[300,1280]{1,0:T(8,128)(2,1)S(1)} %get-tuple-element.18.y_ref.right_ref, bf16[208,128]{1,0:T(8,128)(2,1)S(1)} %shard_map.75.after_ref.left_ref), custom_call_target="tpu_custom_call" | custom-call | flops 230400000 | bytes 1536000 | tf_op jit(solution)/shard_map/pallas_call | solution.py:372
  46.1 1.5 %shard_map.77 = (f32[304,384]{1,0:T(8,128)S(1)}, f32[416,128]{1,0:T(8,128)S(1)}) custom-call(f32[304,384]{1,0:T(8,128)S(1)} %shard_map.74.refs_0_.before_ref, f32[384,128]{1,0:T(8,128)S(1)} %get-tuple-element.21.after_ref), custom_call_target="tpu_custom_call" | custom-call | flops 4000000000 | bytes 100000 | tf_op jit(solution)/shard_map/pallas_call | solution.py:615
  47.6 1.5 %collective-permute-start.11 = (f32[384,128]{1,0:T(8,128)S(1)}, f32[384,128]{1,0:T(8,128)S(1)}, u32[]{:S(2)}, u32[]{:S(2)}) collective-permute-start(f32[384,128]{1,0:T(8,128)S(1)} %shard_map.79.left_ref), channel_id=1, source_target_pairs={{0,2},{1,5},{2,0},{3,7},{4,6},{5,1},{6,4},{7,3},{8,10},{9,13},{10,... | collective-permute-start | bytes 589832 | tf_op jit(solution)/shard_map/ppermute | solution.py:808
  49.2 3.4 %collective-permute-start.13 = (f32[416,128]{1,0:T(8,128)S(1)}, f32[416,128]{1,0:T(8,128)S(1)}, u32[]{:S(2)}, u32[]{:S(2)}) collective-permute-start(f32[416,128]{1,0:T(8,128)S(1)} %get-tuple-element.26), channel_id=1, source_target_pairs={{0,8},{8,16},{16,24},{1,9},{9,17},{17,25},{2,10},{10,18},{18,26},{... | collective-permute-start | bytes 638984 | tf_op jit(solution)/shard_map/ppermute | solution.py:752
  52.6 0.8 %collective-permute-done.11.right_ref = f32[384,128]{1,0:T(8,128)S(1)} collective-permute-done((f32[384,128]{1,0:T(8,128)S(1)}, f32[384,128]{1,0:T(8,128)S(1)}, u32[]{:S(2)}, u32[]{:S(2)}) %collective-permute-start.11) | collective-permute-done | bytes 196640 | tf_op jit(solution)/shard_map/ppermute | solution.py:808
  53.4 1.9 %collective-permute-start.12 = (f32[384,128]{1,0:T(8,128)S(1)}, f32[384,128]{1,0:T(8,128)S(1)}, u32[]{:S(2)}, u32[]{:S(2)}) collective-permute-start(f32[384,128]{1,0:T(8,128)S(1)} %shard_map.80.left_ref), channel_id=1, source_target_pairs={{0,4},{1,3},{2,6},{3,1},{4,0},{5,7},{6,2},{7,5},{8,12},{9,11},{10,... | collective-permute-start | bytes 589832 | tf_op jit(solution)/shard_map/ppermute | solution.py:809
  55.5 1.5 %shard_map.78 = (bf16[300,1280]{1,0:T(8,128)(2,1)}, f32[8,128]{1,0:T(8,128)S(1)}) custom-call(f32[304,384]{1,0:T(8,128)S(1)} %get-tuple-element.22.inverse_ref.refs_0_, bf16[300,1280]{1,0:T(8,128)(2,1)S(1)} %get-tuple-element.18.y_ref.right_ref), custom_call_target="tpu_custom_call" | custom-call | flops 100000 | bytes 100000 | tf_op jit(solution)/shard_map/pallas_call | solution.py:670
  57.1 2.1 %collective-permute-done.12.right_ref = f32[384,128]{1,0:T(8,128)S(1)} collective-permute-done((f32[384,128]{1,0:T(8,128)S(1)}, f32[384,128]{1,0:T(8,128)S(1)}, u32[]{:S(2)}, u32[]{:S(2)}) %collective-permute-start.12) | collective-permute-done | bytes 196640 | tf_op jit(solution)/shard_map/ppermute | solution.py:809
  59.2 1.3 %shard_map.82.left_ref = bf16[304,384]{1,0:T(8,128)(2,1)S(1)} custom-call(s32[1]{0:T(128)} %bitcast.core_ref, f32[384,128]{1,0:T(8,128)S(1)} %shard_map.81.mine_ref, f32[304,384]{1,0:T(8,128)S(1)} %get-tuple-element.22.inverse_ref.refs_0_, f32[416,128]{1,0:T(8,128)S(1)} %collective-permute-done.13.previous_ref), custom_call_target="tpu_custom_call" | custom-call | flops 100000 | bytes 100000 | tf_op jit(solution)/shard_map/pallas_call | solution.py:704
  61.1 1.0 %collective-permute-done.16.other_ref = bf16[208,128]{1,0:T(8,128)(2,1)S(1)} collective-permute-done((bf16[208,128]{1,0:T(8,128)(2,1)S(1)}, bf16[208,128]{1,0:T(8,128)(2,1)S(1)}, u32[]{:S(2)}, u32[]{:S(2)}) %collective-permute-start.16) | collective-permute-done | bytes 53280 | tf_op jit(solution)/shard_map/ppermute | solution.py:756
  62.1 1.2 %shard_map.84 = (f32[300,1,300]{2,1,0:T(1,128)}, f32[300,1,300]{2,1,0:T(1,128)}) custom-call(s32[1]{0:T(128)} %bitcast.core_ref, bf16[304,384]{1,0:T(8,128)(2,1)S(1)} %shard_map.82.left_ref, bf16[304,384]{1,0:T(8,128)(2,1)S(1)} %collective-permute-done.14.right_ref, bf16[208,128]{1,0:T(8,128)(2,1)S(1)} %shard_map.83.mine_ref, ...), custom_call_target="tpu_custom_call" | custom-call | flops 100000 | bytes 100000 | tf_op jit(solution)/shard_map/pallas_call | solution.py:734
  (35 shorter events, 3.6 us)
Async XLA Ops:
  0.6 9.3 %copy-start = (bf16[1,1280,300]{1,2,0:T(8,128)(2,1)S(1)}, bf16[1,1280,300]{1,2,0:T(8,128)(2,1)}, u32[]{:S(2)}) copy-start(bf16[1,1280,300]{1,2,0:T(8,128)(2,1)} %param.4) | copy-start | bytes 2304004
  0.6 12.6 %collective-permute-start = (bf16[300,1280]{1,0:T(8,128)(2,1)}, bf16[300,1280]{1,0:T(8,128)(2,1)S(1)}, u32[]{:S(2)}, u32[]{:S(2)}) collective-permute-start(bf16[300,1280]{1,0:T(8,128)(2,1)} %bitcast.14), channel_id=1, source_target_pairs={{1,0},{2,1},{3,2},{4,3},{5,4},{6,5},{7,6},{9,8},{10,9},{11,10},{12... | collective-permute-start | bytes 2304008 | tf_op jit(solution)/shard_map/ppermute | solution.py:752
  2.1 0.7 %copy-start.1 = (s32[1,2,10,10]{3,1,2,0:T(2,128)S(1)}, s32[1,2,10,10]{3,1,2,0:T(2,128)}, u32[]{:S(2)}) copy-start(s32[1,2,10,10]{3,1,2,0:T(2,128)} %param.7) | copy-start | bytes 2404
  2.8 7.1 %copy-start.2 = (s32[1,2,10,10]{3,1,2,0:T(2,128)S(1)}, s32[1,2,10,10]{3,1,2,0:T(2,128)}, u32[]{:S(2)}) copy-start(s32[1,2,10,10]{3,1,2,0:T(2,128)} %param.7) | copy-start | bytes 2404
  6.8 9.6 %collective-permute-start.1 = (bf16[300,1280]{1,0:T(8,128)(2,1)S(1)}, bf16[300,1280]{1,0:T(8,128)(2,1)S(1)}, u32[]{:S(2)}, u32[]{:S(2)}) collective-permute-start(bf16[300,1280]{1,0:T(8,128)(2,1)S(1)} %shard_map.69), channel_id=1, source_target_pairs={{0,1},{1,2},{2,3},{3,4},{4,5},{5,6},{6,7},{8,9},{9,10},{10,11},{11... | collective-permute-start | bytes 2304008 | tf_op jit(solution)/shard_map/ppermute | solution.py:752
  16.9 8.4 %collective-permute-start.2 = (f32[208,128]{1,0:T(8,128)S(1)}, f32[208,128]{1,0:T(8,128)S(1)}, u32[]{:S(2)}, u32[]{:S(2)}) collective-permute-start(f32[208,128]{1,0:T(8,128)S(1)} %get-tuple-element.17), channel_id=1, source_target_pairs={{0,1},{1,0},{2,3},{3,2},{4,5},{5,4},{6,7},{7,6},{8,9},{9,8},{10,11... | collective-permute-start | bytes 319496 | tf_op jit(solution)/shard_map/ppermute | solution.py:756
  21.8 23.2 %collective-permute-start.8 = (bf16[300,1280]{1,0:T(8,128)(2,1)S(1)}, bf16[300,1280]{1,0:T(8,128)(2,1)S(1)}, u32[]{:S(2)}, u32[]{:S(2)}) collective-permute-start(bf16[300,1280]{1,0:T(8,128)(2,1)S(1)} %get-tuple-element.18.y_ref.right_ref), channel_id=1, source_target_pairs={{0,8},{8,16},{16,24},{1,9},{9,17},{17,25},{2,10},{10,18},{18,26},{... | collective-permute-start | bytes 2304008 | tf_op jit(solution)/shard_map/ppermute | solution.py:752
  25.4 9.0 %collective-permute-start.3 = (f32[208,128]{1,0:T(8,128)S(1)}, f32[208,128]{1,0:T(8,128)S(1)}, u32[]{:S(2)}, u32[]{:S(2)}) collective-permute-start(f32[208,128]{1,0:T(8,128)S(1)} %add.8.after_ref.own_ref), channel_id=1, source_target_pairs={{0,6},{1,7},{2,4},{3,5},{4,2},{5,3},{6,0},{7,1},{8,14},{9,15},{10,... | collective-permute-start | bytes 319496 | tf_op jit(solution)/shard_map/ppermute | solution.py:774
  30.6 5.9 %collective-permute-start.4 = (f32[208,128]{1,0:T(8,128)S(1)}, f32[208,128]{1,0:T(8,128)S(1)}, u32[]{:S(2)}, u32[]{:S(2)}) collective-permute-start(f32[208,128]{1,0:T(8,128)S(1)} %add.8.after_ref.own_ref), channel_id=1, source_target_pairs={{0,2},{1,3},{2,0},{3,1},{4,6},{5,7},{6,4},{7,5},{8,10},{9,11},{10,... | collective-permute-start | bytes 319496 | tf_op jit(solution)/shard_map/ppermute | solution.py:774
  31.2 5.3 %collective-permute-start.5 = (f32[208,128]{1,0:T(8,128)S(1)}, f32[208,128]{1,0:T(8,128)S(1)}, u32[]{:S(2)}, u32[]{:S(2)}) collective-permute-start(f32[208,128]{1,0:T(8,128)S(1)} %add.8.after_ref.own_ref), channel_id=1, source_target_pairs={{0,4},{1,5},{2,6},{3,7},{4,0},{5,1},{6,2},{7,3},{8,12},{9,13},{10,... | collective-permute-start | bytes 319496 | tf_op jit(solution)/shard_map/ppermute | solution.py:774
  31.7 1.3 %collective-permute-start.6 = (bf16[208,128]{1,0:T(8,128)(2,1)S(1)}, bf16[208,128]{1,0:T(8,128)(2,1)S(1)}, u32[]{:S(2)}, u32[]{:S(2)}) collective-permute-start(bf16[208,128]{1,0:T(8,128)(2,1)S(1)} %get-tuple-element.20), channel_id=1, source_target_pairs={{0,1},{1,0},{2,3},{3,2},{4,5},{5,4},{6,7},{7,6},{8,9},{9,8},{10,11... | collective-permute-start | bytes 159752 | tf_op jit(solution)/shard_map/ppermute | solution.py:756
  36.6 1.6 %collective-permute-start.7 = (f32[208,128]{1,0:T(8,128)S(1)}, f32[208,128]{1,0:T(8,128)S(1)}, u32[]{:S(2)}, u32[]{:S(2)}) collective-permute-start(f32[208,128]{1,0:T(8,128)S(1)} %shard_map.73.mine_ref), channel_id=1, source_target_pairs={{0,1},{1,0},{2,3},{3,2},{4,5},{5,4},{6,7},{7,6},{8,9},{9,8},{10,11... | collective-permute-start | bytes 319496 | tf_op jit(solution)/shard_map/ppermute | solution.py:756
  36.6 8.4 %collective-permute-start.9 = (bf16[208,128]{1,0:T(8,128)(2,1)S(1)}, bf16[208,128]{1,0:T(8,128)(2,1)S(1)}, u32[]{:S(2)}, u32[]{:S(2)}) collective-permute-start(bf16[208,128]{1,0:T(8,128)(2,1)S(1)} %shard_map.72.after_ref.left_ref), channel_id=1, source_target_pairs={{0,2},{1,5},{2,0},{3,7},{4,6},{5,1},{6,4},{7,3},{8,10},{9,13},{10,... | collective-permute-start | bytes 159752 | tf_op jit(solution)/shard_map/ppermute | solution.py:799
  45.8 1.8 %collective-permute-start.10 = (f32[384,128]{1,0:T(8,128)S(1)}, f32[384,128]{1,0:T(8,128)S(1)}, u32[]{:S(2)}, u32[]{:S(2)}) collective-permute-start(f32[384,128]{1,0:T(8,128)S(1)} %get-tuple-element.21.after_ref), channel_id=1, source_target_pairs={{0,1},{1,0},{2,3},{3,2},{4,5},{5,4},{6,7},{7,6},{8,9},{9,8},{10,11... | collective-permute-start | bytes 589832 | tf_op jit(solution)/shard_map/ppermute | solution.py:756
  47.6 5.7 %collective-permute-start.11 = (f32[384,128]{1,0:T(8,128)S(1)}, f32[384,128]{1,0:T(8,128)S(1)}, u32[]{:S(2)}, u32[]{:S(2)}) collective-permute-start(f32[384,128]{1,0:T(8,128)S(1)} %shard_map.79.left_ref), channel_id=1, source_target_pairs={{0,2},{1,5},{2,0},{3,7},{4,6},{5,1},{6,4},{7,3},{8,10},{9,13},{10,... | collective-permute-start | bytes 589832 | tf_op jit(solution)/shard_map/ppermute | solution.py:808
  49.2 10.0 %collective-permute-start.13 = (f32[416,128]{1,0:T(8,128)S(1)}, f32[416,128]{1,0:T(8,128)S(1)}, u32[]{:S(2)}, u32[]{:S(2)}) collective-permute-start(f32[416,128]{1,0:T(8,128)S(1)} %get-tuple-element.26), channel_id=1, source_target_pairs={{0,8},{8,16},{16,24},{1,9},{9,17},{17,25},{2,10},{10,18},{18,26},{... | collective-permute-start | bytes 638984 | tf_op jit(solution)/shard_map/ppermute | solution.py:752
  53.4 5.7 %collective-permute-start.12 = (f32[384,128]{1,0:T(8,128)S(1)}, f32[384,128]{1,0:T(8,128)S(1)}, u32[]{:S(2)}, u32[]{:S(2)}) collective-permute-start(f32[384,128]{1,0:T(8,128)S(1)} %shard_map.80.left_ref), channel_id=1, source_target_pairs={{0,4},{1,3},{2,6},{3,1},{4,0},{5,7},{6,2},{7,5},{8,12},{9,11},{10,... | collective-permute-start | bytes 589832 | tf_op jit(solution)/shard_map/ppermute | solution.py:809
  55.3 5.2 %collective-permute-start.15 = (bf16[208,128]{1,0:T(8,128)(2,1)S(1)}, bf16[208,128]{1,0:T(8,128)(2,1)S(1)}, u32[]{:S(2)}, u32[]{:S(2)}) collective-permute-start(bf16[208,128]{1,0:T(8,128)(2,1)S(1)} %shard_map.75.after_ref.left_ref), channel_id=1, source_target_pairs={{0,4},{1,3},{2,6},{3,1},{4,0},{5,7},{6,2},{7,5},{8,12},{9,11},{10,... | collective-permute-start | bytes 159752 | tf_op jit(solution)/shard_map/ppermute | solution.py:812
  60.5 1.6 %collective-permute-start.14 = (bf16[304,384]{1,0:T(8,128)(2,1)S(1)}, bf16[304,384]{1,0:T(8,128)(2,1)S(1)}, u32[]{:S(2)}, u32[]{:S(2)}) collective-permute-start(bf16[304,384]{1,0:T(8,128)(2,1)S(1)} %shard_map.82.left_ref), channel_id=1, source_target_pairs={{0,1},{1,0},{2,3},{3,2},{4,5},{5,4},{6,7},{7,6},{8,9},{9,8},{10,11... | collective-permute-start | bytes 700424 | tf_op jit(solution)/shard_map/ppermute | solution.py:756
  60.6 1.5 %collective-permute-start.16 = (bf16[208,128]{1,0:T(8,128)(2,1)S(1)}, bf16[208,128]{1,0:T(8,128)(2,1)S(1)}, u32[]{:S(2)}, u32[]{:S(2)}) collective-permute-start(bf16[208,128]{1,0:T(8,128)(2,1)S(1)} %shard_map.83.mine_ref), channel_id=1, source_target_pairs={{0,1},{1,0},{2,3},{3,2},{4,5},{5,4},{6,7},{7,6},{8,9},{9,8},{10,11... | collective-permute-start | bytes 159752 | tf_op jit(solution)/shard_map/ppermute | solution.py:756

commit v8 on v7

--- a/solution.py
+++ b/solution.py
@@ -685,12 +685,13 @@
 
 
 def part_kernel(
-    channels, scale, core_ref, mine_ref, inverse_ref, previous_ref, out_ref,
+    channels, scale, core_ref, mine_ref, chip_ref, inverse_ref, previous_ref, after_ref, out_ref,
     pack_ref, lower_ref, before_ref,
 ):
     rows, wide = inverse_ref.shape
     half = mine_ref.shape[0]
-    join(pack_ref, core_ref[0], mine_ref[...], jnp.zeros((half, LANES), jnp.float32))
+    mine = mine_ref[...] + chip_ref[...]
+    join(pack_ref, core_ref[0], mine, jnp.zeros((half, LANES), jnp.float32))
     turned = dot3(full_matrix(pack_ref, channels), inverse_ref[...], ((1,), (1,)))
     unfold(previous_ref, lower_ref, channels, False)
     lower_matrix(lower_ref, before_ref)
@@ -700,10 +701,10 @@
         out_ref[:, rows:wide] = jnp.zeros((rows, wide - rows), out_ref.dtype)
 
 
-def correlation_part(core, mine, inverse, previous, channels, total_rows):
+def correlation_part(core, mine, chip, inverse, previous, after, channels, total_rows):
     return pl.pallas_call(
         functools.partial(part_kernel, channels, 1.0 / total_rows),
-        in_specs=[SCALARS] + [WHOLE] * 3,
+        in_specs=[SCALARS] + [WHOLE] * 4 + [ANYWHERE],
         out_specs=WHOLE,
         out_shape=jax.ShapeDtypeStruct(inverse.shape, jnp.bfloat16),
         scratch_shapes=[
@@ -713,7 +714,7 @@
         ],
         compiler_params=params(),
         cost_estimate=cost(10**5, 10**5),
-    )(core, mine, inverse, previous)
+    )(core, mine, chip, inverse, previous, after)
 
 
 def both_kernel(
@@ -806,8 +807,10 @@
     q_t, basis_token = basis(inverse, y_t)
     for pairs in rounds[:-1]:
         m_sum = add_after(m_sum, lax.ppermute(m_sum, "rows", pairs))
-    m_sum = add_after(m_sum, lax.ppermute(m_sum, "rows", rounds[-1]), basis_token)
-    part = correlation_part(core, m_sum, inverse, previous, channels, total_rows)
+    chip = lax.ppermute(m_sum, "rows", rounds[-1])
+    part = correlation_part(
+        core, m_sum, chip, inverse, previous, basis_token, channels, total_rows
+    )
     for pairs in rounds[1:]:
         r_sum = add_after(r_sum, lax.ppermute(r_sum, "rows", pairs), flops=LAST_RAY_FLOPS)
     correlation, rayleigh = both_parts(

time: 63.6 us -> 63.6 us (level)
    ppermute x1, waiting for transfers between devices: 2.1 us -> 1.22 us  [shards(): chip = lax.ppermute(m_sum, 'rows', rounds[-1])]
    ppermute x4, waiting for transfers between devices: 0.01 us -> 0.88 us  [from_behind(): lax.ppermute(value, axis, [(source, source + steps) for source in range(l...]
  transfers between devices with their start and end apart: 17 -> 17, of which waited for: 6 -> 7; matrix products, arithmetic and copies ran while one was open for 0% -> 0% of each run, Pallas kernels for 35% -> 35%
where the time goes in v8:
time: 63.6 us; the launch traced here: 63.2 us
  starting transfers between devices  28.4 us (45%)
  Pallas kernels  24.6 us (39%)
  waiting for transfers between devices  8.57 us (13%)
  between operations  0.9 us (1%)
  local copies, waits for them, and re-layouts  0.7 us (1%)
    ppermute x4, starting transfers between devices, from_behind(): lax.ppermute(value, axis, [(source, source + steps) for source in range(l...  11.5 us
    pallas_call x2, Pallas kernels, tile_product(): pl.pallas_call(functools.partial(tile_kernel, which, in_turn), in_specs=[...  7.31 us
    pallas_call x1, Pallas kernels, first_stage(): pl.pallas_call(functools.partial(first_stage_kernel, channels, 1.0 / tota...  6.82 us
    ppermute x3, starting transfers between devices, sum_chips(): lax.ppermute(value, 'rows', [(s, s ^ bits) for s in range(count)])  5.89 us
    ppermute x6, starting transfers between devices, other_core(): lax.ppermute(value, 'rows', [(s, s ^ 1) for s in range(lax.axis_size('row...  5.89 us
    ppermute x3, waiting for transfers between devices, sum_chips(): lax.ppermute(value, 'rows', [(s, s ^ bits) for s in range(count)])  3.49 us
    pallas_call x1, Pallas kernels, later_product(): pl.pallas_call(later_kernel, in_specs=[WHOLE, WHOLE, ANYWHERE, WHOLE], ou...  3.14 us
    ppermute x6, waiting for transfers between devices, other_core(): lax.ppermute(value, 'rows', [(s, s ^ 1) for s in range(lax.axis_size('row...  2.21 us
  transfers between devices with their start and end apart: 17, of which 7 were waited for; matrix products, arithmetic and copies ran while one was open for 0% of the time, Pallas kernels for 35%

profile of v8, /device:TPU:0, one launch (start us, length us, event | category | flops | bytes accessed | tf_op | source)
XLA Modules:
  0.0 63.2 jit_solution(18275752769057357219)
XLA Ops:
  0.6 1.4 %collective-permute-start = (bf16[300,1280]{1,0:T(8,128)(2,1)}, bf16[300,1280]{1,0:T(8,128)(2,1)S(1)}, u32[]{:S(2)}, u32[]{:S(2)}) collective-permute-start(bf16[300,1280]{1,0:T(8,128)(2,1)} %bitcast.14), channel_id=1, source_target_pairs={{1,0},{2,1},{3,2},{4,3},{5,4},{6,5},{7,6},{9,8},{10,9},{11,10},{12... | collective-permute-start | bytes 2304008 | tf_op jit(solution)/shard_map/ppermute | solution.py:753
  2.8 4.0 %shard_map.69 = bf16[300,1280]{1,0:T(8,128)(2,1)S(1)} custom-call(s32[10,2,10]{2,1,0:T(2,128)S(1)} %bitcast.18, bf16[300,1280]{1,0:T(8,128)(2,1)} %bitcast.15, bf16[1280,1280]{1,0:T(8,128)(2,1)} %bitcast.21), custom_call_target="tpu_custom_call" | custom-call | flops 983040000 | bytes 3276800 | tf_op jit(solution)/shard_map/pallas_call | solution.py:112
  6.8 3.1 %collective-permute-start.1 = (bf16[300,1280]{1,0:T(8,128)(2,1)S(1)}, bf16[300,1280]{1,0:T(8,128)(2,1)S(1)}, u32[]{:S(2)}, u32[]{:S(2)}) collective-permute-start(bf16[300,1280]{1,0:T(8,128)(2,1)S(1)} %shard_map.69), channel_id=1, source_target_pairs={{0,1},{1,2},{2,3},{3,4},{4,5},{5,6},{6,7},{8,9},{9,10},{10,11},{11... | collective-permute-start | bytes 2304008 | tf_op jit(solution)/shard_map/ppermute | solution.py:753
  9.9 3.3 %shard_map.67.first_ref = f32[300,1280]{1,0:T(8,128)S(1)} custom-call(s32[10,2,10]{2,1,0:T(2,128)S(1)} %bitcast.19, bf16[300,1280]{1,0:T(8,128)(2,1)S(1)} %bitcast.16, bf16[1280,1280]{1,0:T(8,128)(2,1)} %bitcast.23), custom_call_target="tpu_custom_call" | custom-call | flops 983040000 | bytes 3276800 | tf_op jit(solution)/shard_map/pallas_call | solution.py:112
  13.2 3.1 %shard_map.68.part_ref = f32[300,1280]{1,0:T(8,128)S(1)} custom-call(s32[10,2,10]{2,1,0:T(2,128)S(1)} %bitcast.20, bf16[300,1280]{1,0:T(8,128)(2,1)S(1)} %collective-permute-done.later_ref, bf16[1280,1280]{1,0:T(8,128)(2,1)} %bitcast.22, f32[300,1280]{1,0:T(8,128)S(1)} %shard_map.67.first_ref), custom_call_target="tpu_custom_call" | custom-call | flops 983040000 | bytes 3276800 | tf_op jit(solution)/shard_map/pallas_call | solution.py:147
  16.9 4.9 %collective-permute-start.2 = (f32[208,128]{1,0:T(8,128)S(1)}, f32[208,128]{1,0:T(8,128)S(1)}, u32[]{:S(2)}, u32[]{:S(2)}) collective-permute-start(f32[208,128]{1,0:T(8,128)S(1)} %get-tuple-element.17), channel_id=1, source_target_pairs={{0,1},{1,0},{2,3},{3,2},{4,5},{5,4},{6,7},{7,6},{8,9},{9,8},{10,11... | collective-permute-start | bytes 319496 | tf_op jit(solution)/shard_map/ppermute | solution.py:757
  21.8 3.5 %collective-permute-start.8 = (bf16[300,1280]{1,0:T(8,128)(2,1)S(1)}, bf16[300,1280]{1,0:T(8,128)(2,1)S(1)}, u32[]{:S(2)}, u32[]{:S(2)}) collective-permute-start(bf16[300,1280]{1,0:T(8,128)(2,1)S(1)} %get-tuple-element.18.y_ref.right_ref), channel_id=1, source_target_pairs={{0,8},{8,16},{16,24},{1,9},{9,17},{17,25},{2,10},{10,18},{18,26},{... | collective-permute-start | bytes 2304008 | tf_op jit(solution)/shard_map/ppermute | solution.py:753
  25.4 5.2 %collective-permute-start.3 = (f32[208,128]{1,0:T(8,128)S(1)}, f32[208,128]{1,0:T(8,128)S(1)}, u32[]{:S(2)}, u32[]{:S(2)}) collective-permute-start(f32[208,128]{1,0:T(8,128)S(1)} %add.8.after_ref.own_ref), channel_id=1, source_target_pairs={{0,6},{1,7},{2,4},{3,5},{4,2},{5,3},{6,0},{7,1},{8,14},{9,15},{10,... | collective-permute-start | bytes 319496 | tf_op jit(solution)/shard_map/ppermute | solution.py:775
  31.8 1.2 %collective-permute-done.6.right_ref = bf16[208,128]{1,0:T(8,128)(2,1)S(1)} collective-permute-done((bf16[208,128]{1,0:T(8,128)(2,1)S(1)}, bf16[208,128]{1,0:T(8,128)(2,1)S(1)}, u32[]{:S(2)}, u32[]{:S(2)}) %collective-permute-start.6) | collective-permute-done | bytes 53280 | tf_op jit(solution)/shard_map/ppermute | solution.py:757
  33.0 1.3 %collective-permute-done.3.both_ref = f32[208,128]{1,0:T(8,128)S(1)} collective-permute-done((f32[208,128]{1,0:T(8,128)S(1)}, f32[208,128]{1,0:T(8,128)S(1)}, u32[]{:S(2)}, u32[]{:S(2)}) %collective-permute-start.3) | collective-permute-done | bytes 106528 | tf_op jit(solution)/shard_map/ppermute | solution.py:775
  34.4 2.2 %collective-permute-done.4.first_ref = f32[208,128]{1,0:T(8,128)S(1)} collective-permute-done((f32[208,128]{1,0:T(8,128)S(1)}, f32[208,128]{1,0:T(8,128)S(1)}, u32[]{:S(2)}, u32[]{:S(2)}) %collective-permute-start.4) | collective-permute-done | bytes 106528 | tf_op jit(solution)/shard_map/ppermute | solution.py:775
  36.6 1.5 %collective-permute-start.9 = (bf16[208,128]{1,0:T(8,128)(2,1)S(1)}, bf16[208,128]{1,0:T(8,128)(2,1)S(1)}, u32[]{:S(2)}, u32[]{:S(2)}) collective-permute-start(bf16[208,128]{1,0:T(8,128)(2,1)S(1)} %shard_map.72.after_ref.left_ref), channel_id=1, source_target_pairs={{0,2},{1,5},{2,0},{3,7},{4,6},{5,1},{6,4},{7,3},{8,10},{9,13},{10,... | collective-permute-start | bytes 159752 | tf_op jit(solution)/shard_map/ppermute | solution.py:800
  38.2 6.8 %shard_map.74.refs_0_.before_ref = f32[304,384]{1,0:T(8,128)S(1)} custom-call(s32[1]{0:T(128)} %bitcast.core_ref, f32[208,128]{1,0:T(8,128)S(1)} %shard_map.73.mine_ref, f32[208,128]{1,0:T(8,128)S(1)} %collective-permute-done.7.other_ref), custom_call_target="tpu_custom_call" | custom-call | flops 5000000000 | bytes 1000000 | tf_op jit(solution)/shard_map/pallas_call | solution.py:599
  45.0 0.8 %shard_map.76 = (f32[384,128]{1,0:T(8,128)S(1)}, f32[384,128]{1,0:T(8,128)S(1)}) custom-call(s32[1]{0:T(128)} %bitcast.core_ref, bf16[300,1280]{1,0:T(8,128)(2,1)S(1)} %collective-permute-done.8.left_ref, bf16[300,1280]{1,0:T(8,128)(2,1)S(1)} %get-tuple-element.18.y_ref.right_ref, bf16[208,128]{1,0:T(8,128)(2,1)S(1)} %shard_map.75.after_ref.left_ref), custom_call_target="tpu_custom_call" | custom-call | flops 230400000 | bytes 1536000 | tf_op jit(solution)/shard_map/pallas_call | solution.py:372
  46.1 1.5 %shard_map.77 = (f32[304,384]{1,0:T(8,128)S(1)}, f32[416,128]{1,0:T(8,128)S(1)}) custom-call(f32[304,384]{1,0:T(8,128)S(1)} %shard_map.74.refs_0_.before_ref, f32[384,128]{1,0:T(8,128)S(1)} %get-tuple-element.21.after_ref), custom_call_target="tpu_custom_call" | custom-call | flops 4000000000 | bytes 100000 | tf_op jit(solution)/shard_map/pallas_call | solution.py:615
  47.6 1.5 %collective-permute-start.11 = (f32[384,128]{1,0:T(8,128)S(1)}, f32[384,128]{1,0:T(8,128)S(1)}, u32[]{:S(2)}, u32[]{:S(2)}) collective-permute-start(f32[384,128]{1,0:T(8,128)S(1)} %shard_map.79.left_ref), channel_id=1, source_target_pairs={{0,2},{1,5},{2,0},{3,7},{4,6},{5,1},{6,4},{7,3},{8,10},{9,13},{10,... | collective-permute-start | bytes 589832 | tf_op jit(solution)/shard_map/ppermute | solution.py:809
  49.2 3.4 %collective-permute-start.13 = (f32[416,128]{1,0:T(8,128)S(1)}, f32[416,128]{1,0:T(8,128)S(1)}, u32[]{:S(2)}, u32[]{:S(2)}) collective-permute-start(f32[416,128]{1,0:T(8,128)S(1)} %get-tuple-element.25), channel_id=1, source_target_pairs={{0,8},{8,16},{16,24},{1,9},{9,17},{17,25},{2,10},{10,18},{18,26},{... | collective-permute-start | bytes 638984 | tf_op jit(solution)/shard_map/ppermute | solution.py:753
  53.4 1.9 %collective-permute-start.12 = (f32[384,128]{1,0:T(8,128)S(1)}, f32[384,128]{1,0:T(8,128)S(1)}, u32[]{:S(2)}, u32[]{:S(2)}) collective-permute-start(f32[384,128]{1,0:T(8,128)S(1)} %shard_map.80.mine_ref), channel_id=1, source_target_pairs={{0,4},{1,3},{2,6},{3,1},{4,0},{5,7},{6,2},{7,5},{8,12},{9,11},{10,... | collective-permute-start | bytes 589832 | tf_op jit(solution)/shard_map/ppermute | solution.py:810
  55.5 1.5 %shard_map.78 = (bf16[300,1280]{1,0:T(8,128)(2,1)}, f32[8,128]{1,0:T(8,128)S(1)}) custom-call(f32[304,384]{1,0:T(8,128)S(1)} %get-tuple-element.22.inverse_ref.refs_0_, bf16[300,1280]{1,0:T(8,128)(2,1)S(1)} %get-tuple-element.18.y_ref.right_ref), custom_call_target="tpu_custom_call" | custom-call | flops 100000 | bytes 100000 | tf_op jit(solution)/shard_map/pallas_call | solution.py:670
  57.0 0.9 %collective-permute-done.13.previous_ref = f32[416,128]{1,0:T(8,128)S(1)} collective-permute-done((f32[416,128]{1,0:T(8,128)S(1)}, f32[416,128]{1,0:T(8,128)S(1)}, u32[]{:S(2)}, u32[]{:S(2)}) %collective-permute-start.13) | collective-permute-done | bytes 213024 | tf_op jit(solution)/shard_map/ppermute | solution.py:753
  57.9 1.2 %collective-permute-done.12.chip_ref = f32[384,128]{1,0:T(8,128)S(1)} collective-permute-done((f32[384,128]{1,0:T(8,128)S(1)}, f32[384,128]{1,0:T(8,128)S(1)}, u32[]{:S(2)}, u32[]{:S(2)}) %collective-permute-start.12) | collective-permute-done | bytes 196640 | tf_op jit(solution)/shard_map/ppermute | solution.py:810
  59.1 1.3 %shard_map.81.left_ref = bf16[304,384]{1,0:T(8,128)(2,1)S(1)} custom-call(s32[1]{0:T(128)} %bitcast.core_ref, f32[384,128]{1,0:T(8,128)S(1)} %shard_map.80.mine_ref, f32[384,128]{1,0:T(8,128)S(1)} %collective-permute-done.12.chip_ref, f32[304,384]{1,0:T(8,128)S(1)} %get-tuple-element.22.inverse_ref.refs_0_, ...), custom_call_target="tpu_custom_call" | custom-call | flops 100000 | bytes 100000 | tf_op jit(solution)/shard_map/pallas_call | solution.py:705
  61.1 1.0 %collective-permute-done.16.other_ref = bf16[208,128]{1,0:T(8,128)(2,1)S(1)} collective-permute-done((bf16[208,128]{1,0:T(8,128)(2,1)S(1)}, bf16[208,128]{1,0:T(8,128)(2,1)S(1)}, u32[]{:S(2)}, u32[]{:S(2)}) %collective-permute-start.16) | collective-permute-done | bytes 53280 | tf_op jit(solution)/shard_map/ppermute | solution.py:757
  62.1 1.2 %shard_map.83 = (f32[300,1,300]{2,1,0:T(1,128)}, f32[300,1,300]{2,1,0:T(1,128)}) custom-call(s32[1]{0:T(128)} %bitcast.core_ref, bf16[304,384]{1,0:T(8,128)(2,1)S(1)} %shard_map.81.left_ref, bf16[304,384]{1,0:T(8,128)(2,1)S(1)} %collective-permute-done.14.right_ref, bf16[208,128]{1,0:T(8,128)(2,1)S(1)} %shard_map.82.mine_ref, ...), custom_call_target="tpu_custom_call" | custom-call | flops 100000 | bytes 100000 | tf_op jit(solution)/shard_map/pallas_call | solution.py:735
  (34 shorter events, 4.4 us)
Async XLA Ops:
  0.6 9.3 %copy-start = (bf16[1,1280,300]{1,2,0:T(8,128)(2,1)S(1)}, bf16[1,1280,300]{1,2,0:T(8,128)(2,1)}, u32[]{:S(2)}) copy-start(bf16[1,1280,300]{1,2,0:T(8,128)(2,1)} %param.4) | copy-start | bytes 2304004
  0.6 12.6 %collective-permute-start = (bf16[300,1280]{1,0:T(8,128)(2,1)}, bf16[300,1280]{1,0:T(8,128)(2,1)S(1)}, u32[]{:S(2)}, u32[]{:S(2)}) collective-permute-start(bf16[300,1280]{1,0:T(8,128)(2,1)} %bitcast.14), channel_id=1, source_target_pairs={{1,0},{2,1},{3,2},{4,3},{5,4},{6,5},{7,6},{9,8},{10,9},{11,10},{12... | collective-permute-start | bytes 2304008 | tf_op jit(solution)/shard_map/ppermute | solution.py:753
  2.1 0.7 %copy-start.1 = (s32[1,2,10,10]{3,1,2,0:T(2,128)S(1)}, s32[1,2,10,10]{3,1,2,0:T(2,128)}, u32[]{:S(2)}) copy-start(s32[1,2,10,10]{3,1,2,0:T(2,128)} %param.7) | copy-start | bytes 2404
  2.8 7.1 %copy-start.2 = (s32[1,2,10,10]{3,1,2,0:T(2,128)S(1)}, s32[1,2,10,10]{3,1,2,0:T(2,128)}, u32[]{:S(2)}) copy-start(s32[1,2,10,10]{3,1,2,0:T(2,128)} %param.7) | copy-start | bytes 2404
  6.8 9.6 %collective-permute-start.1 = (bf16[300,1280]{1,0:T(8,128)(2,1)S(1)}, bf16[300,1280]{1,0:T(8,128)(2,1)S(1)}, u32[]{:S(2)}, u32[]{:S(2)}) collective-permute-start(bf16[300,1280]{1,0:T(8,128)(2,1)S(1)} %shard_map.69), channel_id=1, source_target_pairs={{0,1},{1,2},{2,3},{3,4},{4,5},{5,6},{6,7},{8,9},{9,10},{10,11},{11... | collective-permute-start | bytes 2304008 | tf_op jit(solution)/shard_map/ppermute | solution.py:753
  16.9 8.4 %collective-permute-start.2 = (f32[208,128]{1,0:T(8,128)S(1)}, f32[208,128]{1,0:T(8,128)S(1)}, u32[]{:S(2)}, u32[]{:S(2)}) collective-permute-start(f32[208,128]{1,0:T(8,128)S(1)} %get-tuple-element.17), channel_id=1, source_target_pairs={{0,1},{1,0},{2,3},{3,2},{4,5},{5,4},{6,7},{7,6},{8,9},{9,8},{10,11... | collective-permute-start | bytes 319496 | tf_op jit(solution)/shard_map/ppermute | solution.py:757
  21.8 23.2 %collective-permute-start.8 = (bf16[300,1280]{1,0:T(8,128)(2,1)S(1)}, bf16[300,1280]{1,0:T(8,128)(2,1)S(1)}, u32[]{:S(2)}, u32[]{:S(2)}) collective-permute-start(bf16[300,1280]{1,0:T(8,128)(2,1)S(1)} %get-tuple-element.18.y_ref.right_ref), channel_id=1, source_target_pairs={{0,8},{8,16},{16,24},{1,9},{9,17},{17,25},{2,10},{10,18},{18,26},{... | collective-permute-start | bytes 2304008 | tf_op jit(solution)/shard_map/ppermute | solution.py:753
  25.4 9.0 %collective-permute-start.3 = (f32[208,128]{1,0:T(8,128)S(1)}, f32[208,128]{1,0:T(8,128)S(1)}, u32[]{:S(2)}, u32[]{:S(2)}) collective-permute-start(f32[208,128]{1,0:T(8,128)S(1)} %add.8.after_ref.own_ref), channel_id=1, source_target_pairs={{0,6},{1,7},{2,4},{3,5},{4,2},{5,3},{6,0},{7,1},{8,14},{9,15},{10,... | collective-permute-start | bytes 319496 | tf_op jit(solution)/shard_map/ppermute | solution.py:775
  30.6 5.9 %collective-permute-start.4 = (f32[208,128]{1,0:T(8,128)S(1)}, f32[208,128]{1,0:T(8,128)S(1)}, u32[]{:S(2)}, u32[]{:S(2)}) collective-permute-start(f32[208,128]{1,0:T(8,128)S(1)} %add.8.after_ref.own_ref), channel_id=1, source_target_pairs={{0,2},{1,3},{2,0},{3,1},{4,6},{5,7},{6,4},{7,5},{8,10},{9,11},{10,... | collective-permute-start | bytes 319496 | tf_op jit(solution)/shard_map/ppermute | solution.py:775
  31.2 5.3 %collective-permute-start.5 = (f32[208,128]{1,0:T(8,128)S(1)}, f32[208,128]{1,0:T(8,128)S(1)}, u32[]{:S(2)}, u32[]{:S(2)}) collective-permute-start(f32[208,128]{1,0:T(8,128)S(1)} %add.8.after_ref.own_ref), channel_id=1, source_target_pairs={{0,4},{1,5},{2,6},{3,7},{4,0},{5,1},{6,2},{7,3},{8,12},{9,13},{10,... | collective-permute-start | bytes 319496 | tf_op jit(solution)/shard_map/ppermute | solution.py:775
  31.7 1.3 %collective-permute-start.6 = (bf16[208,128]{1,0:T(8,128)(2,1)S(1)}, bf16[208,128]{1,0:T(8,128)(2,1)S(1)}, u32[]{:S(2)}, u32[]{:S(2)}) collective-permute-start(bf16[208,128]{1,0:T(8,128)(2,1)S(1)} %get-tuple-element.20), channel_id=1, source_target_pairs={{0,1},{1,0},{2,3},{3,2},{4,5},{5,4},{6,7},{7,6},{8,9},{9,8},{10,11... | collective-permute-start | bytes 159752 | tf_op jit(solution)/shard_map/ppermute | solution.py:757
  36.6 1.6 %collective-permute-start.7 = (f32[208,128]{1,0:T(8,128)S(1)}, f32[208,128]{1,0:T(8,128)S(1)}, u32[]{:S(2)}, u32[]{:S(2)}) collective-permute-start(f32[208,128]{1,0:T(8,128)S(1)} %shard_map.73.mine_ref), channel_id=1, source_target_pairs={{0,1},{1,0},{2,3},{3,2},{4,5},{5,4},{6,7},{7,6},{8,9},{9,8},{10,11... | collective-permute-start | bytes 319496 | tf_op jit(solution)/shard_map/ppermute | solution.py:757
  36.6 8.4 %collective-permute-start.9 = (bf16[208,128]{1,0:T(8,128)(2,1)S(1)}, bf16[208,128]{1,0:T(8,128)(2,1)S(1)}, u32[]{:S(2)}, u32[]{:S(2)}) collective-permute-start(bf16[208,128]{1,0:T(8,128)(2,1)S(1)} %shard_map.72.after_ref.left_ref), channel_id=1, source_target_pairs={{0,2},{1,5},{2,0},{3,7},{4,6},{5,1},{6,4},{7,3},{8,10},{9,13},{10,... | collective-permute-start | bytes 159752 | tf_op jit(solution)/shard_map/ppermute | solution.py:800
  45.8 1.8 %collective-permute-start.10 = (f32[384,128]{1,0:T(8,128)S(1)}, f32[384,128]{1,0:T(8,128)S(1)}, u32[]{:S(2)}, u32[]{:S(2)}) collective-permute-start(f32[384,128]{1,0:T(8,128)S(1)} %get-tuple-element.21.after_ref), channel_id=1, source_target_pairs={{0,1},{1,0},{2,3},{3,2},{4,5},{5,4},{6,7},{7,6},{8,9},{9,8},{10,11... | collective-permute-start | bytes 589832 | tf_op jit(solution)/shard_map/ppermute | solution.py:757
  47.6 5.7 %collective-permute-start.11 = (f32[384,128]{1,0:T(8,128)S(1)}, f32[384,128]{1,0:T(8,128)S(1)}, u32[]{:S(2)}, u32[]{:S(2)}) collective-permute-start(f32[384,128]{1,0:T(8,128)S(1)} %shard_map.79.left_ref), channel_id=1, source_target_pairs={{0,2},{1,5},{2,0},{3,7},{4,6},{5,1},{6,4},{7,3},{8,10},{9,13},{10,... | collective-permute-start | bytes 589832 | tf_op jit(solution)/shard_map/ppermute | solution.py:809
  49.2 8.7 %collective-permute-start.13 = (f32[416,128]{1,0:T(8,128)S(1)}, f32[416,128]{1,0:T(8,128)S(1)}, u32[]{:S(2)}, u32[]{:S(2)}) collective-permute-start(f32[416,128]{1,0:T(8,128)S(1)} %get-tuple-element.25), channel_id=1, source_target_pairs={{0,8},{8,16},{16,24},{1,9},{9,17},{17,25},{2,10},{10,18},{18,26},{... | collective-permute-start | bytes 638984 | tf_op jit(solution)/shard_map/ppermute | solution.py:753
  53.4 5.7 %collective-permute-start.12 = (f32[384,128]{1,0:T(8,128)S(1)}, f32[384,128]{1,0:T(8,128)S(1)}, u32[]{:S(2)}, u32[]{:S(2)}) collective-permute-start(f32[384,128]{1,0:T(8,128)S(1)} %shard_map.80.mine_ref), channel_id=1, source_target_pairs={{0,4},{1,3},{2,6},{3,1},{4,0},{5,7},{6,2},{7,5},{8,12},{9,11},{10,... | collective-permute-start | bytes 589832 | tf_op jit(solution)/shard_map/ppermute | solution.py:810
  55.3 5.2 %collective-permute-start.15 = (bf16[208,128]{1,0:T(8,128)(2,1)S(1)}, bf16[208,128]{1,0:T(8,128)(2,1)S(1)}, u32[]{:S(2)}, u32[]{:S(2)}) collective-permute-start(bf16[208,128]{1,0:T(8,128)(2,1)S(1)} %shard_map.75.after_ref.left_ref), channel_id=1, source_target_pairs={{0,4},{1,3},{2,6},{3,1},{4,0},{5,7},{6,2},{7,5},{8,12},{9,11},{10,... | collective-permute-start | bytes 159752 | tf_op jit(solution)/shard_map/ppermute | solution.py:815
  60.4 1.6 %collective-permute-start.14 = (bf16[304,384]{1,0:T(8,128)(2,1)S(1)}, bf16[304,384]{1,0:T(8,128)(2,1)S(1)}, u32[]{:S(2)}, u32[]{:S(2)}) collective-permute-start(bf16[304,384]{1,0:T(8,128)(2,1)S(1)} %shard_map.81.left_ref), channel_id=1, source_target_pairs={{0,1},{1,0},{2,3},{3,2},{4,5},{5,4},{6,7},{7,6},{8,9},{9,8},{10,11... | collective-permute-start | bytes 700424 | tf_op jit(solution)/shard_map/ppermute | solution.py:757
  60.5 1.5 %collective-permute-start.16 = (bf16[208,128]{1,0:T(8,128)(2,1)S(1)}, bf16[208,128]{1,0:T(8,128)(2,1)S(1)}, u32[]{:S(2)}, u32[]{:S(2)}) collective-permute-start(bf16[208,128]{1,0:T(8,128)(2,1)S(1)} %shard_map.82.mine_ref), channel_id=1, source_target_pairs={{0,1},{1,0},{2,3},{3,2},{4,5},{5,4},{6,7},{7,6},{8,9},{9,8},{10,11... | collective-permute-start | bytes 159752 | tf_op jit(solution)/shard_map/ppermute | solution.py:757
